TPU v7x, 32 devices: a whole 2x2x4 slice. The times are simulated.
32 devices in a mesh: group: 2 (over x), reader: 16 (over z, y, core).
Axes of the slice: x: 2, y: 2, z: 4, core: 2. Of those that a mesh axis runs over, the one named last changes fastest.
Arguments:
- answer_lengths: int32 [64], P('group'), parts along dimension 0, may hold values from 1 to 256, 4096 in all
- mixer_input: bfloat16 [8192, 4096], P(('group', 'reader')), parts along dimension 0, may hold values from -6 to 6
- gate_input: bfloat16 [8192, 4096], P(('group', 'reader')), parts along dimension 0, may hold values from -6 to 6
- state_write: bfloat16 [8192, 512], P(('group', 'reader')), parts along dimension 0, may hold values from -6 to 6
- state_read: bfloat16 [8192, 512], P(('group', 'reader')), parts along dimension 0, may hold values from -0.5 to 0.5
- step_raw: float32 [8192, 64], P(('group', 'reader')), parts along dimension 0, may hold values from -4 to 50
- decay_rate: float32 [64], replicated, may hold values from 0.006 to 0.15
- skip_gain: float32 [64], replicated, may hold values from 0.5 to 2
- norm_gain: float32 [4096], replicated, may hold values from 0.1 to 1.9
- prompt_state: float32 [8192, 128], P(('group', 'reader')), parts along dimension 0, may hold values from -24 to 24
- queries: bfloat16 [8192, 2048], P(('group', 'reader')), parts along dimension 0, may hold values from -160 to 160
- answer_keys: bfloat16 [8192, 512], P(('group', 'reader')), parts along dimension 0, may hold values from -6 to 6
- answer_values: bfloat16 [8192, 512], P(('group', 'reader')), parts along dimension 0, may hold values from -48 to 48
- prompt_keys: bfloat16 [256, 512], P(('group', 'reader')), parts along dimension 0, may hold values from -4 to 4
- prompt_values: bfloat16 [256, 512], P(('group', 'reader')), parts along dimension 0, may hold values from -48 to 48
Outputs:
- mixer_out: bfloat16 [8192, 4096], P(('group', 'reader')), parts along dimension 0
- attention_out: bfloat16 [8192, 2048], P(('group', 'reader')), parts along dimension 0
There are 2 independent parts, one for each index of `group`. A program takes and returns all parts, laid end to end along the dimension named above; an argument that names none is the same for every part. Nothing has to cross between parts.
Inputs may be any that keep to these rules, and one draw needn't show every extreme that they name: `answer_lengths`: the answers fill the 4096 tokens in order, back to back; the longest has exactly 256 tokens.
All inputs are finite; a program needn't handle non-finite values.
Results may differ from a plain program's by a relative error of at most 0.0047.
Values may be sent and summed in bfloat16 or wider, within the bound.
No kernel may reach another device: no remote copies, remote signals or barrier semaphores. Data moves between devices by JAX's collectives and lax.ppermute only.
A program may use at most 128 MiB of HBM per device.

v0:
```python
import functools
import math

import jax
import jax.numpy as jnp
from jax import lax
from jax.experimental import pallas as pl
from jax.experimental.pallas import tpu as pltpu
from jax.sharding import PartitionSpec as P

HD = 128
LANES = 128
LOG2E = 1.4426950408889634
F32 = jnp.float32
BF16 = jnp.bfloat16
MIB = 1 << 20


def iota(shape, dim):
    return lax.broadcasted_iota(jnp.int32, shape, dim)


def dot(a, b, ca=1, cb=0):
    return lax.dot_general(a, b, (((ca,), (cb,)), ((), ())), preferred_element_type=F32)


def expander(heads, group, per_group, channels):
    shape = (2 * heads, per_group * channels)
    row = iota(shape, 0)
    head = jnp.where(row >= heads, row - heads, row) - group * per_group
    column = iota(shape, 1)
    first = head * channels
    return jnp.where((column >= first) & (column < first + channels), 1.0, 0.0).astype(BF16)


def two_parts(value, heads):
    high = value.astype(BF16).astype(F32)
    return jnp.where(iota(value.shape, 1) < heads, high, value - high).astype(BF16)


def pack_kernel(state_ref, keys_ref, values_ref, near_keys_ref, near_values_ref, out_ref, near_ref):
    rows = state_ref.shape[0]
    out_ref[:rows, :] = state_ref[...].astype(BF16)
    parts = []
    for ref in (keys_ref, values_ref):
        wide = ref[...].astype(F32)
        for head in range(wide.shape[1] // HD):
            parts.append(wide[:, head * HD : (head + 1) * HD])
    out_ref[rows:, :] = jnp.concatenate(parts, axis=0).astype(BF16)
    width = near_keys_ref.shape[1]
    near_ref[:, :width] = near_keys_ref[...]
    near_ref[:, width:] = near_values_ref[...]


def tail_kernel(
    base_ref,
    lengths_ref,
    raw_ref,
    rate_ref,
    x_ref,
    write_ref,
    tail_ref,
    level_ref,
    column_ref,
    start_ref,
    weight_ref,
    *,
    heads,
    per_group,
    channels,
):
    group = pl.program_id(0)
    tokens = x_ref.shape[0]
    columns = heads * channels

    @pl.when(group == 0)
    def _():
        base = base_ref[0, 0].astype(F32)
        lengths = lengths_ref[...].astype(F32)
        answers = lengths.shape[1]
        square = (answers, answers)
        ends = jnp.sum(
            jnp.where(iota(square, 1) <= iota(square, 0), lengths, 0.0), axis=1, keepdims=True
        )
        place = base + iota((1, tokens), 1).astype(F32)
        start = jnp.max(jnp.where(ends <= place, ends, 0.0), axis=0, keepdims=True) - base
        start = jnp.broadcast_to(start, (LANES, tokens)).T
        start_ref[...] = start
        wide = jnp.concatenate([start] * (tokens // LANES), axis=1)
        square = (tokens, tokens)
        source = iota(square, 1)
        mask = (source.astype(F32) >= wide) & (source <= iota(square, 0))
        mask = jnp.where(mask, 1.0, 0.0).astype(BF16)
        raw = jnp.concatenate([raw_ref[...]] * 2, axis=1)
        rate = jnp.concatenate([rate_ref[...]] * 2, axis=1)
        step = jnp.maximum(raw, 0.0) + jnp.log1p(jnp.exp(-jnp.abs(raw)))
        falling = -rate * step
        first = falling.astype(BF16)
        rest = falling - first.astype(F32)
        second = rest.astype(BF16)
        third = (rest - second.astype(F32)).astype(BF16)
        level = dot(mask, first) + (dot(mask, second) + dot(mask, third))
        level_ref[...] = level
        column = level * LOG2E - jnp.log(step) * LOG2E
        column_ref[...] = column.T[:heads, :]
        last = level[tokens - 1 :, :]
        own = iota((tokens, 2 * heads), 0).astype(F32) >= start[tokens - 1 :, : 2 * heads]
        weight = jnp.where(own, jnp.exp(last - level) * step, 0.0)
        weight_ref[...] = two_parts(weight, heads)
        decay = jnp.exp(jnp.broadcast_to(last, (16, 2 * heads)))
        high = decay.astype(BF16).astype(F32)
        row = iota(decay.shape, 0)
        decay = jnp.where(row == 0, high, jnp.where(row == 1, decay - high, 0.0))
        tail_ref[:, columns:] = jnp.zeros((tail_ref.shape[0], 2 * heads), BF16)
        tail_ref[:16, columns:] = decay.astype(BF16)

    spread = expander(heads, group, per_group, channels)
    weight = dot(weight_ref[...], spread)
    weighted = (x_ref[...].astype(F32) * weight).astype(BF16)
    width = per_group * channels
    tail_ref[:, pl.ds(pl.multiple_of(group * width, width), width)] = dot(
        write_ref[...], weighted, 0, 0
    ).astype(BF16)


def inner_kernel(
    start_ref,
    level_ref,
    column_ref,
    skip_ref,
    x_ref,
    write_ref,
    read_ref,
    out_ref,
    *,
    heads,
    per_group,
    channels,
):
    group = pl.program_id(0)
    tokens = x_ref.shape[0]
    both = dot(read_ref[...], write_ref[...], 1, 1)
    square = (tokens, tokens)
    source = iota(square, 1)
    wide = jnp.concatenate([start_ref[...]] * (tokens // LANES), axis=1)
    both = jnp.where((source.astype(F32) >= wide) & (source <= iota(square, 0)), both, 0.0)
    lanes = level_ref.shape[1]
    level = pltpu.roll(level_ref[...] * LOG2E, lanes - group * per_group, 1)
    skip = jnp.concatenate([skip_ref[...]] * 2, axis=1)
    skip = two_parts(jnp.broadcast_to(skip, (16, 2 * heads)), heads)
    skip = dot(skip, expander(heads, group, per_group, channels))[:1, :]
    per_tile = LANES // channels
    lane = iota((LANES, LANES), 1)
    for tile in range(per_group // per_tile):
        at = slice(tile * LANES, (tile + 1) * LANES)
        x = x_ref[:, at]
        for block in range(tokens // LANES):
            rows = slice(block * LANES, (block + 1) * LANES)
            reach = (block + 1) * LANES
            total = None
            for part in range(per_tile):
                head = tile * per_tile + part
                gap = level[rows, head : head + 1] - column_ref[head : head + 1, :reach]
                mixing = (jnp.exp2(jnp.minimum(gap, 64.0)) * both[rows, :reach]).astype(BF16)
                result = dot(mixing, x[:reach, :])
                total = result if total is None else jnp.where(
                    lane < part * channels, total, result
                )
            total = total + skip[:, at] * x[rows, :].astype(F32)
            out_ref[rows, at] = total.astype(BF16)


def attend_kernel(
    start_ref,
    query_ref,
    key_ref,
    value_ref,
    prior_key_ref,
    prior_value_ref,
    gathered_ref,
    out_ref,
    bias_ref,
    *,
    state_rows,
    prompt_rows,
    kv_count,
):
    head = pl.program_id(0)
    tokens = query_ref.shape[0]
    devices = gathered_ref.shape[0]
    scale = LOG2E / math.sqrt(HD)

    @pl.when(head == 0)
    def _():
        shape = (tokens, 2 * tokens)
        place = iota(shape, 1) - tokens
        wide = jnp.concatenate([start_ref[...]] * (2 * tokens // LANES), axis=1)
        allowed = (place.astype(F32) >= wide) & (place <= iota(shape, 0))
        bias_ref[...] = jnp.where(allowed, 0.0, -jnp.inf)

    def prompt(which):
        at = pl.multiple_of(state_rows + (which * kv_count + head) // 2 * 2 * prompt_rows, 16)
        pair = gathered_ref[:, pl.ds(at, 2 * prompt_rows), :].astype(F32)
        odd = lax.rem(head, 2) == 1
        part = jnp.where(odd, pair[:, prompt_rows:, :], pair[:, :prompt_rows, :])
        return part.reshape(devices * prompt_rows, HD).astype(BF16)

    prompt_keys = prompt(0)
    ones = jnp.ones((tokens, LANES), BF16)
    prompt_values = prompt(1)
    prompt_values = jnp.concatenate(
        [prompt_values, jnp.ones((prompt_values.shape[0], LANES), BF16)], axis=1
    )
    near_keys = jnp.concatenate([prior_key_ref[...], key_ref[...]], axis=0)
    near_values = jnp.concatenate(
        [
            jnp.concatenate([prior_value_ref[...], ones], axis=1),
            jnp.concatenate([value_ref[...], ones], axis=1),
        ],
        axis=0,
    )
    for query in range(query_ref.shape[1] // HD):
        at = slice(query * HD, (query + 1) * HD)
        for block in range(tokens // LANES):
            rows = slice(block * LANES, (block + 1) * LANES)
            reach = tokens + (block + 1) * LANES
            q = query_ref[rows, at]
            far = dot(q, prompt_keys, 1, 1)
            near = dot(q, near_keys[:reach, :], 1, 1) + bias_ref[rows, :reach]
            top = jnp.maximum(
                jnp.max(far, axis=1, keepdims=True), jnp.max(near, axis=1, keepdims=True)
            )
            far = jnp.exp2((far - top) * scale).astype(BF16)
            near = jnp.exp2((near - top) * scale).astype(BF16)
            summed = dot(far, prompt_values) + dot(near, near_values[:reach, :])
            out_ref[rows, at] = (summed[:, :HD] / summed[:, HD:]).astype(BF16)


def final_kernel(
    start_ref,
    level_ref,
    tail_ref,
    decay_ref,
    gathered_ref,
    read_ref,
    inner_ref,
    gate_ref,
    gain_ref,
    out_ref,
    *,
    state_rows,
    heads,
    per_group,
    channels,
):
    group = pl.program_id(0)
    tokens = read_ref.shape[0]
    level = jnp.exp(level_ref[...])
    carried = start_ref[:, : 2 * heads] < 0
    decay = decay_ref[...].astype(F32)
    decay = decay[0:1, :] + decay[1:2, :]
    spread = expander(heads, group, per_group, channels)
    from_prompt = dot(two_parts(jnp.where(carried, level * decay, level), heads), spread)
    from_prior = dot(two_parts(jnp.where(carried, level, 0.0), heads), spread)
    seeds = gathered_ref[:, :state_rows, :]
    seeds = seeds.reshape(seeds.shape[0] * state_rows, seeds.shape[2])
    read = read_ref[...]
    mixed = inner_ref[...].astype(F32)
    mixed = mixed + from_prompt * dot(read, seeds, 1, 1)
    mixed = mixed + from_prior * dot(read, tail_ref[...])
    gate = gate_ref[...].astype(F32)
    gated = mixed * (gate * (0.5 + 0.5 * jnp.tanh(0.5 * gate)))
    scale = lax.rsqrt(jnp.mean(gated * gated, axis=1, keepdims=True) + 1e-05)
    out_ref[...] = (gated * scale * gain_ref[...]).astype(BF16)


def shifted(value, axis, by):
    length = lax.axis_size(axis)
    return lax.ppermute(value, axis, [(i, i + by) for i in range(length - by)])


def params(limit=40):
    return pltpu.CompilerParams(vmem_limit_bytes=limit * MIB)


def whole(shape):
    return pl.BlockSpec(shape, lambda g: (0,) * len(shape))


def local(
    answer_lengths,
    mixer_input,
    gate_input,
    state_write,
    state_read,
    step_raw,
    decay_rate,
    skip_gain,
    norm_gain,
    prompt_state,
    queries,
    answer_keys,
    answer_values,
    prompt_keys,
    prompt_values,
):
    tokens, columns = mixer_input.shape
    heads = decay_rate.shape[0]
    state_rows, state = prompt_state.shape
    groups = state_write.shape[1] // state
    per_group = heads // groups
    channels = columns // heads
    width = per_group * channels
    prompt_rows, kv_width = prompt_keys.shape
    kv_count = kv_width // HD
    devices = lax.axis_size("reader")
    base = (lax.axis_index("reader") * tokens).astype(jnp.int32).reshape(1, 1)
    lengths = answer_lengths.reshape(1, -1)
    sizes = dict(heads=heads, per_group=per_group, channels=channels)
    packed_rows = state_rows + 2 * prompt_rows * kv_count

    packed, near = pl.pallas_call(
        pack_kernel,
        out_shape=(
            jax.ShapeDtypeStruct((packed_rows, HD), BF16),
            jax.ShapeDtypeStruct((tokens, 2 * kv_width), BF16),
        ),
        compiler_params=params(16),
        name="pack",
    )(prompt_state, prompt_keys, prompt_values, answer_keys, answer_values)
    gathered = lax.all_gather(packed, "reader", axis=0, tiled=False)
    prior = shifted(near, "reader", 1)

    by_group = lambda rows: pl.BlockSpec((rows, state), lambda g: (0, g))
    wide = pl.BlockSpec((tokens, width), lambda g: (0, g))
    tail, level, column, start = pl.pallas_call(
        functools.partial(tail_kernel, **sizes),
        grid=(groups,),
        in_specs=[
            pl.BlockSpec(memory_space=pltpu.SMEM),
            whole(lengths.shape),
            whole(step_raw.shape),
            whole((1, heads)),
            wide,
            by_group(tokens),
        ],
        out_specs=(
            whole((state, columns + 2 * heads)),
            whole((tokens, 2 * heads)),
            whole((heads, tokens)),
            whole((tokens, LANES)),
        ),
        out_shape=(
            jax.ShapeDtypeStruct((state, columns + 2 * heads), BF16),
            jax.ShapeDtypeStruct((tokens, 2 * heads), F32),
            jax.ShapeDtypeStruct((heads, tokens), F32),
            jax.ShapeDtypeStruct((tokens, LANES), F32),
        ),
        scratch_shapes=[pltpu.VMEM((tokens, 2 * heads), BF16)],
        compiler_params=params(),
        name="tail",
    )(base, lengths, step_raw, decay_rate.reshape(1, -1), mixer_input, state_write)
    tail = shifted(tail, "reader", 1)

    inner = pl.pallas_call(
        functools.partial(inner_kernel, **sizes),
        grid=(groups,),
        in_specs=[
            whole((tokens, LANES)),
            whole((tokens, 2 * heads)),
            pl.BlockSpec((per_group, tokens), lambda g: (g, 0)),
            whole((1, heads)),
            wide,
            by_group(tokens),
            by_group(tokens),
        ],
        out_specs=wide,
        out_shape=jax.ShapeDtypeStruct((tokens, columns), BF16),
        compiler_params=params(),
        cost_estimate=pl.CostEstimate(
            flops=heads * tokens * tokens * channels * 8,
            bytes_accessed=tokens * columns * 4,
            transcendentals=heads * tokens * tokens,
        ),
        name="inner",
    )(start, level, column, skip_gain.reshape(1, -1), mixer_input, state_write, state_read)

    group_size = queries.shape[1] // kv_width
    attention_out = pl.pallas_call(
        functools.partial(
            attend_kernel, state_rows=state_rows, prompt_rows=prompt_rows, kv_count=kv_count
        ),
        grid=(kv_count,),
        in_specs=[
            whole((tokens, LANES)),
            pl.BlockSpec((tokens, group_size * HD), lambda k: (0, k)),
            pl.BlockSpec((tokens, HD), lambda k: (0, k)),
            pl.BlockSpec((tokens, HD), lambda k: (0, k)),
            pl.BlockSpec((tokens, HD), lambda k: (0, k)),
            pl.BlockSpec((tokens, HD), lambda k: (0, kv_count + k)),
            whole((devices, packed_rows, HD)),
        ],
        out_specs=pl.BlockSpec((tokens, group_size * HD), lambda k: (0, k)),
        out_shape=jax.ShapeDtypeStruct(queries.shape, BF16),
        scratch_shapes=[pltpu.VMEM((tokens, 2 * tokens), F32)],
        compiler_params=params(),
        name="attend",
    )(start, queries, answer_keys, answer_values, prior, prior, gathered)

    mixer_out = pl.pallas_call(
        functools.partial(final_kernel, state_rows=state_rows, **sizes),
        grid=(groups,),
        in_specs=[
            whole((tokens, LANES)),
            whole((tokens, 2 * heads)),
            pl.BlockSpec((state, width), lambda g: (0, g)),
            pl.BlockSpec((16, 2 * heads), lambda g: (0, columns // (2 * heads))),
            pl.BlockSpec((devices // groups, packed_rows, HD), lambda g: (g, 0, 0)),
            by_group(tokens),
            wide,
            wide,
            pl.BlockSpec((1, width), lambda g: (0, g)),
        ],
        out_specs=wide,
        out_shape=jax.ShapeDtypeStruct((tokens, columns), BF16),
        compiler_params=params(),
        name="final",
    )(start, level, tail, tail, gathered, state_read, inner, gate_input, norm_gain.reshape(1, -1))
    return (mixer_out, attention_out)


def solution(mesh):
    rows = P(("group", "reader"), None)
    in_specs = (P("group"),) + (rows,) * 5 + (P(),) * 3 + (rows,) * 6
    return jax.shard_map(
        local, mesh=mesh, in_specs=in_specs, out_specs=(rows, rows), check_vma=False
    )
```

profile of v0, /device:TPU:0, one launch (start us, length us, event | category | flops | bytes accessed | tf_op | source)
XLA Modules:
  0.0 81.8 jit_solution(6438028415639599864)
XLA Ops:
  7.2 0.0 all-gather.3.cloned.1.call-start
  7.2 0.0 copy-start.8
  7.2 0.9 %copy-done.8 = bf16[256,512]{1,0:T(8,128)(2,1)S(1)} copy-done((bf16[256,512]{1,0:T(8,128)(2,1)S(1)}, bf16[256,512]{1,0:T(8,128)(2,1)}, u32[]{:S(2)}) %copy-start.8) | copy-done | bytes 262168
  8.2 0.0 copy-start.10
  8.2 0.9 %copy-done.10 = bf16[256,512]{1,0:T(8,128)(2,1)S(1)} copy-done((bf16[256,512]{1,0:T(8,128)(2,1)S(1)}, bf16[256,512]{1,0:T(8,128)(2,1)}, u32[]{:S(2)}) %copy-start.10) | copy-done | bytes 262168
  9.1 0.0 copy-start.21
  9.1 0.9 %copy-done.21 = f32[256,128]{1,0:T(8,128)S(1)} copy-done((f32[256,128]{1,0:T(8,128)S(1)}, f32[256,128]{1,0:T(8,128)}, u32[]{:S(2)}) %copy-start.21) | copy-done | bytes 131096
  10.0 0.0 copy-start.23
  10.0 0.7 copy-done.23
  10.7 0.0 copy-start.24
  10.7 0.7 copy-done.24
  11.4 0.0 copy-start.27
  11.4 0.9 %pack.1 = (bf16[320,128]{1,0:T(8,128)(2,1)}, bf16[256,1024]{1,0:T(8,128)(2,1)}) custom-call(f32[256,128]{1,0:T(8,128)S(1)} %copy-done.21, bf16[8,512]{1,0:T(8,128)(2,1)S(1)} %copy-done.23, bf16[8,512]{1,0:T(8,128)(2,1)S(1)} %copy-done.24, bf16[256,512]{1,0:T(8,128)(2,1)S(1)} %copy-done.8, bf16[256,512]{1,0:T(8,128)(2,1)S(1)} %copy-done.10), custom_call_target="tpu_custom_call" | custom-call | tf_op jit(solution)/shard_map/pack/pallas_call | solution.py:322
  12.3 0.0 all-gather.3.cloned.1.call-update
  12.3 0.9 %copy.17.raw_ref = f32[256,64]{1,0:T(8,128)S(1)} copy(f32[256,64]{0,1:T(8,128)} %param.20) | data formatting | bytes 131072 | tf_op args[5]
  13.3 0.0 copy-start.5
  13.3 1.6 %copy-done.5 = bf16[256,4096]{1,0:T(8,128)(2,1)S(1)} copy-done((bf16[256,4096]{1,0:T(8,128)(2,1)S(1)}, bf16[256,4096]{1,0:T(8,128)(2,1)}, u32[]{:S(2)}) %copy-start.5) | copy-done | bytes 2097176
  14.8 0.0 copy-start.15
  14.8 0.9 %copy-done.15 = bf16[256,512]{1,0:T(8,128)(2,1)S(1)} copy-done((bf16[256,512]{1,0:T(8,128)(2,1)S(1)}, bf16[256,512]{1,0:T(8,128)(2,1)}, u32[]{:S(2)}) %copy-start.15) | copy-done | bytes 262168
  15.8 0.0 copy-start.25
  15.8 0.7 copy-done.25
  16.5 0.0 copy-start.26
  16.5 0.7 copy-done.26
  17.1 0.0 copy-start.6
  17.1 0.0 copy-start.16
  17.1 3.7 %tail.1 = (bf16[128,4224]{1,0:T(8,128)(2,1)}, f32[256,128]{1,0:T(8,128)S(1)}, f32[64,256]{1,0:T(8,128)S(1)}, f32[256,128]{1,0:T(8,128)S(1)}) custom-call(s32[1,1]{1,0:T(1,128)} %bitcast.base_ref, s32[1,32]{1,0:T(1,128)S(1)} %bitcast.9, f32[256,64]{1,0:T(8,128)S(1)} %copy.17.raw_ref, f32[1,64]{1,0:T(1,128)S(1)} %bitcast.10, bf16[256,4096]{1,0:T(8,128)(2,1)S(1)} %copy-done.5, ...), custom_call_target="tpu_custom_call" | custom-call | tf_op jit(solution)/shard_map/tail/pallas_call | solution.py:336
  20.8 0.0 copy-start.19
  20.8 2.4 %collective-permute-start = (bf16[128,4224]{1,0:T(8,128)(2,1)}, bf16[128,4224]{1,0:T(8,128)(2,1)S(1)}, u32[]{:S(2)}, u32[]{:S(2)}) collective-permute-start(bf16[128,4224]{1,0:T(8,128)(2,1)} %get-tuple-element.10), channel_id=1, source_target_pairs={{0,1},{1,2},{2,3},{3,4},{4,5},{5,6},{6,7},{7,8},{8,9},{9,10},{10,1... | collective-permute-start | bytes 3244040 | tf_op jit(solution)/shard_map/ppermute | solution.py:279
  23.2 4.5 %collective-permute-start.1 = (bf16[256,1024]{1,0:T(8,128)(2,1)}, bf16[256,1024]{1,0:T(8,128)(2,1)S(1)}, u32[]{:S(2)}, u32[]{:S(2)}) collective-permute-start(bf16[256,1024]{1,0:T(8,128)(2,1)} %get-tuple-element.13), channel_id=1, source_target_pairs={{0,1},{1,2},{2,3},{3,4},{4,5},{5,6},{6,7},{7,8},{8,9},{9,10},{10,1... | collective-permute-start | bytes 1572872 | tf_op jit(solution)/shard_map/ppermute | solution.py:279
  27.7 0.0 copy-done.27
  27.8 0.0 copy-done.6
  27.8 0.0 copy-done.16
  27.8 0.0 copy-start.17
  27.8 0.9 %copy-done.17 = bf16[256,512]{1,0:T(8,128)(2,1)S(1)} copy-done((bf16[256,512]{1,0:T(8,128)(2,1)S(1)}, bf16[256,512]{1,0:T(8,128)(2,1)}, u32[]{:S(2)}) %copy-start.17) | copy-done | bytes 262168
  28.7 0.0 copy-start.9
  28.7 4.6 %inner.1.inner_ref = bf16[256,4096]{1,0:T(8,128)(2,1)S(1)} custom-call(f32[256,128]{1,0:T(8,128)S(1)} %get-tuple-element.8.start_ref, f32[256,128]{1,0:T(8,128)S(1)} %get-tuple-element.9.level_ref, f32[64,256]{1,0:T(8,128)S(1)} %get-tuple-element.12.column_ref, f32[1,64]{1,0:T(1,128)S(1)} %bitcast.11, bf16[256,4096]{1,0:T(8,128)(2,1)S(1)} %copy-done.6, ...), custom_call_target="tpu_custom_call" | custom-call | flops 2147483648 | bytes 4194304 | tf_op jit(solution)/shard_map/inner/pallas_call | solution.py:365
  33.4 0.0 copy-done.12
  33.4 0.0 copy-done.19
  33.4 0.0 collective-permute-done.1.prior_key_ref.prior_value_ref
  33.4 0.0 copy-start.3
  33.4 0.8 copy-done.3
  34.2 22.3 %all-gather.3.cloned.1.call-done = bf16[5120,128]{1,0:T(8,128)(2,1)} async-done(((bf16[320,128]{1,0:T(8,128)(2,1)}), bf16[5120,128]{1,0:T(8,128)(2,1)}) %all-gather.3.cloned.1.call-update) | async-done | bytes 1310736 | tf_op jit(solution)/shard_map/all_gather | solution.py:331
  56.5 0.0 copy-done.9
  56.5 0.0 copy-start
  56.5 1.3 %copy-done = bf16[5120,128]{1,0:T(8,128)(2,1)S(1)} copy-done((bf16[5120,128]{1,0:T(8,128)(2,1)S(1)}, bf16[5120,128]{1,0:T(8,128)(2,1)}, u32[]{:S(2)}) %copy-start) | copy-done | bytes 1310744
  57.8 0.0 copy-start.4
  57.8 1.0 %copy-done.4 = bf16[256,1024]{1,0:T(8,128)(2,1)S(1)} copy-done((bf16[256,1024]{1,0:T(8,128)(2,1)S(1)}, bf16[256,1024]{1,0:T(8,128)(2,1)}, u32[]{:S(2)}) %copy-start.4) | copy-done | bytes 524312
  58.8 0.0 copy-start.7
  58.9 1.2 %copy-done.7 = bf16[256,2048]{1,0:T(8,128)(2,1)S(1)} copy-done((bf16[256,2048]{1,0:T(8,128)(2,1)S(1)}, bf16[256,2048]{1,0:T(8,128)(2,1)}, u32[]{:S(2)}) %copy-start.7) | copy-done | bytes 1048600
  60.1 0.0 copy-start.11
  60.1 0.9 %copy-done.11 = bf16[256,512]{1,0:T(8,128)(2,1)S(1)} copy-done((bf16[256,512]{1,0:T(8,128)(2,1)S(1)}, bf16[256,512]{1,0:T(8,128)(2,1)}, u32[]{:S(2)}) %copy-start.11) | copy-done | bytes 262168
  61.0 0.0 copy-start.13
  61.0 0.9 %copy-done.13 = f32[256,128]{1,0:T(8,128)S(1)} copy-done((f32[256,128]{1,0:T(8,128)S(1)}, f32[256,128]{1,0:T(8,128)}, u32[]{:S(2)}) %copy-start.13) | copy-done | bytes 131096
  61.9 0.0 copy-start.20
  62.0 0.0 copy-start.22
  62.0 6.7 %attend.1 = bf16[256,2048]{1,0:T(8,128)(2,1)} custom-call(f32[256,128]{1,0:T(8,128)S(1)} %copy-done.13, bf16[256,2048]{1,0:T(8,128)(2,1)S(1)} %copy-done.7, bf16[256,512]{1,0:T(8,128)(2,1)S(1)} %copy-done.9, bf16[256,512]{1,0:T(8,128)(2,1)S(1)} %copy-done.11, bf16[256,1024]{1,0:T(8,128)(2,1)S(1)} %copy-done.4, bf16[256,1024]{1,0:T(8,128)(2,1)S(1)} %copy-done.4, ...), custom_call_target="tpu_custom_call" | custom-call | tf_op jit(solution)/shard_map/attend/pallas_call | solution.py:389
  68.7 0.0 collective-permute-done.tail_ref.decay_ref
  68.7 0.0 copy-done.1
  68.7 0.0 copy-done.2
  68.7 0.0 copy-done.14
  68.7 0.0 copy-done.18
  68.7 0.0 copy-done.20
  68.7 0.0 copy-done.22
  68.7 6.2 %final.1 = bf16[256,4096]{1,0:T(8,128)(2,1)} custom-call(f32[256,128]{1,0:T(8,128)S(1)} %copy-done.14, f32[256,128]{1,0:T(8,128)S(1)} %copy-done.20, bf16[128,4224]{1,0:T(8,128)(2,1)S(1)} %collective-permute-done.tail_ref.decay_ref, bf16[128,4224]{1,0:T(8,128)(2,1)S(1)} %collective-permute-done.tail_ref.decay_ref, bf16[16,320,128]{2,1,0:T(8,128)(2,1)S(1)} %bitcast.7, ...), custom_call_target="tpu_custom_call" | custom-call | tf_op jit(solution)/shard_map/final/pallas_call | solution.py:410
  (5 shorter events, 0.0 us)
Async XLA Ops:
  7.2 49.3 %all-gather.3.cloned.1.call-start = ((), (), s32[]{:S(2)}) async-start(), calls=%async_computation | async-start | bytes 1392640 | tf_op jit(solution)/shard_map/all_gather | solution.py:331
  7.2 1.0 %copy-start.8 = (bf16[256,512]{1,0:T(8,128)(2,1)S(1)}, bf16[256,512]{1,0:T(8,128)(2,1)}, u32[]{:S(2)}) copy-start(bf16[256,512]{1,0:T(8,128)(2,1)} %key_ref.1) | copy-start | bytes 786436
  8.2 0.9 %copy-start.10 = (bf16[256,512]{1,0:T(8,128)(2,1)S(1)}, bf16[256,512]{1,0:T(8,128)(2,1)}, u32[]{:S(2)}) copy-start(bf16[256,512]{1,0:T(8,128)(2,1)} %value_ref.1) | copy-start | bytes 786436
  9.1 0.9 %copy-start.21 = (f32[256,128]{1,0:T(8,128)S(1)}, f32[256,128]{1,0:T(8,128)}, u32[]{:S(2)}) copy-start(f32[256,128]{1,0:T(8,128)} %state_ref.1) | copy-start | bytes 393220
  10.0 0.7 copy-start.23
  10.7 0.7 copy-start.24
  11.4 16.3 %copy-start.27 = (f32[64]{0:T(128)S(1)}, f32[64]{0:T(128)}, u32[]{:S(2)}) copy-start(f32[64]{0:T(128)} %param.22) | copy-start | bytes 772
  13.3 1.6 %copy-start.5 = (bf16[256,4096]{1,0:T(8,128)(2,1)S(1)}, bf16[256,4096]{1,0:T(8,128)(2,1)}, u32[]{:S(2)}) copy-start(bf16[256,4096]{1,0:T(8,128)(2,1)} %x_ref.3) | copy-start | bytes 6291460
  14.8 0.9 %copy-start.15 = (bf16[256,512]{1,0:T(8,128)(2,1)S(1)}, bf16[256,512]{1,0:T(8,128)(2,1)}, u32[]{:S(2)}) copy-start(bf16[256,512]{1,0:T(8,128)(2,1)} %write_ref.3) | copy-start | bytes 786436
  15.8 0.7 copy-start.25
  16.5 0.7 copy-start.26
  17.1 10.6 %copy-start.6 = (bf16[256,4096]{1,0:T(8,128)(2,1)S(1)}, bf16[256,4096]{1,0:T(8,128)(2,1)}, u32[]{:S(2)}) copy-start(bf16[256,4096]{1,0:T(8,128)(2,1)} %x_ref.3) | copy-start | bytes 6291460
  17.1 10.7 %copy-start.16 = (bf16[256,512]{1,0:T(8,128)(2,1)S(1)}, bf16[256,512]{1,0:T(8,128)(2,1)}, u32[]{:S(2)}) copy-start(bf16[256,512]{1,0:T(8,128)(2,1)} %write_ref.3) | copy-start | bytes 786436
  20.8 12.6 %copy-start.12 = (f32[256,128]{1,0:T(8,128)}, f32[256,128]{1,0:T(8,128)S(1)}, u32[]{:S(2)}) copy-start(f32[256,128]{1,0:T(8,128)S(1)} %get-tuple-element.8.start_ref) | copy-start | bytes 393220
  20.8 12.6 %copy-start.19 = (f32[256,128]{1,0:T(8,128)}, f32[256,128]{1,0:T(8,128)S(1)}, u32[]{:S(2)}) copy-start(f32[256,128]{1,0:T(8,128)S(1)} %get-tuple-element.9.level_ref) | copy-start | bytes 393220
  20.8 47.9 %collective-permute-start = (bf16[128,4224]{1,0:T(8,128)(2,1)}, bf16[128,4224]{1,0:T(8,128)(2,1)S(1)}, u32[]{:S(2)}, u32[]{:S(2)}) collective-permute-start(bf16[128,4224]{1,0:T(8,128)(2,1)} %get-tuple-element.10), channel_id=1, source_target_pairs={{0,1},{1,2},{2,3},{3,4},{4,5},{5,6},{6,7},{7,8},{8,9},{9,10},{10,1... | collective-permute-start | bytes 3244040 | tf_op jit(solution)/shard_map/ppermute | solution.py:279
  23.2 10.2 %collective-permute-start.1 = (bf16[256,1024]{1,0:T(8,128)(2,1)}, bf16[256,1024]{1,0:T(8,128)(2,1)S(1)}, u32[]{:S(2)}, u32[]{:S(2)}) collective-permute-start(bf16[256,1024]{1,0:T(8,128)(2,1)} %get-tuple-element.13), channel_id=1, source_target_pairs={{0,1},{1,2},{2,3},{3,4},{4,5},{5,6},{6,7},{7,8},{8,9},{9,10},{10,1... | collective-permute-start | bytes 1572872 | tf_op jit(solution)/shard_map/ppermute | solution.py:279
  27.8 1.0 %copy-start.17 = (bf16[256,512]{1,0:T(8,128)(2,1)S(1)}, bf16[256,512]{1,0:T(8,128)(2,1)}, u32[]{:S(2)}) copy-start(bf16[256,512]{1,0:T(8,128)(2,1)} %read_ref.3) | copy-start | bytes 786436
  28.7 27.8 %copy-start.9 = (bf16[256,512]{1,0:T(8,128)(2,1)S(1)}, bf16[256,512]{1,0:T(8,128)(2,1)}, u32[]{:S(2)}) copy-start(bf16[256,512]{1,0:T(8,128)(2,1)} %key_ref.1) | copy-start | bytes 786436
  33.4 0.8 copy-start.3
  56.5 1.3 %copy-start = (bf16[5120,128]{1,0:T(8,128)(2,1)S(1)}, bf16[5120,128]{1,0:T(8,128)(2,1)}, u32[]{:S(2)}) copy-start(bf16[5120,128]{1,0:T(8,128)(2,1)} %all-gather.3.cloned.1.call-done) | copy-start | bytes 3932164
  57.8 1.0 %copy-start.4 = (bf16[256,1024]{1,0:T(8,128)(2,1)S(1)}, bf16[256,1024]{1,0:T(8,128)(2,1)}, u32[]{:S(2)}) copy-start(bf16[256,1024]{1,0:T(8,128)(2,1)} %copy-done.3) | copy-start | bytes 1572868
  58.8 1.2 %copy-start.7 = (bf16[256,2048]{1,0:T(8,128)(2,1)S(1)}, bf16[256,2048]{1,0:T(8,128)(2,1)}, u32[]{:S(2)}) copy-start(bf16[256,2048]{1,0:T(8,128)(2,1)} %query_ref.1) | copy-start | bytes 3145732
  60.1 0.9 %copy-start.11 = (bf16[256,512]{1,0:T(8,128)(2,1)S(1)}, bf16[256,512]{1,0:T(8,128)(2,1)}, u32[]{:S(2)}) copy-start(bf16[256,512]{1,0:T(8,128)(2,1)} %value_ref.1) | copy-start | bytes 786436
  61.0 0.9 %copy-start.13 = (f32[256,128]{1,0:T(8,128)S(1)}, f32[256,128]{1,0:T(8,128)}, u32[]{:S(2)}) copy-start(f32[256,128]{1,0:T(8,128)} %copy-done.12) | copy-start | bytes 393220
  61.9 6.8 %copy-start.1 = (bf16[5120,128]{1,0:T(8,128)(2,1)S(1)}, bf16[5120,128]{1,0:T(8,128)(2,1)}, u32[]{:S(2)}) copy-start(bf16[5120,128]{1,0:T(8,128)(2,1)} %all-gather.3.cloned.1.call-done) | copy-start | bytes 3932164
  61.9 6.8 %copy-start.2 = (bf16[256,4096]{1,0:T(8,128)(2,1)S(1)}, bf16[256,4096]{1,0:T(8,128)(2,1)}, u32[]{:S(2)}) copy-start(bf16[256,4096]{1,0:T(8,128)(2,1)} %gate_ref.1) | copy-start | bytes 6291460
  61.9 6.8 %copy-start.14 = (f32[256,128]{1,0:T(8,128)S(1)}, f32[256,128]{1,0:T(8,128)}, u32[]{:S(2)}) copy-start(f32[256,128]{1,0:T(8,128)} %copy-done.12) | copy-start | bytes 393220
  61.9 6.8 %copy-start.18 = (bf16[256,512]{1,0:T(8,128)(2,1)S(1)}, bf16[256,512]{1,0:T(8,128)(2,1)}, u32[]{:S(2)}) copy-start(bf16[256,512]{1,0:T(8,128)(2,1)} %read_ref.3) | copy-start | bytes 786436
  61.9 6.8 %copy-start.20 = (f32[256,128]{1,0:T(8,128)S(1)}, f32[256,128]{1,0:T(8,128)}, u32[]{:S(2)}) copy-start(f32[256,128]{1,0:T(8,128)} %copy-done.19) | copy-start | bytes 393220
  62.0 6.8 %copy-start.22 = (f32[4096]{0:T(1024)S(1)}, f32[4096]{0:T(1024)}, u32[]{:S(2)}) copy-start(f32[4096]{0:T(1024)} %param.23) | copy-start | bytes 49156
Sparse Core Ops, SparseCore 0:
  12.4 44.0 all-gather.2
where the time goes:
time: 82.5 us; the launch traced here: 81.8 us
  waiting for transfers between devices  22.3 us (27%)
  Pallas kernels  22.1 us (27%)
  local copies, waits for them, and re-layouts  16.2 us (20%)
  between operations  14.2 us (17%)
  starting transfers between devices  6.95 us (8%)
    all_gather x1, waiting for transfers between devices, local(): gathered = lax.all_gather(packed, 'reader', axis=0, tiled=False)  22.3 us
    unnamed x57, local copies, waits for them, and re-layouts  16.2 us
    ppermute x2, starting transfers between devices, shifted(): return lax.ppermute(value, axis, [(i, i + by) for i in range(length - by)])  6.91 us
    pallas_call x1, Pallas kernels, local(): pl.pallas_call(functools.partial(attend_kernel, state_rows=state_rows, pr...  6.72 us
    pallas_call x1, Pallas kernels, local(): pl.pallas_call(functools.partial(final_kernel, state_rows=state_rows, **s...  6.22 us
    pallas_call x1, Pallas kernels, local(): pl.pallas_call(functools.partial(inner_kernel, **sizes), grid=(groups,),...  4.64 us
    pallas_call x1, Pallas kernels, local(): pl.pallas_call(functools.partial(tail_kernel, **sizes), grid=(groups,), i...  3.7 us
  transfers between devices with their start and end apart: 3, of which 1 were waited for; matrix products, arithmetic and copies ran while one was open for 1% of the time, Pallas kernels for 18%

commit v1 on v0

--- a/solution.py
+++ b/solution.py
@@ -38,7 +38,7 @@
     return jnp.where(iota(value.shape, 1) < heads, high, value - high).astype(BF16)
 
 
-def pack_kernel(state_ref, keys_ref, values_ref, near_keys_ref, near_values_ref, out_ref, near_ref):
+def pack_kernel(state_ref, keys_ref, values_ref, out_ref):
     rows = state_ref.shape[0]
     out_ref[:rows, :] = state_ref[...].astype(BF16)
     parts = []
@@ -47,18 +47,16 @@
         for head in range(wide.shape[1] // HD):
             parts.append(wide[:, head * HD : (head + 1) * HD])
     out_ref[rows:, :] = jnp.concatenate(parts, axis=0).astype(BF16)
-    width = near_keys_ref.shape[1]
-    near_ref[:, :width] = near_keys_ref[...]
-    near_ref[:, width:] = near_values_ref[...]
 
 
 def tail_kernel(
-    base_ref,
     lengths_ref,
     raw_ref,
     rate_ref,
     x_ref,
     write_ref,
+    keys_ref,
+    values_ref,
     tail_ref,
     level_ref,
     column_ref,
@@ -75,7 +73,7 @@
 
     @pl.when(group == 0)
     def _():
-        base = base_ref[0, 0].astype(F32)
+        base = (lax.axis_index("reader") * tokens).astype(F32)
         lengths = lengths_ref[...].astype(F32)
         answers = lengths.shape[1]
         square = (answers, answers)
@@ -91,18 +89,21 @@
         source = iota(square, 1)
         mask = (source.astype(F32) >= wide) & (source <= iota(square, 0))
         mask = jnp.where(mask, 1.0, 0.0).astype(BF16)
-        raw = jnp.concatenate([raw_ref[...]] * 2, axis=1)
-        rate = jnp.concatenate([rate_ref[...]] * 2, axis=1)
+        raw = raw_ref[...]
+        rate = jnp.broadcast_to(rate_ref[...], (heads, heads))
+        diagonal = iota((heads, heads), 0) == iota((heads, heads), 1)
+        rate = jnp.sum(jnp.where(diagonal, rate, 0.0), axis=1, keepdims=True)
         step = jnp.maximum(raw, 0.0) + jnp.log1p(jnp.exp(-jnp.abs(raw)))
         falling = -rate * step
         first = falling.astype(BF16)
         rest = falling - first.astype(F32)
         second = rest.astype(BF16)
         third = (rest - second.astype(F32)).astype(BF16)
-        level = dot(mask, first) + (dot(mask, second) + dot(mask, third))
+        level = dot(first, mask, 1, 1) + (dot(second, mask, 1, 1) + dot(third, mask, 1, 1))
+        column_ref[...] = level * LOG2E - jnp.log(step) * LOG2E
+        level = jnp.concatenate([level, level], axis=0).T
+        step = jnp.concatenate([step, step], axis=0).T
         level_ref[...] = level
-        column = level * LOG2E - jnp.log(step) * LOG2E
-        column_ref[...] = column.T[:heads, :]
         last = level[tokens - 1 :, :]
         own = iota((tokens, 2 * heads), 0).astype(F32) >= start[tokens - 1 :, : 2 * heads]
         weight = jnp.where(own, jnp.exp(last - level) * step, 0.0)
@@ -111,8 +112,14 @@
         high = decay.astype(BF16).astype(F32)
         row = iota(decay.shape, 0)
         decay = jnp.where(row == 0, high, jnp.where(row == 1, decay - high, 0.0))
-        tail_ref[:, columns:] = jnp.zeros((tail_ref.shape[0], 2 * heads), BF16)
-        tail_ref[:16, columns:] = decay.astype(BF16)
+        at = columns + 2 * heads
+        tail_ref[:, columns:at] = jnp.zeros((tail_ref.shape[0], 2 * heads), BF16)
+        tail_ref[:16, columns:at] = decay.astype(BF16)
+        depth, width = tail_ref.shape[0], keys_ref.shape[1]
+        for ref in (keys_ref, values_ref):
+            for half in range(tokens // depth):
+                tail_ref[:, at : at + width] = ref[half * depth : (half + 1) * depth, :]
+                at += width
 
     spread = expander(heads, group, per_group, channels)
     weight = dot(weight_ref[...], spread)
@@ -175,19 +182,18 @@
     query_ref,
     key_ref,
     value_ref,
-    prior_key_ref,
-    prior_value_ref,
-    gathered_ref,
-    out_ref,
-    bias_ref,
-    *,
+    mine_ref,
+    other_ref,
+    *rest,
+    halves,
     state_rows,
     prompt_rows,
     kv_count,
 ):
+    prior_refs, (out_ref, bias_ref) = rest[:-2], rest[-2:]
     head = pl.program_id(0)
     tokens = query_ref.shape[0]
-    devices = gathered_ref.shape[0]
+    devices = 2 * mine_ref.shape[0]
     scale = LOG2E / math.sqrt(HD)
 
     @pl.when(head == 0)
@@ -200,7 +206,8 @@
 
     def prompt(which):
         at = pl.multiple_of(state_rows + (which * kv_count + head) // 2 * 2 * prompt_rows, 16)
-        pair = gathered_ref[:, pl.ds(at, 2 * prompt_rows), :].astype(F32)
+        at = pl.ds(at, 2 * prompt_rows)
+        pair = jnp.concatenate([mine_ref[:, at, :], other_ref[:, at, :]], axis=0).astype(F32)
         odd = lax.rem(head, 2) == 1
         part = jnp.where(odd, pair[:, prompt_rows:, :], pair[:, :prompt_rows, :])
         return part.reshape(devices * prompt_rows, HD).astype(BF16)
@@ -211,13 +218,10 @@
     prompt_values = jnp.concatenate(
         [prompt_values, jnp.ones((prompt_values.shape[0], LANES), BF16)], axis=1
     )
-    near_keys = jnp.concatenate([prior_key_ref[...], key_ref[...]], axis=0)
+    near_keys = jnp.concatenate([ref[...] for ref in prior_refs[:halves]] + [key_ref[...]], axis=0)
+    near_values = [ref[...] for ref in prior_refs[halves:]] + [value_ref[...]]
     near_values = jnp.concatenate(
-        [
-            jnp.concatenate([prior_value_ref[...], ones], axis=1),
-            jnp.concatenate([value_ref[...], ones], axis=1),
-        ],
-        axis=0,
+        [jnp.concatenate(near_values, axis=0), jnp.concatenate([ones, ones], axis=0)], axis=1
     )
     for query in range(query_ref.shape[1] // HD):
         at = slice(query * HD, (query + 1) * HD)
@@ -241,7 +245,8 @@
     level_ref,
     tail_ref,
     decay_ref,
-    gathered_ref,
+    mine_ref,
+    other_ref,
     read_ref,
     inner_ref,
     gate_ref,
@@ -262,8 +267,12 @@
     spread = expander(heads, group, per_group, channels)
     from_prompt = dot(two_parts(jnp.where(carried, level * decay, level), heads), spread)
     from_prior = dot(two_parts(jnp.where(carried, level, 0.0), heads), spread)
-    seeds = gathered_ref[:, :state_rows, :]
-    seeds = seeds.reshape(seeds.shape[0] * state_rows, seeds.shape[2])
+    odd = lax.rem(lax.axis_index("reader"), 2) == 1
+    seeds = []
+    for pair in range(mine_ref.shape[0]):
+        mine, other = mine_ref[pair, :state_rows, :], other_ref[pair, :state_rows, :]
+        seeds += [jnp.where(odd, other, mine), jnp.where(odd, mine, other)]
+    seeds = jnp.concatenate(seeds, axis=0)
     read = read_ref[...]
     mixed = inner_ref[...].astype(F32)
     mixed = mixed + from_prompt * dot(read, seeds, 1, 1)
@@ -279,7 +288,7 @@
     return lax.ppermute(value, axis, [(i, i + by) for i in range(length - by)])
 
 
-def params(limit=40):
+def params(limit=32):
     return pltpu.CompilerParams(vmem_limit_bytes=limit * MIB)
 
 
@@ -314,44 +323,55 @@
     prompt_rows, kv_width = prompt_keys.shape
     kv_count = kv_width // HD
     devices = lax.axis_size("reader")
-    base = (lax.axis_index("reader") * tokens).astype(jnp.int32).reshape(1, 1)
-    lengths = answer_lengths.reshape(1, -1)
+    in_hbm = lambda value: pltpu.with_memory_space_constraint(value, pltpu.MemorySpace.HBM)
+    mixer_input, gate_input, state_write, state_read = map(
+        in_hbm, (mixer_input, gate_input, state_write, state_read)
+    )
+    prompt_state, queries, answer_keys, answer_values, prompt_keys, prompt_values = map(
+        in_hbm, (prompt_state, queries, answer_keys, answer_values, prompt_keys, prompt_values)
+    )
+    lengths, rate, skip, gain = map(
+        lambda value: in_hbm(value.reshape(1, -1)),
+        (answer_lengths, decay_rate, skip_gain, norm_gain),
+    )
     sizes = dict(heads=heads, per_group=per_group, channels=channels)
     packed_rows = state_rows + 2 * prompt_rows * kv_count
 
-    packed, near = pl.pallas_call(
+    packed = pl.pallas_call(
         pack_kernel,
-        out_shape=(
-            jax.ShapeDtypeStruct((packed_rows, HD), BF16),
-            jax.ShapeDtypeStruct((tokens, 2 * kv_width), BF16),
-        ),
-        compiler_params=params(16),
+        out_shape=jax.ShapeDtypeStruct((packed_rows, HD), BF16),
+        compiler_params=params(),
         name="pack",
-    )(prompt_state, prompt_keys, prompt_values, answer_keys, answer_values)
-    gathered = lax.all_gather(packed, "reader", axis=0, tiled=False)
-    prior = shifted(near, "reader", 1)
-
+    )(prompt_state, prompt_keys, prompt_values)
+    lanes_of = [list(range(first, devices, 2)) for first in range(2)]
+    mine = lax.all_gather(packed, "reader", axis=0, tiled=False, axis_index_groups=lanes_of)
+    packed, raw = lax.optimization_barrier((packed, step_raw.T))
+    raw = in_hbm(raw)
+
+    halves = tokens // state
+    tail_width = columns + 2 * heads + 2 * halves * kv_width
     by_group = lambda rows: pl.BlockSpec((rows, state), lambda g: (0, g))
     wide = pl.BlockSpec((tokens, width), lambda g: (0, g))
     tail, level, column, start = pl.pallas_call(
         functools.partial(tail_kernel, **sizes),
         grid=(groups,),
         in_specs=[
-            pl.BlockSpec(memory_space=pltpu.SMEM),
             whole(lengths.shape),
-            whole(step_raw.shape),
+            whole(raw.shape),
             whole((1, heads)),
             wide,
             by_group(tokens),
+            whole(answer_keys.shape),
+            whole(answer_values.shape),
         ],
         out_specs=(
-            whole((state, columns + 2 * heads)),
+            whole((state, tail_width)),
             whole((tokens, 2 * heads)),
             whole((heads, tokens)),
             whole((tokens, LANES)),
         ),
         out_shape=(
-            jax.ShapeDtypeStruct((state, columns + 2 * heads), BF16),
+            jax.ShapeDtypeStruct((state, tail_width), BF16),
             jax.ShapeDtypeStruct((tokens, 2 * heads), F32),
             jax.ShapeDtypeStruct((heads, tokens), F32),
             jax.ShapeDtypeStruct((tokens, LANES), F32),
@@ -359,7 +379,7 @@
         scratch_shapes=[pltpu.VMEM((tokens, 2 * heads), BF16)],
         compiler_params=params(),
         name="tail",
-    )(base, lengths, step_raw, decay_rate.reshape(1, -1), mixer_input, state_write)
+    )(lengths, raw, rate, mixer_input, state_write, answer_keys, answer_values)
     tail = shifted(tail, "reader", 1)
 
     inner = pl.pallas_call(
@@ -383,12 +403,23 @@
             transcendentals=heads * tokens * tokens,
         ),
         name="inner",
-    )(start, level, column, skip_gain.reshape(1, -1), mixer_input, state_write, state_read)
-
+    )(start, level, column, skip, mixer_input, state_write, state_read)
+
+    mine, inner = lax.optimization_barrier((mine, inner))
+    other = lax.ppermute(mine, "reader", [(i, i ^ 1) for i in range(devices)])
+    mine = in_hbm(mine)
+    prior_at = (columns + 2 * heads) // HD
+    prior_part = lambda part: pl.BlockSpec(
+        (state, HD), lambda k: (0, prior_at + part * kv_count + k)
+    )
     group_size = queries.shape[1] // kv_width
     attention_out = pl.pallas_call(
         functools.partial(
-            attend_kernel, state_rows=state_rows, prompt_rows=prompt_rows, kv_count=kv_count
+            attend_kernel,
+            halves=halves,
+            state_rows=state_rows,
+            prompt_rows=prompt_rows,
+            kv_count=kv_count,
         ),
         grid=(kv_count,),
         in_specs=[
@@ -396,16 +427,16 @@
             pl.BlockSpec((tokens, group_size * HD), lambda k: (0, k)),
             pl.BlockSpec((tokens, HD), lambda k: (0, k)),
             pl.BlockSpec((tokens, HD), lambda k: (0, k)),
-            pl.BlockSpec((tokens, HD), lambda k: (0, k)),
-            pl.BlockSpec((tokens, HD), lambda k: (0, kv_count + k)),
-            whole((devices, packed_rows, HD)),
-        ],
+            whole((devices // 2, packed_rows, HD)),
+            whole((devices // 2, packed_rows, HD)),
+        ]
+        + [prior_part(part) for part in range(2 * halves)],
         out_specs=pl.BlockSpec((tokens, group_size * HD), lambda k: (0, k)),
         out_shape=jax.ShapeDtypeStruct(queries.shape, BF16),
         scratch_shapes=[pltpu.VMEM((tokens, 2 * tokens), F32)],
         compiler_params=params(),
         name="attend",
-    )(start, queries, answer_keys, answer_values, prior, prior, gathered)
+    )(start, queries, answer_keys, answer_values, mine, other, *[tail] * (2 * halves))
 
     mixer_out = pl.pallas_call(
         functools.partial(final_kernel, state_rows=state_rows, **sizes),
@@ -415,7 +446,8 @@
             whole((tokens, 2 * heads)),
             pl.BlockSpec((state, width), lambda g: (0, g)),
             pl.BlockSpec((16, 2 * heads), lambda g: (0, columns // (2 * heads))),
-            pl.BlockSpec((devices // groups, packed_rows, HD), lambda g: (g, 0, 0)),
+            pl.BlockSpec((devices // groups // 2, packed_rows, HD), lambda g: (g, 0, 0)),
+            pl.BlockSpec((devices // groups // 2, packed_rows, HD), lambda g: (g, 0, 0)),
             by_group(tokens),
             wide,
             wide,
@@ -425,7 +457,7 @@
         out_shape=jax.ShapeDtypeStruct((tokens, columns), BF16),
         compiler_params=params(),
         name="final",
-    )(start, level, tail, tail, gathered, state_read, inner, gate_input, norm_gain.reshape(1, -1))
+    )(start, level, tail, tail, mine, other, state_read, inner, gate_input, gain)
     return (mixer_out, attention_out)
 
 

time: 82.5 us -> 74.5 us (0.903)
  blocking collectives: 0 us -> 43 us
  waiting for transfers between devices: 22.3 us -> 2.1 us
  local copies, waits for them, and re-layouts: 16.2 us -> 0.01 us
  between operations: 14.2 us -> 0.66 us
  starting transfers between devices: 6.95 us -> 2.46 us
  Pallas kernels: 22.1 us -> 25.8 us
    all_gather x0 -> x1, blocking collectives: none -> 43 us  [local(): lax.all_gather(packed, 'reader', axis=0, tiled=False, axis_index_groups=l...]
    all_gather x1 -> x0, waiting for transfers between devices: 22.3 us -> none  [local(): gathered = lax.all_gather(packed, 'reader', axis=0, tiled=False)]
    unnamed x57 -> x2, local copies, waits for them, and re-layouts: 16.2 us -> 0.01 us
    ppermute x2 -> x1, starting transfers between devices: 6.91 us -> 2.46 us  [shifted(): return lax.ppermute(value, axis, [(i, i + by) for i in range(length - by)])]
    ppermute x0 -> x1, waiting for transfers between devices: none -> 2.1 us  [local(): other = lax.ppermute(mine, 'reader', [(i, i ^ 1) for i in range(devices)])]
    pallas_call x2, Pallas kernels: 7.59 us -> 8.77 us  [the longest x1 7.84 us: local(): pl.pallas_call(functools.partial(attend_kernel, halves=halves, state_rows...]
    pallas_call x1, Pallas kernels: 6.22 us -> 7.07 us  [local(): pl.pallas_call(functools.partial(final_kernel, state_rows=state_rows, **s...]
    pallas_call x1, Pallas kernels: 4.64 us -> 5.47 us  [local(): pl.pallas_call(functools.partial(inner_kernel, **sizes), grid=(groups,),...]
  transfers between devices with their start and end apart: 3 -> 2, of which waited for: 1 -> 1; matrix products, arithmetic and copies ran while one was open for 1% -> 0% of each run, Pallas kernels for 18% -> 7%
where the time goes in v1:
time: 74.5 us; the launch traced here: 74.1 us
  blocking collectives  43 us (58%)
  Pallas kernels  25.8 us (35%)
  starting transfers between devices  2.46 us (3%)
  waiting for transfers between devices  2.1 us (3%)
    all_gather x1, blocking collectives, local(): lax.all_gather(packed, 'reader', axis=0, tiled=False, axis_index_groups=l...  43 us
    pallas_call x1, Pallas kernels, local(): pl.pallas_call(functools.partial(attend_kernel, halves=halves, state_rows...  7.84 us
    pallas_call x1, Pallas kernels, local(): pl.pallas_call(functools.partial(final_kernel, state_rows=state_rows, **s...  7.07 us
    pallas_call x1, Pallas kernels, local(): pl.pallas_call(functools.partial(inner_kernel, **sizes), grid=(groups,),...  5.47 us
    pallas_call x1, Pallas kernels, local(): pl.pallas_call(functools.partial(tail_kernel, **sizes), grid=(groups,), i...  4.53 us
    ppermute x1, starting transfers between devices, shifted(): return lax.ppermute(value, axis, [(i, i + by) for i in range(length - by)])  2.46 us
    ppermute x1, waiting for transfers between devices, local(): other = lax.ppermute(mine, 'reader', [(i, i ^ 1) for i in range(devices)])  2.1 us
  transfers between devices with their start and end apart: 2, of which 1 were waited for; matrix products, arithmetic and copies ran while one was open for 0% of the time, Pallas kernels for 7%

profile of v1, /device:TPU:0, one launch (start us, length us, event | category | flops | bytes accessed | tf_op | source)
XLA Modules:
  0.0 74.1 jit_solution(313418459938935018)
XLA Ops:
  0.6 0.9 %pack.1 = bf16[320,128]{1,0:T(8,128)(2,1)S(1)} custom-call(f32[256,128]{1,0:T(8,128)} %state_ref.1, bf16[8,512]{1,0:T(8,128)(2,1)} %keys_ref.2, bf16[8,512]{1,0:T(8,128)(2,1)} %values_ref.2), custom_call_target="tpu_custom_call" | custom-call | tf_op jit(solution)/shard_map/pack/pallas_call | solution.py:340
  1.6 4.5 %tail.1 = (bf16[128,6272]{1,0:T(8,128)(2,1)S(1)}, f32[256,128]{1,0:T(8,128)S(1)}, f32[64,256]{1,0:T(8,128)S(1)}, f32[256,128]{1,0:T(8,128)S(1)}) custom-call(s32[1,32]{1,0:T(1,128)} %bitcast.11, f32[64,256]{1,0:T(8,128)} %bitcast.9, f32[1,64]{1,0:T(1,128)} %bitcast.12, bf16[256,4096]{1,0:T(8,128)(2,1)} %x_ref.3, bf16[256,512]{1,0:T(8,128)(2,1)} %write_ref.3, ...), custom_call_target="tpu_custom_call" | custom-call | tf_op jit(solution)/shard_map/tail/pallas_call | solution.py:355
  6.1 2.5 %collective-permute-start = (bf16[128,6272]{1,0:T(8,128)(2,1)S(1)}, bf16[128,6272]{1,0:T(8,128)(2,1)S(1)}, u32[]{:S(2)}, u32[]{:S(2)}) collective-permute-start(bf16[128,6272]{1,0:T(8,128)(2,1)S(1)} %get-tuple-element.12), channel_id=1, source_target_pairs={{0,1},{1,2},{2,3},{3,4},{4,5},{5,6},{6,7},{7,8},{8,9},{9,10},{10,1... | collective-permute-start | bytes 4816904 | tf_op jit(solution)/shard_map/ppermute | solution.py:288
  8.6 5.5 %inner.1.inner_ref = bf16[256,4096]{1,0:T(8,128)(2,1)S(1)} custom-call(f32[256,128]{1,0:T(8,128)S(1)} %get-tuple-element.10.start_ref, f32[256,128]{1,0:T(8,128)S(1)} %get-tuple-element.11.level_ref, f32[64,256]{1,0:T(8,128)S(1)} %get-tuple-element.13.column_ref, f32[1,64]{1,0:T(1,128)} %bitcast.13, bf16[256,4096]{1,0:T(8,128)(2,1)} %x_ref.3, ...), custom_call_target="tpu_custom_call" | custom-call | flops 2147483648 | bytes 4194304 | tf_op jit(solution)/shard_map/inner/pallas_call | solution.py:385
  14.1 43.0 %all-gather = bf16[2560,128]{1,0:T(8,128)(2,1)S(1)} all-gather(bf16[320,128]{1,0:T(8,128)(2,1)S(1)} %pack.1), channel_id=2, replica_groups={{0,2,4,6,8,10,12,14},{1,3,5,7,9,11,13,15},{16,18,20,22,24,26,28,30},{17..., dimensions={0}, use_global_device_ids=true | all-gather | bytes 737280 | tf_op jit(solution)/shard_map/all_gather | solution.py:347
  57.1 0.0 copy-start
  57.1 0.0 collective-permute-start.1
  57.1 2.1 %collective-permute-done.1.other_ref = bf16[8,320,128]{2,1,0:T(8,128)(2,1)S(1)} collective-permute-done((bf16[8,320,128]{2,1,0:T(8,128)(2,1)S(1)}, bf16[8,320,128]{2,1,0:T(8,128)(2,1)S(1)}, u32[]{:S(2)}, u32[]{:S(2)}) %collective-permute-start.1) | collective-permute-done | bytes 655392 | tf_op jit(solution)/shard_map/ppermute | solution.py:409
  59.2 0.0 collective-permute-done.tail_ref.decay_ref.rest_0_.rest_1_.rest_2_.rest_3_
  59.2 0.0 copy-done
  59.2 7.8 %attend.1 = bf16[256,2048]{1,0:T(8,128)(2,1)} custom-call(f32[256,128]{1,0:T(8,128)S(1)} %get-tuple-element.10.start_ref, bf16[256,2048]{1,0:T(8,128)(2,1)} %query_ref.1, bf16[256,512]{1,0:T(8,128)(2,1)} %key_ref.1, bf16[256,512]{1,0:T(8,128)(2,1)} %value_ref.1, bf16[8,320,128]{2,1,0:T(8,128)(2,1)} %bitcast.7, ...), custom_call_target="tpu_custom_call" | custom-call | tf_op jit(solution)/shard_map/attend/pallas_call | solution.py:416
  67.0 7.1 %final.1 = bf16[256,4096]{1,0:T(8,128)(2,1)} custom-call(f32[256,128]{1,0:T(8,128)S(1)} %get-tuple-element.10.start_ref, f32[256,128]{1,0:T(8,128)S(1)} %get-tuple-element.11.level_ref, bf16[128,6272]{1,0:T(8,128)(2,1)S(1)} %collective-permute-done.tail_ref.decay_ref.rest_0_.rest_1_.rest_2_.rest_3_, ...), custom_call_target="tpu_custom_call" | custom-call | tf_op jit(solution)/shard_map/final/pallas_call | solution.py:441
Async XLA Ops:
  6.1 53.1 %collective-permute-start = (bf16[128,6272]{1,0:T(8,128)(2,1)S(1)}, bf16[128,6272]{1,0:T(8,128)(2,1)S(1)}, u32[]{:S(2)}, u32[]{:S(2)}) collective-permute-start(bf16[128,6272]{1,0:T(8,128)(2,1)S(1)} %get-tuple-element.12), channel_id=1, source_target_pairs={{0,1},{1,2},{2,3},{3,4},{4,5},{5,6},{6,7},{7,8},{8,9},{9,10},{10,1... | collective-permute-start | bytes 4816904 | tf_op jit(solution)/shard_map/ppermute | solution.py:288
  57.1 2.1 %copy-start = (bf16[2560,128]{1,0:T(8,128)(2,1)}, bf16[2560,128]{1,0:T(8,128)(2,1)S(1)}, u32[]{:S(2)}) copy-start(bf16[2560,128]{1,0:T(8,128)(2,1)S(1)} %all-gather) | copy-start | bytes 1966084
  57.1 2.1 %collective-permute-start.1 = (bf16[8,320,128]{2,1,0:T(8,128)(2,1)S(1)}, bf16[8,320,128]{2,1,0:T(8,128)(2,1)S(1)}, u32[]{:S(2)}, u32[]{:S(2)}) collective-permute-start(bf16[8,320,128]{2,1,0:T(8,128)(2,1)S(1)} %bitcast.6), channel_id=1, source_target_pairs={{0,1},{1,0},{2,3},{3,2},{4,5},{5,4},{6,7},{7,6},{8,9},{9,8},{10,11... | collective-permute-start | bytes 1966088 | tf_op jit(solution)/shard_map/ppermute | solution.py:409

commit v2 on v1

--- a/solution.py
+++ b/solution.py
@@ -40,13 +40,16 @@
 
 def pack_kernel(state_ref, keys_ref, values_ref, out_ref):
     rows = state_ref.shape[0]
-    out_ref[:rows, :] = state_ref[...].astype(BF16)
+    state = state_ref[...].astype(BF16)
     parts = []
     for ref in (keys_ref, values_ref):
         wide = ref[...].astype(F32)
         for head in range(wide.shape[1] // HD):
             parts.append(wide[:, head * HD : (head + 1) * HD])
-    out_ref[rows:, :] = jnp.concatenate(parts, axis=0).astype(BF16)
+    parts = jnp.concatenate(parts, axis=0).astype(BF16)
+    for copy in range(out_ref.shape[0]):
+        out_ref[copy, :rows, :] = state
+        out_ref[copy, rows:, :] = parts
 
 
 def tail_kernel(
@@ -339,13 +342,13 @@
 
     packed = pl.pallas_call(
         pack_kernel,
-        out_shape=jax.ShapeDtypeStruct((packed_rows, HD), BF16),
+        out_shape=jax.ShapeDtypeStruct((devices // 2, packed_rows, HD), BF16),
         compiler_params=params(),
         name="pack",
     )(prompt_state, prompt_keys, prompt_values)
     lanes_of = [list(range(first, devices, 2)) for first in range(2)]
-    mine = lax.all_gather(packed, "reader", axis=0, tiled=False, axis_index_groups=lanes_of)
     packed, raw = lax.optimization_barrier((packed, step_raw.T))
+    mine = lax.all_to_all(packed, "reader", 0, 0, axis_index_groups=lanes_of, tiled=True)
     raw = in_hbm(raw)
 
     halves = tokens // state
@@ -407,7 +410,6 @@
 
     mine, inner = lax.optimization_barrier((mine, inner))
     other = lax.ppermute(mine, "reader", [(i, i ^ 1) for i in range(devices)])
-    mine = in_hbm(mine)
     prior_at = (columns + 2 * heads) // HD
     prior_part = lambda part: pl.BlockSpec(
         (state, HD), lambda k: (0, prior_at + part * kv_count + k)

time: 74.5 us -> 56.6 us (0.76)
  the two profiles are of different devices: /device:TPU:0 before, /device:TPU:18 now
where the time goes in v2:
time: 56.6 us; the launch traced here: 56.2 us
  Pallas kernels  27.4 us (48%)
  waiting for transfers between devices  17.2 us (30%)
  starting transfers between devices  9.65 us (17%)
  local copies, waits for them, and re-layouts  1.32 us (2%)
  between operations  0.66 us (1%)
    ppermute x1, waiting for transfers between devices, shifted(): return lax.ppermute(value, axis, [(i, i + by) for i in range(length - by)])  17.2 us
    pallas_call x1, Pallas kernels, local(): pl.pallas_call(functools.partial(attend_kernel, halves=halves, state_rows...  7.49 us
    pallas_call x1, Pallas kernels, local(): pl.pallas_call(functools.partial(final_kernel, state_rows=state_rows, **s...  7 us
    all_to_all x1, starting transfers between devices, local(): lax.all_to_all(packed, 'reader', 0, 0, axis_index_groups=lanes_of, tiled=...  6.17 us
    pallas_call x1, Pallas kernels, local(): pl.pallas_call(functools.partial(tail_kernel, **sizes), grid=(groups,), i...  5.63 us
    pallas_call x1, Pallas kernels, local(): pl.pallas_call(functools.partial(inner_kernel, **sizes), grid=(groups,),...  5.47 us
    ppermute x1, starting transfers between devices, shifted(): return lax.ppermute(value, axis, [(i, i + by) for i in range(length - by)])  1.91 us
    pallas_call x1, Pallas kernels, local(): pl.pallas_call(pack_kernel, out_shape=jax.ShapeDtypeStruct((devices // 2,...  1.81 us
  transfers between devices with their start and end apart: 3, of which 1 were waited for; matrix products, arithmetic and copies ran while one was open for 0% of the time, Pallas kernels for 20%

profile of v2, /device:TPU:18, one launch (start us, length us, event | category | flops | bytes accessed | tf_op | source)
XLA Modules:
  0.0 56.2 jit_solution(15426525578468321483)
XLA Ops:
  0.6 1.8 %pack.1 = bf16[8,320,128]{2,1,0:T(8,128)(2,1)} custom-call(f32[256,128]{1,0:T(8,128)} %state_ref.1, bf16[8,512]{1,0:T(8,128)(2,1)} %keys_ref.2, bf16[8,512]{1,0:T(8,128)(2,1)} %values_ref.2), custom_call_target="tpu_custom_call" | custom-call | tf_op jit(solution)/shard_map/pack/pallas_call | solution.py:343
  2.4 6.2 %all-to-all-start = ((bf16[8,320,128]{2,1,0:T(8,128)(2,1)}), bf16[8,320,128]{2,1,0:T(8,128)(2,1)S(1)}, u32[]{:S(2)}, u32[]{:S(2)}) async-start(bf16[8,320,128]{2,1,0:T(8,128)(2,1)} %pack.1), calls=%async_computation | async-start | bytes 1310720 | tf_op jit(solution)/shard_map/all_to_all | solution.py:351
  8.6 5.6 %tail.1 = (bf16[128,6272]{1,0:T(8,128)(2,1)}, f32[256,128]{1,0:T(8,128)S(1)}, f32[64,256]{1,0:T(8,128)S(1)}, f32[256,128]{1,0:T(8,128)S(1)}) custom-call(s32[1,32]{1,0:T(1,128)} %bitcast.7, f32[64,256]{1,0:T(8,128)} %bitcast.5, f32[1,64]{1,0:T(1,128)} %bitcast.8, bf16[256,4096]{1,0:T(8,128)(2,1)} %x_ref.3, bf16[256,512]{1,0:T(8,128)(2,1)} %write_ref.3, ...), custom_call_target="tpu_custom_call" | custom-call | tf_op jit(solution)/shard_map/tail/pallas_call | solution.py:358
  14.2 1.9 %collective-permute-start = (bf16[128,6272]{1,0:T(8,128)(2,1)}, bf16[128,6272]{1,0:T(8,128)(2,1)S(1)}, u32[]{:S(2)}, u32[]{:S(2)}) collective-permute-start(bf16[128,6272]{1,0:T(8,128)(2,1)} %get-tuple-element.13), channel_id=1, source_target_pairs={{0,1},{1,2},{2,3},{3,4},{4,5},{5,6},{6,7},{7,8},{8,9},{9,10},{10,1... | collective-permute-start | bytes 4816904 | tf_op jit(solution)/shard_map/ppermute | solution.py:291
  16.2 5.5 %inner.1.inner_ref = bf16[256,4096]{1,0:T(8,128)(2,1)S(1)} custom-call(f32[256,128]{1,0:T(8,128)S(1)} %get-tuple-element.11.start_ref, f32[256,128]{1,0:T(8,128)S(1)} %get-tuple-element.12.level_ref, f32[64,256]{1,0:T(8,128)S(1)} %get-tuple-element.15.column_ref, f32[1,64]{1,0:T(1,128)} %bitcast.9, bf16[256,4096]{1,0:T(8,128)(2,1)} %x_ref.3, ...), custom_call_target="tpu_custom_call" | custom-call | flops 2147483648 | bytes 4194304 | tf_op jit(solution)/shard_map/inner/pallas_call | solution.py:388
  21.6 0.0 copy-start
  21.7 1.3 %copy-done = bf16[256,4096]{1,0:T(8,128)(2,1)} copy-done((bf16[256,4096]{1,0:T(8,128)(2,1)}, bf16[256,4096]{1,0:T(8,128)(2,1)S(1)}, u32[]{:S(2)}) %copy-start) | copy-done | bytes 2097176
  23.0 0.0 all-to-all-done.mine_ref
  23.0 0.0 copy-start.1
  23.0 1.6 %collective-permute-start.1 = (bf16[8,320,128]{2,1,0:T(8,128)(2,1)S(1)}, bf16[8,320,128]{2,1,0:T(8,128)(2,1)S(1)}, u32[]{:S(2)}, u32[]{:S(2)}) collective-permute-start(bf16[8,320,128]{2,1,0:T(8,128)(2,1)S(1)} %all-to-all-done.mine_ref), channel_id=1, source_target_pairs={{0,1},{1,0},{2,3},{3,2},{4,5},{5,4},{6,7},{7,6},{8,9},{9,8},{10,11... | collective-permute-start | bytes 1966088 | tf_op jit(solution)/shard_map/ppermute | solution.py:412
  24.5 17.2 %collective-permute-done.tail_ref.decay_ref.rest_0_.rest_1_.rest_2_.rest_3_ = bf16[128,6272]{1,0:T(8,128)(2,1)S(1)} collective-permute-done((bf16[128,6272]{1,0:T(8,128)(2,1)}, bf16[128,6272]{1,0:T(8,128)(2,1)S(1)}, u32[]{:S(2)}, u32[]{:S(2)}) %collective-permute-start) | collective-permute-done | bytes 1605664 | tf_op jit(solution)/shard_map/ppermute | solution.py:291
  41.7 0.0 collective-permute-done.1.other_ref
  41.7 7.5 %attend.1 = bf16[256,2048]{1,0:T(8,128)(2,1)} custom-call(f32[256,128]{1,0:T(8,128)S(1)} %get-tuple-element.11.start_ref, bf16[256,2048]{1,0:T(8,128)(2,1)} %query_ref.1, bf16[256,512]{1,0:T(8,128)(2,1)} %key_ref.1, bf16[256,512]{1,0:T(8,128)(2,1)} %value_ref.1, bf16[8,320,128]{2,1,0:T(8,128)(2,1)S(1)} %all-to-all-done.mine_ref, ...), custom_call_target="tpu_custom_call" | custom-call | tf_op jit(solution)/shard_map/attend/pallas_call | solution.py:418
  49.2 0.0 copy-done.1
  49.2 7.0 %final.1 = bf16[256,4096]{1,0:T(8,128)(2,1)} custom-call(f32[256,128]{1,0:T(8,128)S(1)} %get-tuple-element.11.start_ref, f32[256,128]{1,0:T(8,128)S(1)} %get-tuple-element.12.level_ref, bf16[128,6272]{1,0:T(8,128)(2,1)S(1)} %collective-permute-done.tail_ref.decay_ref.rest_0_.rest_1_.rest_2_.rest_3_, ...), custom_call_target="tpu_custom_call" | custom-call | tf_op jit(solution)/shard_map/final/pallas_call | solution.py:443
Async XLA Ops:
  2.4 20.5 %all-to-all-start = ((bf16[8,320,128]{2,1,0:T(8,128)(2,1)}), bf16[8,320,128]{2,1,0:T(8,128)(2,1)S(1)}, u32[]{:S(2)}, u32[]{:S(2)}) async-start(bf16[8,320,128]{2,1,0:T(8,128)(2,1)} %pack.1), calls=%async_computation | async-start | bytes 1310720 | tf_op jit(solution)/shard_map/all_to_all | solution.py:351
  14.2 27.5 %collective-permute-start = (bf16[128,6272]{1,0:T(8,128)(2,1)}, bf16[128,6272]{1,0:T(8,128)(2,1)S(1)}, u32[]{:S(2)}, u32[]{:S(2)}) collective-permute-start(bf16[128,6272]{1,0:T(8,128)(2,1)} %get-tuple-element.13), channel_id=1, source_target_pairs={{0,1},{1,2},{2,3},{3,4},{4,5},{5,6},{6,7},{7,8},{8,9},{9,10},{10,1... | collective-permute-start | bytes 4816904 | tf_op jit(solution)/shard_map/ppermute | solution.py:291
  21.6 1.3 %copy-start = (bf16[256,4096]{1,0:T(8,128)(2,1)}, bf16[256,4096]{1,0:T(8,128)(2,1)S(1)}, u32[]{:S(2)}) copy-start(bf16[256,4096]{1,0:T(8,128)(2,1)S(1)} %inner.1.inner_ref) | copy-start | bytes 6291460
  23.0 26.2 %copy-start.1 = (bf16[256,4096]{1,0:T(8,128)(2,1)S(1)}, bf16[256,4096]{1,0:T(8,128)(2,1)}, u32[]{:S(2)}) copy-start(bf16[256,4096]{1,0:T(8,128)(2,1)} %copy-done) | copy-start | bytes 6291460
  23.0 18.7 %collective-permute-start.1 = (bf16[8,320,128]{2,1,0:T(8,128)(2,1)S(1)}, bf16[8,320,128]{2,1,0:T(8,128)(2,1)S(1)}, u32[]{:S(2)}, u32[]{:S(2)}) collective-permute-start(bf16[8,320,128]{2,1,0:T(8,128)(2,1)S(1)} %all-to-all-done.mine_ref), channel_id=1, source_target_pairs={{0,1},{1,0},{2,3},{3,2},{4,5},{5,4},{6,7},{7,6},{8,9},{9,8},{10,11... | collective-permute-start | bytes 1966088 | tf_op jit(solution)/shard_map/ppermute | solution.py:412

commit v3 on v2

--- a/solution.py
+++ b/solution.py
@@ -10,6 +10,7 @@
 
 HD = 128
 LANES = 128
+NEAR = 4
 LOG2E = 1.4426950408889634
 F32 = jnp.float32
 BF16 = jnp.bfloat16
@@ -38,7 +39,7 @@
     return jnp.where(iota(value.shape, 1) < heads, high, value - high).astype(BF16)
 
 
-def pack_kernel(state_ref, keys_ref, values_ref, out_ref):
+def pack_kernel(state_ref, keys_ref, values_ref, near_keys_ref, near_values_ref, out_ref, near_ref):
     rows = state_ref.shape[0]
     state = state_ref[...].astype(BF16)
     parts = []
@@ -50,6 +51,9 @@
     for copy in range(out_ref.shape[0]):
         out_ref[copy, :rows, :] = state
         out_ref[copy, rows:, :] = parts
+    width = near_keys_ref.shape[1]
+    near_ref[:, :width] = near_keys_ref[...]
+    near_ref[:, width:] = near_values_ref[...]
 
 
 def tail_kernel(
@@ -58,8 +62,6 @@
     rate_ref,
     x_ref,
     write_ref,
-    keys_ref,
-    values_ref,
     tail_ref,
     level_ref,
     column_ref,
@@ -115,14 +117,8 @@
         high = decay.astype(BF16).astype(F32)
         row = iota(decay.shape, 0)
         decay = jnp.where(row == 0, high, jnp.where(row == 1, decay - high, 0.0))
-        at = columns + 2 * heads
-        tail_ref[:, columns:at] = jnp.zeros((tail_ref.shape[0], 2 * heads), BF16)
-        tail_ref[:16, columns:at] = decay.astype(BF16)
-        depth, width = tail_ref.shape[0], keys_ref.shape[1]
-        for ref in (keys_ref, values_ref):
-            for half in range(tokens // depth):
-                tail_ref[:, at : at + width] = ref[half * depth : (half + 1) * depth, :]
-                at += width
+        tail_ref[:, columns:] = jnp.zeros((tail_ref.shape[0], 2 * heads), BF16)
+        tail_ref[:16, columns:] = decay.astype(BF16)
 
     spread = expander(heads, group, per_group, channels)
     weight = dot(weight_ref[...], spread)
@@ -141,13 +137,14 @@
     x_ref,
     write_ref,
     read_ref,
-    out_ref,
-    *,
+    *rest,
+    first,
     heads,
     per_group,
     channels,
 ):
-    group = pl.program_id(0)
+    out_ref = rest[-1]
+    group = first + pl.program_id(0)
     tokens = x_ref.shape[0]
     both = dot(read_ref[...], write_ref[...], 1, 1)
     square = (tokens, tokens)
@@ -185,18 +182,17 @@
     query_ref,
     key_ref,
     value_ref,
-    mine_ref,
-    other_ref,
+    prior_key_ref,
+    prior_value_ref,
     *rest,
-    halves,
     state_rows,
     prompt_rows,
     kv_count,
 ):
-    prior_refs, (out_ref, bias_ref) = rest[:-2], rest[-2:]
+    gathered, (out_ref, bias_ref) = rest[:-2], rest[-2:]
     head = pl.program_id(0)
     tokens = query_ref.shape[0]
-    devices = 2 * mine_ref.shape[0]
+    devices = len(gathered) * gathered[0].shape[0]
     scale = LOG2E / math.sqrt(HD)
 
     @pl.when(head == 0)
@@ -210,7 +206,7 @@
     def prompt(which):
         at = pl.multiple_of(state_rows + (which * kv_count + head) // 2 * 2 * prompt_rows, 16)
         at = pl.ds(at, 2 * prompt_rows)
-        pair = jnp.concatenate([mine_ref[:, at, :], other_ref[:, at, :]], axis=0).astype(F32)
+        pair = jnp.concatenate([ref[:, at, :] for ref in gathered], axis=0).astype(F32)
         odd = lax.rem(head, 2) == 1
         part = jnp.where(odd, pair[:, prompt_rows:, :], pair[:, :prompt_rows, :])
         return part.reshape(devices * prompt_rows, HD).astype(BF16)
@@ -221,8 +217,8 @@
     prompt_values = jnp.concatenate(
         [prompt_values, jnp.ones((prompt_values.shape[0], LANES), BF16)], axis=1
     )
-    near_keys = jnp.concatenate([ref[...] for ref in prior_refs[:halves]] + [key_ref[...]], axis=0)
-    near_values = [ref[...] for ref in prior_refs[halves:]] + [value_ref[...]]
+    near_keys = jnp.concatenate([prior_key_ref[...], key_ref[...]], axis=0)
+    near_values = [prior_value_ref[...], value_ref[...]]
     near_values = jnp.concatenate(
         [jnp.concatenate(near_values, axis=0), jnp.concatenate([ones, ones], axis=0)], axis=1
     )
@@ -248,21 +244,18 @@
     level_ref,
     tail_ref,
     decay_ref,
-    mine_ref,
-    other_ref,
     read_ref,
     inner_ref,
     gate_ref,
     gain_ref,
-    out_ref,
-    *,
+    *rest,
     state_rows,
     heads,
     per_group,
     channels,
 ):
+    gathered, out_ref = rest[:-1], rest[-1]
     group = pl.program_id(0)
-    tokens = read_ref.shape[0]
     level = jnp.exp(level_ref[...])
     carried = start_ref[:, : 2 * heads] < 0
     decay = decay_ref[...].astype(F32)
@@ -270,11 +263,16 @@
     spread = expander(heads, group, per_group, channels)
     from_prompt = dot(two_parts(jnp.where(carried, level * decay, level), heads), spread)
     from_prior = dot(two_parts(jnp.where(carried, level, 0.0), heads), spread)
-    odd = lax.rem(lax.axis_index("reader"), 2) == 1
+    own = lax.rem(lax.axis_index("reader"), NEAR)
     seeds = []
-    for pair in range(mine_ref.shape[0]):
-        mine, other = mine_ref[pair, :state_rows, :], other_ref[pair, :state_rows, :]
-        seeds += [jnp.where(odd, other, mine), jnp.where(odd, mine, other)]
+    for run in range(gathered[0].shape[0]):
+        parts = [ref[run, :state_rows, :] for ref in gathered]
+        bit = 1
+        while bit < NEAR:
+            swap = lax.rem(own // bit, 2) == 1
+            parts = [jnp.where(swap, parts[i ^ bit], parts[i]) for i in range(NEAR)]
+            bit *= 2
+        seeds += parts
     seeds = jnp.concatenate(seeds, axis=0)
     read = read_ref[...]
     mixed = inner_ref[...].astype(F32)
@@ -340,19 +338,24 @@
     sizes = dict(heads=heads, per_group=per_group, channels=channels)
     packed_rows = state_rows + 2 * prompt_rows * kv_count
 
-    packed = pl.pallas_call(
+    packed, near = pl.pallas_call(
         pack_kernel,
-        out_shape=jax.ShapeDtypeStruct((devices // 2, packed_rows, HD), BF16),
+        out_shape=(
+            jax.ShapeDtypeStruct((devices // NEAR, packed_rows, HD), BF16),
+            jax.ShapeDtypeStruct((tokens, 2 * kv_width), BF16),
+        ),
         compiler_params=params(),
         name="pack",
-    )(prompt_state, prompt_keys, prompt_values)
-    lanes_of = [list(range(first, devices, 2)) for first in range(2)]
+    )(prompt_state, prompt_keys, prompt_values, answer_keys, answer_values)
+    prior = shifted(near, "reader", 1)
     packed, raw = lax.optimization_barrier((packed, step_raw.T))
-    mine = lax.all_to_all(packed, "reader", 0, 0, axis_index_groups=lanes_of, tiled=True)
+    lines = [list(range(first, devices, NEAR)) for first in range(NEAR)]
+    line = lax.all_to_all(packed, "reader", 0, 0, axis_index_groups=lines, tiled=True)
+    exchanged = lambda value, bit: lax.ppermute(
+        value, "reader", [(i, i ^ bit) for i in range(devices)]
+    )
     raw = in_hbm(raw)
 
-    halves = tokens // state
-    tail_width = columns + 2 * heads + 2 * halves * kv_width
     by_group = lambda rows: pl.BlockSpec((rows, state), lambda g: (0, g))
     wide = pl.BlockSpec((tokens, width), lambda g: (0, g))
     tail, level, column, start = pl.pallas_call(
@@ -364,17 +367,15 @@
             whole((1, heads)),
             wide,
             by_group(tokens),
-            whole(answer_keys.shape),
-            whole(answer_values.shape),
         ],
         out_specs=(
-            whole((state, tail_width)),
+            whole((state, columns + 2 * heads)),
             whole((tokens, 2 * heads)),
             whole((heads, tokens)),
             whole((tokens, LANES)),
         ),
         out_shape=(
-            jax.ShapeDtypeStruct((state, tail_width), BF16),
+            jax.ShapeDtypeStruct((state, columns + 2 * heads), BF16),
             jax.ShapeDtypeStruct((tokens, 2 * heads), F32),
             jax.ShapeDtypeStruct((heads, tokens), F32),
             jax.ShapeDtypeStruct((tokens, LANES), F32),
@@ -382,43 +383,48 @@
         scratch_shapes=[pltpu.VMEM((tokens, 2 * heads), BF16)],
         compiler_params=params(),
         name="tail",
-    )(lengths, raw, rate, mixer_input, state_write, answer_keys, answer_values)
+    )(lengths, raw, rate, mixer_input, state_write)
     tail = shifted(tail, "reader", 1)
 
-    inner = pl.pallas_call(
-        functools.partial(inner_kernel, **sizes),
-        grid=(groups,),
-        in_specs=[
-            whole((tokens, LANES)),
-            whole((tokens, 2 * heads)),
-            pl.BlockSpec((per_group, tokens), lambda g: (g, 0)),
-            whole((1, heads)),
-            wide,
-            by_group(tokens),
-            by_group(tokens),
-        ],
-        out_specs=wide,
-        out_shape=jax.ShapeDtypeStruct((tokens, columns), BF16),
-        compiler_params=params(),
-        cost_estimate=pl.CostEstimate(
-            flops=heads * tokens * tokens * channels * 8,
-            bytes_accessed=tokens * columns * 4,
-            transcendentals=heads * tokens * tokens,
-        ),
-        name="inner",
-    )(start, level, column, skip, mixer_input, state_write, state_read)
-
-    mine, inner = lax.optimization_barrier((mine, inner))
-    other = lax.ppermute(mine, "reader", [(i, i ^ 1) for i in range(devices)])
-    prior_at = (columns + 2 * heads) // HD
-    prior_part = lambda part: pl.BlockSpec(
-        (state, HD), lambda k: (0, prior_at + part * kv_count + k)
-    )
+    prior, line, column = lax.optimization_barrier((prior, line, column))
+
+    def inner_part(first, count, *earlier):
+        blocks = lambda rows, columns: pl.BlockSpec((rows, columns), lambda g: (0, first + g))
+        return pl.pallas_call(
+            functools.partial(inner_kernel, first=first, **sizes),
+            grid=(count,),
+            in_specs=[
+                whole((tokens, LANES)),
+                whole((tokens, 2 * heads)),
+                pl.BlockSpec((per_group, tokens), lambda g: (first + g, 0)),
+                whole((1, heads)),
+                blocks(tokens, width),
+                blocks(tokens, state),
+                blocks(tokens, state),
+            ]
+            + [pl.BlockSpec(memory_space=pl.ANY)] * len(earlier),
+            out_specs=blocks(tokens, width),
+            out_shape=jax.ShapeDtypeStruct((tokens, columns), BF16),
+            input_output_aliases={7: 0} if earlier else {},
+            compiler_params=params(),
+            cost_estimate=pl.CostEstimate(
+                flops=count * per_group * tokens * tokens * channels * 8,
+                bytes_accessed=count * tokens * width * 4,
+                transcendentals=count * per_group * tokens * tokens,
+            ),
+            name="inner",
+        )(start, level, column, skip, mixer_input, state_write, state_read, *earlier)
+
+    half = groups // 2
+    inner = inner_part(0, half)
+    across = exchanged(line, 2)
+    across, inner = lax.optimization_barrier((across, inner))
+    gathered = (line, exchanged(line, 1), across, exchanged(across, 1))
+    inner = inner_part(half, groups - half, inner)
     group_size = queries.shape[1] // kv_width
     attention_out = pl.pallas_call(
         functools.partial(
             attend_kernel,
-            halves=halves,
             state_rows=state_rows,
             prompt_rows=prompt_rows,
             kv_count=kv_count,
@@ -429,16 +435,16 @@
             pl.BlockSpec((tokens, group_size * HD), lambda k: (0, k)),
             pl.BlockSpec((tokens, HD), lambda k: (0, k)),
             pl.BlockSpec((tokens, HD), lambda k: (0, k)),
-            whole((devices // 2, packed_rows, HD)),
-            whole((devices // 2, packed_rows, HD)),
+            pl.BlockSpec((tokens, HD), lambda k: (0, k)),
+            pl.BlockSpec((tokens, HD), lambda k: (0, kv_count + k)),
         ]
-        + [prior_part(part) for part in range(2 * halves)],
+        + [whole((devices // NEAR, packed_rows, HD))] * NEAR,
         out_specs=pl.BlockSpec((tokens, group_size * HD), lambda k: (0, k)),
         out_shape=jax.ShapeDtypeStruct(queries.shape, BF16),
         scratch_shapes=[pltpu.VMEM((tokens, 2 * tokens), F32)],
         compiler_params=params(),
         name="attend",
-    )(start, queries, answer_keys, answer_values, mine, other, *[tail] * (2 * halves))
+    )(start, queries, answer_keys, answer_values, prior, prior, *gathered)
 
     mixer_out = pl.pallas_call(
         functools.partial(final_kernel, state_rows=state_rows, **sizes),
@@ -448,18 +454,17 @@
             whole((tokens, 2 * heads)),
             pl.BlockSpec((state, width), lambda g: (0, g)),
             pl.BlockSpec((16, 2 * heads), lambda g: (0, columns // (2 * heads))),
-            pl.BlockSpec((devices // groups // 2, packed_rows, HD), lambda g: (g, 0, 0)),
-            pl.BlockSpec((devices // groups // 2, packed_rows, HD), lambda g: (g, 0, 0)),
             by_group(tokens),
             wide,
             wide,
             pl.BlockSpec((1, width), lambda g: (0, g)),
-        ],
+        ]
+        + [pl.BlockSpec((devices // groups // NEAR, packed_rows, HD), lambda g: (g, 0, 0))] * NEAR,
         out_specs=wide,
         out_shape=jax.ShapeDtypeStruct((tokens, columns), BF16),
         compiler_params=params(),
         name="final",
-    )(start, level, tail, tail, mine, other, state_read, inner, gate_input, gain)
+    )(start, level, tail, tail, state_read, inner, gate_input, gain, *gathered)
     return (mixer_out, attention_out)
 
 

time: 56.6 us -> 58.7 us (1.037)
  starting transfers between devices: 9.65 us -> 13.2 us
  local copies, waits for them, and re-layouts: 1.32 us -> 0 us
  waiting for transfers between devices: 17.2 us -> 16.4 us
    ppermute x1 -> x2, waiting for transfers between devices: 17.2 us -> 0.01 us  [shifted(): return lax.ppermute(value, axis, [(i, i + by) for i in range(length - by)])]
    ppermute x1 -> x3, waiting for transfers between devices: 0.01 us -> 15.7 us  [local(): lax.ppermute(value, 'reader', [(i, i ^ bit) for i in range(devices)])]
    ppermute x1 -> x2, starting transfers between devices: 1.91 us -> 4.86 us  [shifted(): return lax.ppermute(value, axis, [(i, i + by) for i in range(length - by)])]
    ppermute x1 -> x3, starting transfers between devices: 1.57 us -> 3.13 us  [local(): lax.ppermute(value, 'reader', [(i, i ^ bit) for i in range(devices)])]
    pallas_call x3 -> x4, Pallas kernels: 14.8 us -> 16.1 us  [the longest x1 7.5 us: local(): pl.pallas_call(functools.partial(attend_kernel, state_rows=state_rows, pr...]
    unnamed x4 -> x0, local copies, waits for them, and re-layouts: 1.32 us -> none
    pallas_call x1, Pallas kernels: 5.63 us -> 4.33 us  [local(): pl.pallas_call(functools.partial(tail_kernel, **sizes), grid=(groups,), i...]
    all_to_all x1, starting transfers between devices: 6.17 us -> 5.22 us  [local(): lax.all_to_all(packed, 'reader', 0, 0, axis_index_groups=lines, tiled=True)]
  transfers between devices with their start and end apart: 3 -> 6, of which waited for: 1 -> 2; matrix products, arithmetic and copies ran while one was open for 0% -> 0% of each run, Pallas kernels for 20% -> 32%
where the time goes in v3:
time: 58.7 us; the launch traced here: 57.8 us
  Pallas kernels  27.4 us (47%)
  waiting for transfers between devices  16.4 us (28%)
  starting transfers between devices  13.2 us (22%)
  between operations  0.69 us (1%)
    ppermute x3, waiting for transfers between devices, local(): lax.ppermute(value, 'reader', [(i, i ^ bit) for i in range(devices)])  15.7 us
    pallas_call x1, Pallas kernels, local(): pl.pallas_call(functools.partial(attend_kernel, state_rows=state_rows, pr...  7.5 us
    pallas_call x1, Pallas kernels, local(): pl.pallas_call(functools.partial(final_kernel, state_rows=state_rows, **s...  7 us
    pallas_call x2, Pallas kernels, inner_part(): pl.pallas_call(functools.partial(inner_kernel, first=first, **sizes), gri...  6.55 us
    all_to_all x1, starting transfers between devices, local(): lax.all_to_all(packed, 'reader', 0, 0, axis_index_groups=lines, tiled=True)  5.22 us
    ppermute x2, starting transfers between devices, shifted(): return lax.ppermute(value, axis, [(i, i + by) for i in range(length - by)])  4.86 us
    pallas_call x1, Pallas kernels, local(): pl.pallas_call(functools.partial(tail_kernel, **sizes), grid=(groups,), i...  4.33 us
    ppermute x3, starting transfers between devices, local(): lax.ppermute(value, 'reader', [(i, i ^ bit) for i in range(devices)])  3.13 us
  transfers between devices with their start and end apart: 6, of which 2 were waited for; matrix products, arithmetic and copies ran while one was open for 0% of the time, Pallas kernels for 32%

profile of v3, /device:TPU:18, one launch (start us, length us, event | category | flops | bytes accessed | tf_op | source)
XLA Modules:
  0.0 57.8 jit_solution(4633928860025109551)
XLA Ops:
  0.6 2.1 %pack.1 = (bf16[4,320,128]{2,1,0:T(8,128)(2,1)}, bf16[256,1024]{1,0:T(8,128)(2,1)}) custom-call(f32[256,128]{1,0:T(8,128)} %state_ref.1, bf16[8,512]{1,0:T(8,128)(2,1)} %keys_ref.1, bf16[8,512]{1,0:T(8,128)(2,1)} %values_ref.1, bf16[256,512]{1,0:T(8,128)(2,1)} %key_ref.1, bf16[256,512]{1,0:T(8,128)(2,1)} %value_ref.1), custom_call_target="tpu_custom_call" | custom-call | tf_op jit(solution)/shard_map/pack/pallas_call | solution.py:341
  2.7 1.9 %collective-permute-start.1 = (bf16[256,1024]{1,0:T(8,128)(2,1)}, bf16[256,1024]{1,0:T(8,128)(2,1)S(1)}, u32[]{:S(2)}, u32[]{:S(2)}) collective-permute-start(bf16[256,1024]{1,0:T(8,128)(2,1)} %get-tuple-element.20), channel_id=1, source_target_pairs={{0,1},{1,2},{2,3},{3,4},{4,5},{5,6},{6,7},{7,8},{8,9},{9,10},{10,1... | collective-permute-start | bytes 1572872 | tf_op jit(solution)/shard_map/ppermute | solution.py:289
  4.6 5.2 %all-to-all-start = ((bf16[4,320,128]{2,1,0:T(8,128)(2,1)}), bf16[4,320,128]{2,1,0:T(8,128)(2,1)S(1)}, u32[]{:S(2)}, u32[]{:S(2)}) async-start(bf16[4,320,128]{2,1,0:T(8,128)(2,1)} %get-tuple-element.21), calls=%async_computation | async-start | bytes 655360 | tf_op jit(solution)/shard_map/all_to_all | solution.py:353
  9.8 4.3 %tail.1 = (bf16[128,4224]{1,0:T(8,128)(2,1)S(1)}, f32[256,128]{1,0:T(8,128)S(1)}, f32[64,256]{1,0:T(8,128)S(1)}, f32[256,128]{1,0:T(8,128)S(1)}) custom-call(s32[1,32]{1,0:T(1,128)} %bitcast.9, f32[64,256]{1,0:T(8,128)} %bitcast.5, f32[1,64]{1,0:T(1,128)} %bitcast.10, bf16[256,4096]{1,0:T(8,128)(2,1)} %x_ref.5, bf16[256,512]{1,0:T(8,128)(2,1)} %write_ref.5), custom_call_target="tpu_custom_call" | custom-call | tf_op jit(solution)/shard_map/tail/pallas_call | solution.py:361
  14.2 3.0 %collective-permute-start = (bf16[128,4224]{1,0:T(8,128)(2,1)S(1)}, bf16[128,4224]{1,0:T(8,128)(2,1)S(1)}, u32[]{:S(2)}, u32[]{:S(2)}) collective-permute-start(bf16[128,4224]{1,0:T(8,128)(2,1)S(1)} %get-tuple-element.19), channel_id=1, source_target_pairs={{0,1},{1,2},{2,3},{3,4},{4,5},{5,6},{6,7},{7,8},{8,9},{9,10},{10,1... | collective-permute-start | bytes 3244040 | tf_op jit(solution)/shard_map/ppermute | solution.py:289
  17.1 0.7 %all-to-all-done.rest_0_ = bf16[4,320,128]{2,1,0:T(8,128)(2,1)S(1)} async-done(((bf16[4,320,128]{2,1,0:T(8,128)(2,1)}), bf16[4,320,128]{2,1,0:T(8,128)(2,1)S(1)}, u32[]{:S(2)}, u32[]{:S(2)}) %all-to-all-start) | async-done | bytes 327712 | tf_op jit(solution)/shard_map/all_to_all | solution.py:353
  17.8 0.0 collective-permute-done.1.prior_key_ref.prior_value_ref
  17.8 1.3 %collective-permute-start.2 = (bf16[4,320,128]{2,1,0:T(8,128)(2,1)S(1)}, bf16[4,320,128]{2,1,0:T(8,128)(2,1)S(1)}, u32[]{:S(2)}, u32[]{:S(2)}) collective-permute-start(bf16[4,320,128]{2,1,0:T(8,128)(2,1)S(1)} %all-to-all-done.rest_0_), channel_id=1, source_target_pairs={{0,2},{1,3},{2,0},{3,1},{4,6},{5,7},{6,4},{7,5},{8,10},{9,11},{10,... | collective-permute-start | bytes 983048 | tf_op jit(solution)/shard_map/ppermute | solution.py:354
  19.1 1.7 %collective-permute-start.3 = (bf16[4,320,128]{2,1,0:T(8,128)(2,1)S(1)}, bf16[4,320,128]{2,1,0:T(8,128)(2,1)S(1)}, u32[]{:S(2)}, u32[]{:S(2)}) collective-permute-start(bf16[4,320,128]{2,1,0:T(8,128)(2,1)S(1)} %all-to-all-done.rest_0_), channel_id=1, source_target_pairs={{0,1},{1,0},{2,3},{3,2},{4,5},{5,4},{6,7},{7,6},{8,9},{9,8},{10,11... | collective-permute-start | bytes 983048 | tf_op jit(solution)/shard_map/ppermute | solution.py:354
  20.8 3.3 %inner.2.rest_0_ = bf16[256,4096]{1,0:T(8,128)(2,1)S(1)} custom-call(f32[256,128]{1,0:T(8,128)S(1)} %get-tuple-element.17.start_ref, f32[256,128]{1,0:T(8,128)S(1)} %get-tuple-element.18.level_ref, f32[64,256]{1,0:T(8,128)S(1)} %get-tuple-element.23.column_ref, f32[1,64]{1,0:T(1,128)} %bitcast.7, bf16[256,4096]{1,0:T(8,128)(2,1)} %x_ref.5, ...), custom_call_target="tpu_custom_call" | custom-call | flops 1073741824 | bytes 2097152 | tf_op jit(solution)/shard_map/inner/pallas_call | solution.py:393
  24.1 15.7 %collective-permute-done.2.rest_2_ = bf16[4,320,128]{2,1,0:T(8,128)(2,1)S(1)} collective-permute-done((bf16[4,320,128]{2,1,0:T(8,128)(2,1)S(1)}, bf16[4,320,128]{2,1,0:T(8,128)(2,1)S(1)}, u32[]{:S(2)}, u32[]{:S(2)}) %collective-permute-start.2) | collective-permute-done | bytes 327712 | tf_op jit(solution)/shard_map/ppermute | solution.py:354
  39.9 0.1 collective-permute-start.4
  40.0 3.3 %inner.3.inner_ref = bf16[256,4096]{1,0:T(8,128)(2,1)S(1)} custom-call(f32[256,128]{1,0:T(8,128)S(1)} %get-tuple-element.17.start_ref, f32[256,128]{1,0:T(8,128)S(1)} %get-tuple-element.18.level_ref, f32[64,256]{1,0:T(8,128)S(1)} %get-tuple-element.23.column_ref, f32[1,64]{1,0:T(1,128)} %bitcast.8, ...), custom_call_target="tpu_custom_call", output_to_operand_aliasing={{}: (7, {})} | custom-call | flops 1073741824 | bytes 2097152 | tf_op jit(solution)/shard_map/inner/pallas_call | solution.py:393
  43.3 0.0 collective-permute-done.3.rest_1_
  43.3 0.0 collective-permute-done.4.rest_3_
  43.3 7.5 %attend.1 = bf16[256,2048]{1,0:T(8,128)(2,1)} custom-call(f32[256,128]{1,0:T(8,128)S(1)} %get-tuple-element.17.start_ref, bf16[256,2048]{1,0:T(8,128)(2,1)} %query_ref.1, bf16[256,512]{1,0:T(8,128)(2,1)} %key_ref.1, bf16[256,512]{1,0:T(8,128)(2,1)} %value_ref.1, bf16[256,1024]{1,0:T(8,128)(2,1)S(1)} %collective-permute-done.1.prior_key_ref.prior_value_ref, ...), custom_call_target="tpu_custom_call" | custom-call | tf_op jit(solution)/shard_map/attend/pallas_call | solution.py:425
  50.8 0.0 collective-permute-done.tail_ref.decay_ref
  50.8 7.0 %final.1 = bf16[256,4096]{1,0:T(8,128)(2,1)} custom-call(f32[256,128]{1,0:T(8,128)S(1)} %get-tuple-element.17.start_ref, f32[256,128]{1,0:T(8,128)S(1)} %get-tuple-element.18.level_ref, bf16[128,4224]{1,0:T(8,128)(2,1)S(1)} %collective-permute-done.tail_ref.decay_ref, bf16[128,4224]{1,0:T(8,128)(2,1)S(1)} %collective-permute-done.tail_ref.decay_ref, ...), custom_call_target="tpu_custom_call" | custom-call | tf_op jit(solution)/shard_map/final/pallas_call | solution.py:449
Async XLA Ops:
  2.7 15.1 %collective-permute-start.1 = (bf16[256,1024]{1,0:T(8,128)(2,1)}, bf16[256,1024]{1,0:T(8,128)(2,1)S(1)}, u32[]{:S(2)}, u32[]{:S(2)}) collective-permute-start(bf16[256,1024]{1,0:T(8,128)(2,1)} %get-tuple-element.20), channel_id=1, source_target_pairs={{0,1},{1,2},{2,3},{3,4},{4,5},{5,6},{6,7},{7,8},{8,9},{9,10},{10,1... | collective-permute-start | bytes 1572872 | tf_op jit(solution)/shard_map/ppermute | solution.py:289
  4.6 13.2 %all-to-all-start = ((bf16[4,320,128]{2,1,0:T(8,128)(2,1)}), bf16[4,320,128]{2,1,0:T(8,128)(2,1)S(1)}, u32[]{:S(2)}, u32[]{:S(2)}) async-start(bf16[4,320,128]{2,1,0:T(8,128)(2,1)} %get-tuple-element.21), calls=%async_computation | async-start | bytes 655360 | tf_op jit(solution)/shard_map/all_to_all | solution.py:353
  14.2 36.6 %collective-permute-start = (bf16[128,4224]{1,0:T(8,128)(2,1)S(1)}, bf16[128,4224]{1,0:T(8,128)(2,1)S(1)}, u32[]{:S(2)}, u32[]{:S(2)}) collective-permute-start(bf16[128,4224]{1,0:T(8,128)(2,1)S(1)} %get-tuple-element.19), channel_id=1, source_target_pairs={{0,1},{1,2},{2,3},{3,4},{4,5},{5,6},{6,7},{7,8},{8,9},{9,10},{10,1... | collective-permute-start | bytes 3244040 | tf_op jit(solution)/shard_map/ppermute | solution.py:289
  17.8 22.0 %collective-permute-start.2 = (bf16[4,320,128]{2,1,0:T(8,128)(2,1)S(1)}, bf16[4,320,128]{2,1,0:T(8,128)(2,1)S(1)}, u32[]{:S(2)}, u32[]{:S(2)}) collective-permute-start(bf16[4,320,128]{2,1,0:T(8,128)(2,1)S(1)} %all-to-all-done.rest_0_), channel_id=1, source_target_pairs={{0,2},{1,3},{2,0},{3,1},{4,6},{5,7},{6,4},{7,5},{8,10},{9,11},{10,... | collective-permute-start | bytes 983048 | tf_op jit(solution)/shard_map/ppermute | solution.py:354
  19.1 24.1 %collective-permute-start.3 = (bf16[4,320,128]{2,1,0:T(8,128)(2,1)S(1)}, bf16[4,320,128]{2,1,0:T(8,128)(2,1)S(1)}, u32[]{:S(2)}, u32[]{:S(2)}) collective-permute-start(bf16[4,320,128]{2,1,0:T(8,128)(2,1)S(1)} %all-to-all-done.rest_0_), channel_id=1, source_target_pairs={{0,1},{1,0},{2,3},{3,2},{4,5},{5,4},{6,7},{7,6},{8,9},{9,8},{10,11... | collective-permute-start | bytes 983048 | tf_op jit(solution)/shard_map/ppermute | solution.py:354
  39.9 3.4 %collective-permute-start.4 = (bf16[4,320,128]{2,1,0:T(8,128)(2,1)S(1)}, bf16[4,320,128]{2,1,0:T(8,128)(2,1)S(1)}, u32[]{:S(2)}, u32[]{:S(2)}) collective-permute-start(bf16[4,320,128]{2,1,0:T(8,128)(2,1)S(1)} %collective-permute-done.2.rest_2_), channel_id=1, source_target_pairs={{0,1},{1,0},{2,3},{3,2},{4,5},{5,4},{6,7},{7,6},{8,9},{9,8},{10,11... | collective-permute-start | bytes 983048 | tf_op jit(solution)/shard_map/ppermute | solution.py:354

commit v4 on v3

--- a/solution.py
+++ b/solution.py
@@ -347,10 +347,10 @@
         compiler_params=params(),
         name="pack",
     )(prompt_state, prompt_keys, prompt_values, answer_keys, answer_values)
-    prior = shifted(near, "reader", 1)
     packed, raw = lax.optimization_barrier((packed, step_raw.T))
     lines = [list(range(first, devices, NEAR)) for first in range(NEAR)]
     line = lax.all_to_all(packed, "reader", 0, 0, axis_index_groups=lines, tiled=True)
+    prior = shifted(near, "reader", 1)
     exchanged = lambda value, bit: lax.ppermute(
         value, "reader", [(i, i ^ bit) for i in range(devices)]
     )
@@ -384,7 +384,6 @@
         compiler_params=params(),
         name="tail",
     )(lengths, raw, rate, mixer_input, state_write)
-    tail = shifted(tail, "reader", 1)
 
     prior, line, column = lax.optimization_barrier((prior, line, column))
 
@@ -418,6 +417,8 @@
     half = groups // 2
     inner = inner_part(0, half)
     across = exchanged(line, 2)
+    tail, inner = lax.optimization_barrier((tail, inner))
+    tail = shifted(tail, "reader", 1)
     across, inner = lax.optimization_barrier((across, inner))
     gathered = (line, exchanged(line, 1), across, exchanged(across, 1))
     inner = inner_part(half, groups - half, inner)

time: 58.7 us -> 65.9 us (1.12)
  the two profiles are of different devices: /device:TPU:18 before, /device:TPU:0 now
where the time goes in v4:
time: 65.9 us; the launch traced here: 65.6 us
  Pallas kernels  27.3 us (41%)
  starting transfers between devices  21.2 us (32%)
  waiting for transfers between devices  16.4 us (25%)
  between operations  0.69 us (1%)
    ppermute x3, starting transfers between devices, local(): lax.ppermute(value, 'reader', [(i, i ^ bit) for i in range(devices)])  10.9 us
    ppermute x3, waiting for transfers between devices, local(): lax.ppermute(value, 'reader', [(i, i ^ bit) for i in range(devices)])  9.28 us
    pallas_call x1, Pallas kernels, local(): pl.pallas_call(functools.partial(attend_kernel, state_rows=state_rows, pr...  7.5 us
    all_to_all x1, waiting for transfers between devices, local(): lax.all_to_all(packed, 'reader', 0, 0, axis_index_groups=lines, tiled=True)  7.07 us
    pallas_call x1, Pallas kernels, local(): pl.pallas_call(functools.partial(final_kernel, state_rows=state_rows, **s...  7 us
    pallas_call x2, Pallas kernels, inner_part(): pl.pallas_call(functools.partial(inner_kernel, first=first, **sizes), gri...  6.56 us
    all_to_all x1, starting transfers between devices, local(): lax.all_to_all(packed, 'reader', 0, 0, axis_index_groups=lines, tiled=True)  5.86 us
    ppermute x2, starting transfers between devices, shifted(): return lax.ppermute(value, axis, [(i, i + by) for i in range(length - by)])  4.46 us
  transfers between devices with their start and end apart: 6, of which 2 were waited for; matrix products, arithmetic and copies ran while one was open for 0% of the time, Pallas kernels for 23%

profile of v4, /device:TPU:0, one launch (start us, length us, event | category | flops | bytes accessed | tf_op | source)
XLA Modules:
  0.0 65.6 jit_solution(12582811851548997798)
XLA Ops:
  0.6 1.9 %pack.1 = (bf16[4,320,128]{2,1,0:T(8,128)(2,1)}, bf16[256,1024]{1,0:T(8,128)(2,1)S(1)}) custom-call(f32[256,128]{1,0:T(8,128)} %state_ref.1, bf16[8,512]{1,0:T(8,128)(2,1)} %keys_ref.1, bf16[8,512]{1,0:T(8,128)(2,1)} %values_ref.1, bf16[256,512]{1,0:T(8,128)(2,1)} %key_ref.1, bf16[256,512]{1,0:T(8,128)(2,1)} %value_ref.1), custom_call_target="tpu_custom_call" | custom-call | tf_op jit(solution)/shard_map/pack/pallas_call | solution.py:341
  2.5 2.4 %collective-permute-start = (bf16[256,1024]{1,0:T(8,128)(2,1)S(1)}, bf16[256,1024]{1,0:T(8,128)(2,1)S(1)}, u32[]{:S(2)}, u32[]{:S(2)}) collective-permute-start(bf16[256,1024]{1,0:T(8,128)(2,1)S(1)} %get-tuple-element.22), channel_id=1, source_target_pairs={{0,1},{1,2},{2,3},{3,4},{4,5},{5,6},{6,7},{7,8},{8,9},{9,10},{10,1... | collective-permute-start | bytes 1572872 | tf_op jit(solution)/shard_map/ppermute | solution.py:289
  4.9 5.9 %all-to-all-start = ((bf16[4,320,128]{2,1,0:T(8,128)(2,1)}), bf16[4,320,128]{2,1,0:T(8,128)(2,1)S(1)}, u32[]{:S(2)}, u32[]{:S(2)}) async-start(bf16[4,320,128]{2,1,0:T(8,128)(2,1)} %get-tuple-element.23), calls=%async_computation | async-start | bytes 655360 | tf_op jit(solution)/shard_map/all_to_all | solution.py:352
  10.8 4.3 %tail.1 = (bf16[128,4224]{1,0:T(8,128)(2,1)S(1)}, f32[256,128]{1,0:T(8,128)S(1)}, f32[64,256]{1,0:T(8,128)S(1)}, f32[256,128]{1,0:T(8,128)S(1)}) custom-call(s32[1,32]{1,0:T(1,128)} %bitcast.9, f32[64,256]{1,0:T(8,128)} %bitcast.5, f32[1,64]{1,0:T(1,128)} %bitcast.10, bf16[256,4096]{1,0:T(8,128)(2,1)} %x_ref.5, bf16[256,512]{1,0:T(8,128)(2,1)} %write_ref.5), custom_call_target="tpu_custom_call" | custom-call | tf_op jit(solution)/shard_map/tail/pallas_call | solution.py:361
  15.1 7.1 %all-to-all-done.rest_0_ = bf16[4,320,128]{2,1,0:T(8,128)(2,1)S(1)} async-done(((bf16[4,320,128]{2,1,0:T(8,128)(2,1)}), bf16[4,320,128]{2,1,0:T(8,128)(2,1)S(1)}, u32[]{:S(2)}, u32[]{:S(2)}) %all-to-all-start) | async-done | bytes 327712 | tf_op jit(solution)/shard_map/all_to_all | solution.py:352
  22.2 0.0 collective-permute-done.prior_key_ref.prior_value_ref
  22.2 3.3 %inner.2.rest_0_ = bf16[256,4096]{1,0:T(8,128)(2,1)S(1)} custom-call(f32[256,128]{1,0:T(8,128)S(1)} %get-tuple-element.19.start_ref, f32[256,128]{1,0:T(8,128)S(1)} %get-tuple-element.20.level_ref, f32[64,256]{1,0:T(8,128)S(1)} %get-tuple-element.25.column_ref, f32[1,64]{1,0:T(1,128)} %bitcast.7, bf16[256,4096]{1,0:T(8,128)(2,1)} %x_ref.5, ...), custom_call_target="tpu_custom_call" | custom-call | flops 1073741824 | bytes 2097152 | tf_op jit(solution)/shard_map/inner/pallas_call | solution.py:392
  25.5 2.1 %collective-permute-start.1 = (bf16[128,4224]{1,0:T(8,128)(2,1)S(1)}, bf16[128,4224]{1,0:T(8,128)(2,1)S(1)}, u32[]{:S(2)}, u32[]{:S(2)}) collective-permute-start(bf16[128,4224]{1,0:T(8,128)(2,1)S(1)} %get-tuple-element.26), channel_id=1, source_target_pairs={{0,1},{1,2},{2,3},{3,4},{4,5},{5,6},{6,7},{7,8},{8,9},{9,10},{10,1... | collective-permute-start | bytes 3244040 | tf_op jit(solution)/shard_map/ppermute | solution.py:289
  27.5 1.1 %collective-permute-start.2 = (bf16[4,320,128]{2,1,0:T(8,128)(2,1)S(1)}, bf16[4,320,128]{2,1,0:T(8,128)(2,1)S(1)}, u32[]{:S(2)}, u32[]{:S(2)}) collective-permute-start(bf16[4,320,128]{2,1,0:T(8,128)(2,1)S(1)} %all-to-all-done.rest_0_), channel_id=1, source_target_pairs={{0,2},{1,3},{2,0},{3,1},{4,6},{5,7},{6,4},{7,5},{8,10},{9,11},{10,... | collective-permute-start | bytes 983048 | tf_op jit(solution)/shard_map/ppermute | solution.py:354
  28.6 0.2 collective-permute-start.3
  28.8 9.3 %collective-permute-done.2.rest_2_ = bf16[4,320,128]{2,1,0:T(8,128)(2,1)S(1)} collective-permute-done((bf16[4,320,128]{2,1,0:T(8,128)(2,1)S(1)}, bf16[4,320,128]{2,1,0:T(8,128)(2,1)S(1)}, u32[]{:S(2)}, u32[]{:S(2)}) %collective-permute-start.2) | collective-permute-done | bytes 327712 | tf_op jit(solution)/shard_map/ppermute | solution.py:354
  38.1 9.7 %collective-permute-start.4 = (bf16[4,320,128]{2,1,0:T(8,128)(2,1)S(1)}, bf16[4,320,128]{2,1,0:T(8,128)(2,1)S(1)}, u32[]{:S(2)}, u32[]{:S(2)}) collective-permute-start(bf16[4,320,128]{2,1,0:T(8,128)(2,1)S(1)} %collective-permute-done.2.rest_2_), channel_id=1, source_target_pairs={{0,1},{1,0},{2,3},{3,2},{4,5},{5,4},{6,7},{7,6},{8,9},{9,8},{10,11... | collective-permute-start | bytes 983048 | tf_op jit(solution)/shard_map/ppermute | solution.py:354
  47.7 3.3 %inner.3.inner_ref = bf16[256,4096]{1,0:T(8,128)(2,1)S(1)} custom-call(f32[256,128]{1,0:T(8,128)S(1)} %get-tuple-element.19.start_ref, f32[256,128]{1,0:T(8,128)S(1)} %get-tuple-element.20.level_ref, f32[64,256]{1,0:T(8,128)S(1)} %get-tuple-element.25.column_ref, f32[1,64]{1,0:T(1,128)} %bitcast.8, ...), custom_call_target="tpu_custom_call", output_to_operand_aliasing={{}: (7, {})} | custom-call | flops 1073741824 | bytes 2097152 | tf_op jit(solution)/shard_map/inner/pallas_call | solution.py:392
  51.0 0.0 collective-permute-done.3.rest_1_
  51.0 0.0 collective-permute-done.4.rest_3_
  51.1 7.5 %attend.1 = bf16[256,2048]{1,0:T(8,128)(2,1)} custom-call(f32[256,128]{1,0:T(8,128)S(1)} %get-tuple-element.19.start_ref, bf16[256,2048]{1,0:T(8,128)(2,1)} %query_ref.1, bf16[256,512]{1,0:T(8,128)(2,1)} %key_ref.1, bf16[256,512]{1,0:T(8,128)(2,1)} %value_ref.1, bf16[256,1024]{1,0:T(8,128)(2,1)S(1)} %collective-permute-done.prior_key_ref.prior_value_ref, ...), custom_call_target="tpu_custom_call" | custom-call | tf_op jit(solution)/shard_map/attend/pallas_call | solution.py:426
  58.6 0.0 collective-permute-done.1.tail_ref.decay_ref
  58.6 7.0 %final.1 = bf16[256,4096]{1,0:T(8,128)(2,1)} custom-call(f32[256,128]{1,0:T(8,128)S(1)} %get-tuple-element.19.start_ref, f32[256,128]{1,0:T(8,128)S(1)} %get-tuple-element.20.level_ref, bf16[128,4224]{1,0:T(8,128)(2,1)S(1)} %collective-permute-done.1.tail_ref.decay_ref, bf16[128,4224]{1,0:T(8,128)(2,1)S(1)} %collective-permute-done.1.tail_ref.decay_ref, ...), custom_call_target="tpu_custom_call" | custom-call | tf_op jit(solution)/shard_map/final/pallas_call | solution.py:450
Async XLA Ops:
  2.5 19.7 %collective-permute-start = (bf16[256,1024]{1,0:T(8,128)(2,1)S(1)}, bf16[256,1024]{1,0:T(8,128)(2,1)S(1)}, u32[]{:S(2)}, u32[]{:S(2)}) collective-permute-start(bf16[256,1024]{1,0:T(8,128)(2,1)S(1)} %get-tuple-element.22), channel_id=1, source_target_pairs={{0,1},{1,2},{2,3},{3,4},{4,5},{5,6},{6,7},{7,8},{8,9},{9,10},{10,1... | collective-permute-start | bytes 1572872 | tf_op jit(solution)/shard_map/ppermute | solution.py:289
  4.9 17.3 %all-to-all-start = ((bf16[4,320,128]{2,1,0:T(8,128)(2,1)}), bf16[4,320,128]{2,1,0:T(8,128)(2,1)S(1)}, u32[]{:S(2)}, u32[]{:S(2)}) async-start(bf16[4,320,128]{2,1,0:T(8,128)(2,1)} %get-tuple-element.23), calls=%async_computation | async-start | bytes 655360 | tf_op jit(solution)/shard_map/all_to_all | solution.py:352
  25.5 33.1 %collective-permute-start.1 = (bf16[128,4224]{1,0:T(8,128)(2,1)S(1)}, bf16[128,4224]{1,0:T(8,128)(2,1)S(1)}, u32[]{:S(2)}, u32[]{:S(2)}) collective-permute-start(bf16[128,4224]{1,0:T(8,128)(2,1)S(1)} %get-tuple-element.26), channel_id=1, source_target_pairs={{0,1},{1,2},{2,3},{3,4},{4,5},{5,6},{6,7},{7,8},{8,9},{9,10},{10,1... | collective-permute-start | bytes 3244040 | tf_op jit(solution)/shard_map/ppermute | solution.py:289
  27.5 10.5 %collective-permute-start.2 = (bf16[4,320,128]{2,1,0:T(8,128)(2,1)S(1)}, bf16[4,320,128]{2,1,0:T(8,128)(2,1)S(1)}, u32[]{:S(2)}, u32[]{:S(2)}) collective-permute-start(bf16[4,320,128]{2,1,0:T(8,128)(2,1)S(1)} %all-to-all-done.rest_0_), channel_id=1, source_target_pairs={{0,2},{1,3},{2,0},{3,1},{4,6},{5,7},{6,4},{7,5},{8,10},{9,11},{10,... | collective-permute-start | bytes 983048 | tf_op jit(solution)/shard_map/ppermute | solution.py:354
  28.6 22.4 %collective-permute-start.3 = (bf16[4,320,128]{2,1,0:T(8,128)(2,1)S(1)}, bf16[4,320,128]{2,1,0:T(8,128)(2,1)S(1)}, u32[]{:S(2)}, u32[]{:S(2)}) collective-permute-start(bf16[4,320,128]{2,1,0:T(8,128)(2,1)S(1)} %all-to-all-done.rest_0_), channel_id=1, source_target_pairs={{0,1},{1,0},{2,3},{3,2},{4,5},{5,4},{6,7},{7,6},{8,9},{9,8},{10,11... | collective-permute-start | bytes 983048 | tf_op jit(solution)/shard_map/ppermute | solution.py:354
  38.1 13.0 %collective-permute-start.4 = (bf16[4,320,128]{2,1,0:T(8,128)(2,1)S(1)}, bf16[4,320,128]{2,1,0:T(8,128)(2,1)S(1)}, u32[]{:S(2)}, u32[]{:S(2)}) collective-permute-start(bf16[4,320,128]{2,1,0:T(8,128)(2,1)S(1)} %collective-permute-done.2.rest_2_), channel_id=1, source_target_pairs={{0,1},{1,0},{2,3},{3,2},{4,5},{5,4},{6,7},{7,6},{8,9},{9,8},{10,11... | collective-permute-start | bytes 983048 | tf_op jit(solution)/shard_map/ppermute | solution.py:354

commit v5 on v3

--- a/solution.py
+++ b/solution.py
@@ -10,7 +10,7 @@
 
 HD = 128
 LANES = 128
-NEAR = 4
+NEAR = 2
 LOG2E = 1.4426950408889634
 F32 = jnp.float32
 BF16 = jnp.bfloat16
@@ -347,13 +347,10 @@
         compiler_params=params(),
         name="pack",
     )(prompt_state, prompt_keys, prompt_values, answer_keys, answer_values)
-    prior = shifted(near, "reader", 1)
     packed, raw = lax.optimization_barrier((packed, step_raw.T))
     lines = [list(range(first, devices, NEAR)) for first in range(NEAR)]
     line = lax.all_to_all(packed, "reader", 0, 0, axis_index_groups=lines, tiled=True)
-    exchanged = lambda value, bit: lax.ppermute(
-        value, "reader", [(i, i ^ bit) for i in range(devices)]
-    )
+    prior = shifted(near, "reader", 1)
     raw = in_hbm(raw)
 
     by_group = lambda rows: pl.BlockSpec((rows, state), lambda g: (0, g))
@@ -384,9 +381,9 @@
         compiler_params=params(),
         name="tail",
     )(lengths, raw, rate, mixer_input, state_write)
+
     tail = shifted(tail, "reader", 1)
-
-    prior, line, column = lax.optimization_barrier((prior, line, column))
+    prior, column = lax.optimization_barrier((prior, column))
 
     def inner_part(first, count, *earlier):
         blocks = lambda rows, columns: pl.BlockSpec((rows, columns), lambda g: (0, first + g))
@@ -415,12 +412,11 @@
             name="inner",
         )(start, level, column, skip, mixer_input, state_write, state_read, *earlier)
 
-    half = groups // 2
-    inner = inner_part(0, half)
-    across = exchanged(line, 2)
-    across, inner = lax.optimization_barrier((across, inner))
-    gathered = (line, exchanged(line, 1), across, exchanged(across, 1))
-    inner = inner_part(half, groups - half, inner)
+    inner = inner_part(0, groups - 1)
+    line, inner = lax.optimization_barrier((line, inner))
+    exchanged = lax.ppermute(line, "reader", [(i, i ^ 1) for i in range(devices)])
+    gathered = (line, exchanged)
+    inner = inner_part(groups - 1, 1, inner)
     group_size = queries.shape[1] // kv_width
     attention_out = pl.pallas_call(
         functools.partial(

time: 58.7 us -> 54.1 us (0.922)
  the two profiles are of different devices: /device:TPU:18 before, /device:TPU:19 now
where the time goes in v5:
time: 54.1 us; the launch traced here: 53.6 us
  Pallas kernels  28.3 us (52%)
  starting transfers between devices  21.1 us (39%)
  waiting for transfers between devices  1.99 us (4%)
  local copies, waits for them, and re-layouts  1.47 us (3%)
  between operations  0.68 us (1%)
    ppermute x1, starting transfers between devices, local(): lax.ppermute(line, 'reader', [(i, i ^ 1) for i in range(devices)])  9.38 us
    pallas_call x1, Pallas kernels, local(): pl.pallas_call(functools.partial(attend_kernel, state_rows=state_rows, pr...  7.48 us
    pallas_call x1, Pallas kernels, local(): pl.pallas_call(functools.partial(final_kernel, state_rows=state_rows, **s...  7.01 us
    pallas_call x2, Pallas kernels, inner_part(): pl.pallas_call(functools.partial(inner_kernel, first=first, **sizes), gri...  6.56 us
    ppermute x2, starting transfers between devices, shifted(): return lax.ppermute(value, axis, [(i, i + by) for i in range(length - by)])  6.11 us
    all_to_all x1, starting transfers between devices, local(): lax.all_to_all(packed, 'reader', 0, 0, axis_index_groups=lines, tiled=True)  5.61 us
    pallas_call x1, Pallas kernels, local(): pl.pallas_call(functools.partial(tail_kernel, **sizes), grid=(groups,), i...  5.25 us
    pallas_call x1, Pallas kernels, local(): pl.pallas_call(pack_kernel, out_shape=(jax.ShapeDtypeStruct((devices // N...  2.02 us
  transfers between devices with their start and end apart: 4, of which 1 were waited for; matrix products, arithmetic and copies ran while one was open for 0% of the time, Pallas kernels for 36%

profile of v5, /device:TPU:19, one launch (start us, length us, event | category | flops | bytes accessed | tf_op | source)
XLA Modules:
  0.0 53.6 jit_solution(9722610263181204846)
XLA Ops:
  0.6 2.0 %pack.1 = (bf16[8,320,128]{2,1,0:T(8,128)(2,1)}, bf16[256,1024]{1,0:T(8,128)(2,1)S(1)}) custom-call(f32[256,128]{1,0:T(8,128)} %state_ref.1, bf16[8,512]{1,0:T(8,128)(2,1)} %keys_ref.1, bf16[8,512]{1,0:T(8,128)(2,1)} %values_ref.1, bf16[256,512]{1,0:T(8,128)(2,1)} %key_ref.1, bf16[256,512]{1,0:T(8,128)(2,1)} %value_ref.1), custom_call_target="tpu_custom_call" | custom-call | tf_op jit(solution)/shard_map/pack/pallas_call | solution.py:341
  2.7 5.6 %all-to-all-start = ((bf16[8,320,128]{2,1,0:T(8,128)(2,1)}), bf16[8,320,128]{2,1,0:T(8,128)(2,1)S(1)}, u32[]{:S(2)}, u32[]{:S(2)}) async-start(bf16[8,320,128]{2,1,0:T(8,128)(2,1)} %get-tuple-element.22), calls=%async_computation | async-start | bytes 1310720 | tf_op jit(solution)/shard_map/all_to_all | solution.py:352
  8.3 4.2 %collective-permute-start.1 = (bf16[256,1024]{1,0:T(8,128)(2,1)S(1)}, bf16[256,1024]{1,0:T(8,128)(2,1)S(1)}, u32[]{:S(2)}, u32[]{:S(2)}) collective-permute-start(bf16[256,1024]{1,0:T(8,128)(2,1)S(1)} %get-tuple-element.19), channel_id=1, source_target_pairs={{0,1},{1,2},{2,3},{3,4},{4,5},{5,6},{6,7},{7,8},{8,9},{9,10},{10,1... | collective-permute-start | bytes 1572872 | tf_op jit(solution)/shard_map/ppermute | solution.py:289
  12.5 5.3 %tail.1 = (bf16[128,4224]{1,0:T(8,128)(2,1)}, f32[256,128]{1,0:T(8,128)S(1)}, f32[64,256]{1,0:T(8,128)S(1)}, f32[256,128]{1,0:T(8,128)S(1)}) custom-call(s32[1,32]{1,0:T(1,128)} %bitcast.7, f32[64,256]{1,0:T(8,128)} %bitcast.5, f32[1,64]{1,0:T(1,128)} %bitcast.8, bf16[256,4096]{1,0:T(8,128)(2,1)} %x_ref.5, bf16[256,512]{1,0:T(8,128)(2,1)} %write_ref.5), custom_call_target="tpu_custom_call" | custom-call | tf_op jit(solution)/shard_map/tail/pallas_call | solution.py:358
  17.7 1.9 %collective-permute-start = (bf16[128,4224]{1,0:T(8,128)(2,1)}, bf16[128,4224]{1,0:T(8,128)(2,1)}, u32[]{:S(2)}, u32[]{:S(2)}) collective-permute-start(bf16[128,4224]{1,0:T(8,128)(2,1)} %get-tuple-element.18), channel_id=1, source_target_pairs={{0,1},{1,2},{2,3},{3,4},{4,5},{5,6},{6,7},{7,8},{8,9},{9,10},{10,1... | collective-permute-start | bytes 3244040 | tf_op jit(solution)/shard_map/ppermute | solution.py:289
  19.6 2.0 %collective-permute-done.1.prior_key_ref.prior_value_ref = bf16[256,1024]{1,0:T(8,128)(2,1)S(1)} collective-permute-done((bf16[256,1024]{1,0:T(8,128)(2,1)S(1)}, bf16[256,1024]{1,0:T(8,128)(2,1)S(1)}, u32[]{:S(2)}, u32[]{:S(2)}) %collective-permute-start.1) | collective-permute-done | bytes 524320 | tf_op jit(solution)/shard_map/ppermute | solution.py:289
  21.6 4.4 %inner.2.rest_0_ = bf16[256,4096]{1,0:T(8,128)(2,1)S(1)} custom-call(f32[256,128]{1,0:T(8,128)S(1)} %get-tuple-element.16.start_ref, f32[256,128]{1,0:T(8,128)S(1)} %get-tuple-element.17.level_ref, f32[64,256]{1,0:T(8,128)S(1)} %get-tuple-element.21.column_ref, f32[1,64]{1,0:T(1,128)} %bitcast.9, bf16[256,4096]{1,0:T(8,128)(2,1)} %x_ref.5, ...), custom_call_target="tpu_custom_call" | custom-call | flops 1610612736 | bytes 3145728 | tf_op jit(solution)/shard_map/inner/pallas_call | solution.py:390
  26.0 0.0 copy-start
  26.0 0.6 %copy-done = f32[64,256]{1,0:T(8,128)} copy-done((f32[64,256]{1,0:T(8,128)}, f32[64,256]{1,0:T(8,128)S(1)}, u32[]{:S(2)}) %copy-start) | copy-done | bytes 65560
  26.6 0.0 all-to-all-done.rest_0_
  26.6 9.4 %collective-permute-start.2 = (bf16[8,320,128]{2,1,0:T(8,128)(2,1)S(1)}, bf16[8,320,128]{2,1,0:T(8,128)(2,1)S(1)}, u32[]{:S(2)}, u32[]{:S(2)}) collective-permute-start(bf16[8,320,128]{2,1,0:T(8,128)(2,1)S(1)} %all-to-all-done.rest_0_), channel_id=1, source_target_pairs={{0,1},{1,0},{2,3},{3,2},{4,5},{5,4},{6,7},{7,6},{8,9},{9,8},{10,11... | collective-permute-start | bytes 1966088 | tf_op jit(solution)/shard_map/ppermute | solution.py:417
  36.0 0.0 copy-start.1
  36.0 0.8 %copy-done.1 = f32[64,256]{1,0:T(8,128)S(1)} copy-done((f32[64,256]{1,0:T(8,128)S(1)}, f32[64,256]{1,0:T(8,128)}, u32[]{:S(2)}) %copy-start.1) | copy-done | bytes 65560
  36.8 2.2 %inner.3.inner_ref = bf16[256,4096]{1,0:T(8,128)(2,1)S(1)} custom-call(f32[256,128]{1,0:T(8,128)S(1)} %get-tuple-element.16.start_ref, f32[256,128]{1,0:T(8,128)S(1)} %get-tuple-element.17.level_ref, f32[64,256]{1,0:T(8,128)S(1)} %copy-done.1, f32[1,64]{1,0:T(1,128)} %bitcast.10, bf16[256,4096]{1,0:T(8,128)(2,1)} %x_ref.5, ...), custom_call_target="tpu_custom_call", output_to_operand_aliasing={{}: (7, {})} | custom-call | flops 536870912 | bytes 1048576 | tf_op jit(solution)/shard_map/inner/pallas_call | solution.py:390
  39.0 0.0 collective-permute-done.2.rest_1_
  39.1 7.5 %attend.1 = bf16[256,2048]{1,0:T(8,128)(2,1)} custom-call(f32[256,128]{1,0:T(8,128)S(1)} %get-tuple-element.16.start_ref, bf16[256,2048]{1,0:T(8,128)(2,1)} %query_ref.1, bf16[256,512]{1,0:T(8,128)(2,1)} %key_ref.1, bf16[256,512]{1,0:T(8,128)(2,1)} %value_ref.1, bf16[256,1024]{1,0:T(8,128)(2,1)S(1)} %collective-permute-done.1.prior_key_ref.prior_value_ref, ...), custom_call_target="tpu_custom_call" | custom-call | tf_op jit(solution)/shard_map/attend/pallas_call | solution.py:421
  46.5 0.0 collective-permute-done.tail_ref.decay_ref
  46.5 7.0 %final.1 = bf16[256,4096]{1,0:T(8,128)(2,1)} custom-call(f32[256,128]{1,0:T(8,128)S(1)} %get-tuple-element.16.start_ref, f32[256,128]{1,0:T(8,128)S(1)} %get-tuple-element.17.level_ref, bf16[128,4224]{1,0:T(8,128)(2,1)} %collective-permute-done.tail_ref.decay_ref, bf16[128,4224]{1,0:T(8,128)(2,1)} %collective-permute-done.tail_ref.decay_ref, ...), custom_call_target="tpu_custom_call" | custom-call | tf_op jit(solution)/shard_map/final/pallas_call | solution.py:445
Async XLA Ops:
  2.7 24.0 %all-to-all-start = ((bf16[8,320,128]{2,1,0:T(8,128)(2,1)}), bf16[8,320,128]{2,1,0:T(8,128)(2,1)S(1)}, u32[]{:S(2)}, u32[]{:S(2)}) async-start(bf16[8,320,128]{2,1,0:T(8,128)(2,1)} %get-tuple-element.22), calls=%async_computation | async-start | bytes 1310720 | tf_op jit(solution)/shard_map/all_to_all | solution.py:352
  8.3 13.4 %collective-permute-start.1 = (bf16[256,1024]{1,0:T(8,128)(2,1)S(1)}, bf16[256,1024]{1,0:T(8,128)(2,1)S(1)}, u32[]{:S(2)}, u32[]{:S(2)}) collective-permute-start(bf16[256,1024]{1,0:T(8,128)(2,1)S(1)} %get-tuple-element.19), channel_id=1, source_target_pairs={{0,1},{1,2},{2,3},{3,4},{4,5},{5,6},{6,7},{7,8},{8,9},{9,10},{10,1... | collective-permute-start | bytes 1572872 | tf_op jit(solution)/shard_map/ppermute | solution.py:289
  17.7 28.8 %collective-permute-start = (bf16[128,4224]{1,0:T(8,128)(2,1)}, bf16[128,4224]{1,0:T(8,128)(2,1)}, u32[]{:S(2)}, u32[]{:S(2)}) collective-permute-start(bf16[128,4224]{1,0:T(8,128)(2,1)} %get-tuple-element.18), channel_id=1, source_target_pairs={{0,1},{1,2},{2,3},{3,4},{4,5},{5,6},{6,7},{7,8},{8,9},{9,10},{10,1... | collective-permute-start | bytes 3244040 | tf_op jit(solution)/shard_map/ppermute | solution.py:289
  26.0 0.6 %copy-start = (f32[64,256]{1,0:T(8,128)}, f32[64,256]{1,0:T(8,128)S(1)}, u32[]{:S(2)}) copy-start(f32[64,256]{1,0:T(8,128)S(1)} %get-tuple-element.21.column_ref) | copy-start | bytes 196612
  26.6 12.4 %collective-permute-start.2 = (bf16[8,320,128]{2,1,0:T(8,128)(2,1)S(1)}, bf16[8,320,128]{2,1,0:T(8,128)(2,1)S(1)}, u32[]{:S(2)}, u32[]{:S(2)}) collective-permute-start(bf16[8,320,128]{2,1,0:T(8,128)(2,1)S(1)} %all-to-all-done.rest_0_), channel_id=1, source_target_pairs={{0,1},{1,0},{2,3},{3,2},{4,5},{5,4},{6,7},{7,6},{8,9},{9,8},{10,11... | collective-permute-start | bytes 1966088 | tf_op jit(solution)/shard_map/ppermute | solution.py:417
  36.0 0.8 %copy-start.1 = (f32[64,256]{1,0:T(8,128)S(1)}, f32[64,256]{1,0:T(8,128)}, u32[]{:S(2)}) copy-start(f32[64,256]{1,0:T(8,128)} %copy-done) | copy-start | bytes 196612

commit v6 on v5

v6 whole, which is shorter than its diff:
```python
import functools
import math

import jax
import jax.numpy as jnp
from jax import lax
from jax.experimental import pallas as pl
from jax.experimental.pallas import tpu as pltpu
from jax.sharding import PartitionSpec as P

HD = 128
LANES = 128
WIDE = 256
NEAR = 2
LOG2E = 1.4426950408889634
F32 = jnp.float32
BF16 = jnp.bfloat16
MIB = 1 << 20


def iota(shape, dim):
    return lax.broadcasted_iota(jnp.int32, shape, dim)


def dot(a, b, ca=1, cb=0):
    return lax.dot_general(a, b, (((ca,), (cb,)), ((), ())), preferred_element_type=F32)


def expander(heads, group, per_group, channels):
    shape = (2 * heads, per_group * channels)
    row = iota(shape, 0)
    head = jnp.where(row >= heads, row - heads, row) - group * per_group
    column = iota(shape, 1)
    first = head * channels
    return jnp.where((column >= first) & (column < first + channels), 1.0, 0.0).astype(BF16)


def two_parts(value, heads):
    high = value.astype(BF16).astype(F32)
    return jnp.where(iota(value.shape, 1) < heads, high, value - high)


def to_front(value, head):
    return pltpu.roll(value, value.shape[1] - head, 1)


def spread(value, first, channels):
    lane = iota(value.shape, 1)
    source = sum(
        [jnp.where(lane >= part * channels, 1, 0) for part in range(1, LANES // channels)],
        jnp.full(value.shape, first, jnp.int32),
    )
    return jnp.take_along_axis(value, source, axis=1, mode="promise_in_bounds")


def pack_kernel(
    state_ref,
    keys_ref,
    values_ref,
    near_keys_ref,
    near_values_ref,
    out_ref,
    near_ref,
    own_state_ref,
    own_keys_ref,
    own_values_ref,
    held_ref,
    in_sems,
    near_sems,
    out_sems,
):
    width = near_keys_ref.shape[1]
    loads = [
        pltpu.make_async_copy(source, target, in_sems.at[place])
        for place, (source, target) in enumerate(
            ((state_ref, own_state_ref), (keys_ref, own_keys_ref), (values_ref, own_values_ref))
        )
    ]
    for load in loads:
        load.start()
    moves = [
        pltpu.make_async_copy(ref, near_ref.at[:, part * width : (part + 1) * width], near_sems.at[part])
        for part, ref in enumerate((near_keys_ref, near_values_ref))
    ]
    for move in moves:
        move.start()
    for load in loads:
        load.wait()
    rows = own_state_ref.shape[0]
    held_ref[:rows, :] = own_state_ref[...].astype(BF16)
    parts = []
    for ref in (own_keys_ref, own_values_ref):
        wide = ref[...].astype(F32)
        for head in range(wide.shape[1] // HD):
            parts.append(wide[:, head * HD : (head + 1) * HD])
    held_ref[rows:, :] = jnp.concatenate(parts, axis=0).astype(BF16)
    copies = [
        pltpu.make_async_copy(held_ref, out_ref.at[copy], out_sems.at[copy])
        for copy in range(out_ref.shape[0])
    ]
    for copy in copies:
        copy.start()
    for move in moves + copies:
        move.wait()


def level_part(lengths_ref, raw_ref, rate_ref, level_ref, column_ref, start_ref, weight_ref, tail_ref):
    heads, tokens = raw_ref.shape
    base = (lax.axis_index("reader") * tokens).astype(F32)
    lengths = lengths_ref[...].astype(F32)
    answers = lengths.shape[1]
    square = (answers, answers)
    ends = jnp.sum(
        jnp.where(iota(square, 1) <= iota(square, 0), lengths, 0.0), axis=1, keepdims=True
    )
    place = base + iota((1, tokens), 1).astype(F32)
    start = jnp.max(jnp.where(ends <= place, ends, 0.0), axis=0, keepdims=True) - base
    start = jnp.broadcast_to(start, (LANES, tokens)).T
    start_ref[...] = start
    wide = jnp.concatenate([start] * (tokens // LANES), axis=1)
    square = (tokens, tokens)
    source = iota(square, 1)
    mask = (source.astype(F32) >= wide) & (source <= iota(square, 0))
    mask = jnp.where(mask, 1.0, 0.0).astype(BF16)
    raw = raw_ref[...]
    rate = jnp.broadcast_to(rate_ref[...], (heads, heads))
    diagonal = iota((heads, heads), 0) == iota((heads, heads), 1)
    rate = jnp.sum(jnp.where(diagonal, rate, 0.0), axis=1, keepdims=True)
    step = jnp.maximum(raw, 0.0) + jnp.log1p(jnp.exp(-jnp.abs(raw)))
    falling = -rate * step
    first = falling.astype(BF16)
    rest = falling - first.astype(F32)
    second = rest.astype(BF16)
    third = (rest - second.astype(F32)).astype(BF16)
    level = dot(first, mask, 1, 1) + (dot(second, mask, 1, 1) + dot(third, mask, 1, 1))
    column_ref[...] = level * LOG2E - jnp.log(step) * LOG2E
    last = level[:, tokens - 1 :]
    decay = jnp.exp(jnp.broadcast_to(last, (heads, tail_ref.shape[1])))
    high = decay.astype(BF16)
    low = (decay - high.astype(F32)).astype(BF16)
    tail_ref[tail_ref.shape[0] - 2 * heads :, :] = jnp.concatenate([high, low], axis=0)
    own = iota((heads, tokens), 1).astype(F32) >= start[tokens - 1 :, :1]
    weight = jnp.where(own, jnp.exp(last - level) * step, 0.0)
    weight_ref[...] = jnp.concatenate([weight, weight], axis=0).T
    level_ref[...] = jnp.concatenate([level, level], axis=0).T


def tail_part(group, at, weight_ref, x_ref, write_ref, tail_ref, per_group, channels):
    tokens, width = x_ref.shape
    weight = to_front(weight_ref[...], group * per_group)
    weighted = []
    for tile in range(width // LANES):
        scale = spread(weight, tile * LANES // channels, channels)
        x = x_ref[:, tile * LANES : (tile + 1) * LANES].astype(F32)
        weighted.append((x * scale).astype(BF16))
    state = dot(jnp.concatenate(weighted, axis=1), write_ref[...], 0, 0)
    tail_ref[pl.ds(pl.multiple_of(at, width), width), :] = state.astype(BF16)


def tail_kernel(
    lengths_ref,
    raw_ref,
    rate_ref,
    x_ref,
    write_ref,
    tail_ref,
    level_ref,
    column_ref,
    start_ref,
    weight_ref,
    *,
    per_group,
    channels,
):
    group = pl.program_id(0)

    @pl.when(group == 0)
    def _():
        level_part(
            lengths_ref, raw_ref, rate_ref, level_ref, column_ref, start_ref, weight_ref, tail_ref
        )

    at = group * x_ref.shape[1]
    tail_part(group, at, weight_ref, x_ref, write_ref, tail_ref, per_group, channels)


def inner_kernel(
    start_ref,
    level_ref,
    column_ref,
    skip_ref,
    x_ref,
    write_ref,
    read_ref,
    out_ref,
    *,
    heads,
    per_group,
    channels,
):
    group = pl.program_id(0)
    tokens = x_ref.shape[0]
    both = dot(read_ref[...], write_ref[...], 1, 1)
    square = (tokens, tokens)
    source = iota(square, 1)
    wide = jnp.concatenate([start_ref[...]] * (tokens // LANES), axis=1)
    both = jnp.where((source.astype(F32) >= wide) & (source <= iota(square, 0)), both, 0.0)
    lanes = level_ref.shape[1]
    level = pltpu.roll(level_ref[...] * LOG2E, lanes - group * per_group, 1)
    skip = jnp.concatenate([skip_ref[...]] * 2, axis=1)
    skip = two_parts(jnp.broadcast_to(skip, (16, 2 * heads)), heads).astype(BF16)
    skip = dot(skip, expander(heads, group, per_group, channels))[:1, :]
    per_tile = LANES // channels
    lane = iota((tokens, LANES), 1)
    for tile in range(per_group // per_tile):
        at = slice(tile * LANES, (tile + 1) * LANES)
        x = x_ref[:, at].astype(F32)
        owned = []
        for part in range(per_tile):
            mine = (lane >= part * channels) & (lane < (part + 1) * channels)
            owned.append(jnp.where(mine, x, 0.0).astype(BF16))
        for block in range(tokens // LANES):
            rows = slice(block * LANES, (block + 1) * LANES)
            reach = (block + 1) * LANES
            mixing = []
            for part in range(per_tile):
                head = tile * per_tile + part
                gap = level[rows, head : head + 1] - column_ref[head : head + 1, :reach]
                mixing.append(
                    (jnp.exp2(jnp.minimum(gap, 64.0)) * both[rows, :reach]).astype(BF16)
                )
            total = dot(
                jnp.concatenate(mixing, axis=1),
                jnp.concatenate([value[:reach, :] for value in owned], axis=0),
            )
            out_ref[rows, at] = (total + skip[:, at] * x[rows, :]).astype(BF16)


def attend_kernel(
    start_ref,
    query_ref,
    key_ref,
    value_ref,
    prior_key_ref,
    prior_value_ref,
    *rest,
    state_rows,
    prompt_rows,
    kv_count,
):
    gathered, (out_ref, bias_ref) = rest[:-2], rest[-2:]
    head = pl.program_id(0)
    tokens = query_ref.shape[0]
    prompt_count = len(gathered) * gathered[0].shape[0] * prompt_rows
    queries = query_ref.shape[1] // HD
    scale = LOG2E / math.sqrt(HD)
    reach = tokens + LANES

    @pl.when(head == 0)
    def _():
        shape = (LANES, reach)
        wide = jnp.concatenate([start_ref[...]] * (reach // LANES), axis=1)
        for block in range(tokens // LANES):
            rows = slice(block * LANES, (block + 1) * LANES)
            place = iota(shape, 1) + (block * LANES - tokens)
            allowed = (place.astype(F32) >= wide[rows, :]) & (
                place <= iota(shape, 0) + block * LANES
            )
            bias_ref[rows, :] = jnp.where(allowed, 0.0, -jnp.inf)

    def prompt(which):
        at = pl.multiple_of(state_rows + (which * kv_count + head) // 2 * 2 * prompt_rows, 16)
        at = pl.ds(at, 2 * prompt_rows)
        pair = jnp.concatenate([ref[:, at, :] for ref in gathered], axis=0).astype(F32)
        odd = lax.rem(head, 2) == 1
        part = jnp.where(odd, pair[:, prompt_rows:, :], pair[:, :prompt_rows, :])
        return part.reshape(prompt_count, HD).astype(BF16)

    prompt_keys, prompt_values = prompt(0), prompt(1)
    near_keys = jnp.concatenate([prior_key_ref[...], key_ref[...]], axis=0)
    near_values = jnp.concatenate([prior_value_ref[...], value_ref[...]], axis=0)
    ones = jnp.ones((prompt_count + reach, LANES), BF16)
    for block in range(tokens // LANES):
        rows = slice(block * LANES, (block + 1) * LANES)
        window = slice(block * LANES, block * LANES + reach)
        keys = jnp.concatenate([prompt_keys, near_keys[window, :]], axis=0)
        values = jnp.concatenate([prompt_values, near_values[window, :]], axis=0)
        values = jnp.concatenate([values, ones], axis=1)
        stacked = [query_ref[rows, query * HD : (query + 1) * HD] for query in range(queries)]
        scores = dot(jnp.concatenate(stacked, axis=0), keys, 1, 1)
        weights = []
        for query in range(queries):
            own = scores[query * LANES : (query + 1) * LANES, :]
            far, near = own[:, :prompt_count], own[:, prompt_count:] + bias_ref[rows, :]
            own = jnp.concatenate([far, near], axis=1)
            top = jnp.max(own, axis=1, keepdims=True)
            weights.append(jnp.exp2((own - top) * scale).astype(BF16))
        summed = dot(jnp.concatenate(weights, axis=0), values)
        for query in range(queries):
            own = summed[query * LANES : (query + 1) * LANES, :]
            out_ref[rows, query * HD : (query + 1) * HD] = (own[:, :HD] / own[:, HD:]).astype(BF16)


def final_kernel(
    start_ref,
    level_ref,
    tail_ref,
    decay_ref,
    read_ref,
    inner_ref,
    gate_ref,
    gain_ref,
    *rest,
    state_rows,
    heads,
    per_group,
    channels,
):
    gathered, (out_ref, value_ref) = rest[:NEAR], rest[-2:]
    group = pl.program_id(0)
    tokens, state = read_ref.shape
    width = per_group * channels

    scale = to_front(jnp.exp(level_ref[...]), group * per_group)
    carried = start_ref[:, :state] < 0
    read = read_ref[...].astype(F32)
    read = jnp.concatenate([jnp.where(carried, 0.0, read), jnp.where(carried, read, 0.0)], axis=1)
    read = read.astype(BF16)
    at = pl.multiple_of(group * per_group, per_group)
    decay = decay_ref[pl.ds(at, per_group), :].astype(F32)
    decay = decay + decay_ref[pl.ds(heads + at, per_group), :].astype(F32)
    own = lax.rem(lax.axis_index("reader"), NEAR)
    seeds = []
    for run in range(gathered[0].shape[0]):
        parts = [ref[run, :state_rows, :] for ref in gathered]
        bit = 1
        while bit < NEAR:
            swap = lax.rem(own // bit, 2) == 1
            parts = [jnp.where(swap, parts[i ^ bit], parts[i]) for i in range(NEAR)]
            bit *= 2
        seeds += parts
    seeds = jnp.concatenate(seeds, axis=0)
    squares = [None] * (tokens // LANES)
    for tile in range(width // WIDE):
        at = slice(tile * WIDE, (tile + 1) * WIDE)
        tile_heads = range(at.start // channels, at.stop // channels)
        falls = [jnp.broadcast_to(decay[h : h + 1, :], (channels, state)) for h in tile_heads]
        seed = seeds[at, :]
        entering = seed.astype(F32) * jnp.concatenate(falls, axis=0) + tail_ref[at, :].astype(F32)
        states = jnp.concatenate([seed, entering.astype(BF16)], axis=1)
        for block in range(tokens // LANES):
            rows = slice(block * LANES, (block + 1) * LANES)
            inflow = dot(read[rows, :], states, 1, 1)
            falls = [
                spread(scale[rows, :], (at.start + begin) // channels, channels)
                for begin in range(0, WIDE, LANES)
            ]
            inflow = inflow * jnp.concatenate(falls, axis=1)
            gate = gate_ref[rows, at].astype(F32)
            gated = inner_ref[rows, at].astype(F32) + inflow
            gated = gated * (gate * (0.5 + 0.5 * jnp.tanh(0.5 * gate)))
            value_ref[rows, at] = gated
            square = gated * gated
            for part in range(WIDE // LANES):
                piece = square[:, part * LANES : (part + 1) * LANES]
                squares[block] = piece if squares[block] is None else squares[block] + piece
    for block in range(tokens // LANES):
        rows = slice(block * LANES, (block + 1) * LANES)
        mean = jnp.sum(squares[block], axis=1, keepdims=True) * (1.0 / width)
        norm = lax.rsqrt(mean + 1e-05)
        for tile in range(width // WIDE):
            at = slice(tile * WIDE, (tile + 1) * WIDE)
            out_ref[rows, at] = (value_ref[rows, at] * norm * gain_ref[:, at]).astype(BF16)


def shifted(value, axis, by):
    length = lax.axis_size(axis)
    return lax.ppermute(value, axis, [(i, i + by) for i in range(length - by)])


def params(limit=32):
    return pltpu.CompilerParams(vmem_limit_bytes=limit * MIB)


def whole(shape):
    return pl.BlockSpec(shape, lambda g: (0,) * len(shape))


def local(
    answer_lengths,
    mixer_input,
    gate_input,
    state_write,
    state_read,
    step_raw,
    decay_rate,
    skip_gain,
    norm_gain,
    prompt_state,
    queries,
    answer_keys,
    answer_values,
    prompt_keys,
    prompt_values,
):
    tokens, columns = mixer_input.shape
    heads = decay_rate.shape[0]
    state_rows, state = prompt_state.shape
    groups = state_write.shape[1] // state
    per_group = heads // groups
    channels = columns // heads
    width = per_group * channels
    prompt_rows, kv_width = prompt_keys.shape
    kv_count = kv_width // HD
    devices = lax.axis_size("reader")
    in_hbm = lambda value: pltpu.with_memory_space_constraint(value, pltpu.MemorySpace.HBM)
    mixer_input, gate_input, state_write, state_read = map(
        in_hbm, (mixer_input, gate_input, state_write, state_read)
    )
    prompt_state, queries, answer_keys, answer_values, prompt_keys, prompt_values = map(
        in_hbm, (prompt_state, queries, answer_keys, answer_values, prompt_keys, prompt_values)
    )
    lengths, rate, skip, gain = map(
        lambda value: in_hbm(value.reshape(1, -1)),
        (answer_lengths, decay_rate, skip_gain, norm_gain),
    )
    sizes = dict(heads=heads, per_group=per_group, channels=channels)
    packed_rows = state_rows + 2 * prompt_rows * kv_count

    packed, near = pl.pallas_call(
        pack_kernel,
        out_shape=(
            jax.ShapeDtypeStruct((devices // NEAR, packed_rows, HD), BF16),
            jax.ShapeDtypeStruct((tokens, 2 * kv_width), BF16),
        ),
        in_specs=[pl.BlockSpec(memory_space=pl.ANY)] * 5,
        out_specs=(pl.BlockSpec(memory_space=pl.ANY), pl.BlockSpec(memory_space=pl.ANY)),
        scratch_shapes=[
            pltpu.VMEM(prompt_state.shape, F32),
            pltpu.VMEM(prompt_keys.shape, BF16),
            pltpu.VMEM(prompt_values.shape, BF16),
            pltpu.VMEM((packed_rows, HD), BF16),
            pltpu.SemaphoreType.DMA((3,)),
            pltpu.SemaphoreType.DMA((2,)),
            pltpu.SemaphoreType.DMA((devices // NEAR,)),
        ],
        compiler_params=params(),
        name="pack",
    )(prompt_state, prompt_keys, prompt_values, answer_keys, answer_values)
    packed, raw = lax.optimization_barrier((packed, step_raw.T))
    lines = [list(range(first, devices, NEAR)) for first in range(NEAR)]
    line = lax.all_to_all(packed, "reader", 0, 0, axis_index_groups=lines, tiled=True)
    prior = shifted(near, "reader", 1)
    raw = in_hbm(raw)

    small = pl.CostEstimate(flops=0, bytes_accessed=0, transcendentals=0)
    by_group = lambda rows: pl.BlockSpec((rows, state), lambda g: (0, g))
    wide = pl.BlockSpec((tokens, width), lambda g: (0, g))
    tail, level, column, start, weight = pl.pallas_call(
        functools.partial(tail_kernel, per_group=per_group, channels=channels),
        grid=(groups,),
        in_specs=[
            whole(lengths.shape),
            whole(raw.shape),
            whole((1, heads)),
            wide,
            by_group(tokens),
        ],
        out_specs=(
            whole((columns + 2 * heads, state)),
            whole((tokens, 2 * heads)),
            whole((heads, tokens)),
            whole((tokens, LANES)),
            whole((tokens, 2 * heads)),
        ),
        out_shape=(
            jax.ShapeDtypeStruct((columns + 2 * heads, state), BF16),
            jax.ShapeDtypeStruct((tokens, 2 * heads), F32),
            jax.ShapeDtypeStruct((heads, tokens), F32),
            jax.ShapeDtypeStruct((tokens, LANES), F32),
            jax.ShapeDtypeStruct((tokens, 2 * heads), F32),
        ),
        compiler_params=params(),
        cost_estimate=small,
        name="tail",
    )(lengths, raw, rate, mixer_input, state_write)
    tail = shifted(tail, "reader", 1)
    inner = pl.pallas_call(
        functools.partial(inner_kernel, **sizes),
        grid=(groups,),
        in_specs=[
            whole((tokens, LANES)),
            whole((tokens, 2 * heads)),
            pl.BlockSpec((per_group, tokens), lambda g: (g, 0)),
            whole((1, heads)),
            wide,
            by_group(tokens),
            by_group(tokens),
        ],
        out_specs=wide,
        out_shape=jax.ShapeDtypeStruct((tokens, columns), BF16),
        compiler_params=params(),
        cost_estimate=small,
        name="inner",
    )(start, level, column, skip, mixer_input, state_write, state_read)
    prior, line, inner = lax.optimization_barrier((prior, line, inner))
    gathered = (line, lax.ppermute(line, "reader", [(i, i ^ 1) for i in range(devices)]))

    group_size = queries.shape[1] // kv_width
    attention_out = pl.pallas_call(
        functools.partial(
            attend_kernel,
            state_rows=state_rows,
            prompt_rows=prompt_rows,
            kv_count=kv_count,
        ),
        grid=(kv_count,),
        in_specs=[
            whole((tokens, LANES)),
            pl.BlockSpec((tokens, group_size * HD), lambda k: (0, k)),
            pl.BlockSpec((tokens, HD), lambda k: (0, k)),
            pl.BlockSpec((tokens, HD), lambda k: (0, k)),
            pl.BlockSpec((tokens, HD), lambda k: (0, k)),
            pl.BlockSpec((tokens, HD), lambda k: (0, kv_count + k)),
        ]
        + [whole((devices // NEAR, packed_rows, HD))] * NEAR,
        out_specs=pl.BlockSpec((tokens, group_size * HD), lambda k: (0, k)),
        out_shape=jax.ShapeDtypeStruct(queries.shape, BF16),
        scratch_shapes=[pltpu.VMEM((tokens, tokens + LANES), F32)],
        compiler_params=params(),
        cost_estimate=small,
        name="attend",
    )(start, queries, answer_keys, answer_values, prior, prior, *gathered)

    inner, attention_out = lax.optimization_barrier((inner, attention_out))
    mixer_out = pl.pallas_call(
        functools.partial(final_kernel, state_rows=state_rows, **sizes),
        grid=(groups,),
        in_specs=[
            whole((tokens, LANES)),
            whole((tokens, 2 * heads)),
            pl.BlockSpec((width, state), lambda g: (g, 0)),
            pl.BlockSpec((2 * heads, state), lambda g: (columns // (2 * heads), 0)),
            by_group(tokens),
            wide,
            wide,
            pl.BlockSpec((1, width), lambda g: (0, g)),
        ]
        + [pl.BlockSpec((devices // groups // NEAR, packed_rows, HD), lambda g: (g, 0, 0))] * NEAR,
        out_specs=wide,
        out_shape=jax.ShapeDtypeStruct((tokens, columns), BF16),
        scratch_shapes=[pltpu.VMEM((tokens, width), F32)],
        compiler_params=params(),
        cost_estimate=small,
        name="final",
    )(start, level, tail, tail, state_read, inner, gate_input, gain, *gathered)
    return (mixer_out, attention_out)


def solution(mesh):
    rows = P(("group", "reader"), None)
    in_specs = (P("group"),) + (rows,) * 5 + (P(),) * 3 + (rows,) * 6
    return jax.shard_map(
        local, mesh=mesh, in_specs=in_specs, out_specs=(rows, rows), check_vma=False
    )
```

time: 54.1 us -> 63.6 us (1.18)
  the two profiles are of different devices: /device:TPU:19 before, /device:TPU:18 now
where the time goes in v6:
time: 63.6 us; the launch traced here: 63.1 us
  Pallas kernels  40.9 us (64%)
  starting transfers between devices  11.6 us (18%)
  waiting for transfers between devices  10 us (16%)
  between operations  0.67 us (1%)
    pallas_call x1, Pallas kernels, local(): pl.pallas_call(pack_kernel, out_shape=(jax.ShapeDtypeStruct((devices // N...  17.1 us
    ppermute x2, waiting for transfers between devices, shifted(): return lax.ppermute(value, axis, [(i, i + by) for i in range(length - by)])  7.92 us
    pallas_call x1, Pallas kernels, local(): pl.pallas_call(functools.partial(attend_kernel, state_rows=state_rows, pr...  6.35 us
    all_to_all x1, starting transfers between devices, local(): lax.all_to_all(packed, 'reader', 0, 0, axis_index_groups=lines, tiled=True)  6.18 us
    pallas_call x1, Pallas kernels, local(): pl.pallas_call(functools.partial(tail_kernel, per_group=per_group, channe...  6.04 us
    pallas_call x1, Pallas kernels, local(): pl.pallas_call(functools.partial(final_kernel, state_rows=state_rows, **s...  6.01 us
    pallas_call x1, Pallas kernels, local(): pl.pallas_call(functools.partial(inner_kernel, **sizes), grid=(groups,),...  5.38 us
    ppermute x2, starting transfers between devices, shifted(): return lax.ppermute(value, axis, [(i, i + by) for i in range(length - by)])  5.37 us
  transfers between devices with their start and end apart: 4, of which 3 were waited for; matrix products, arithmetic and copies ran while one was open for 0% of the time, Pallas kernels for 28%

profile of v6, /device:TPU:18, one launch (start us, length us, event | category | flops | bytes accessed | tf_op | source)
XLA Modules:
  0.0 63.1 jit_solution(1973763184339887812)
XLA Ops:
  0.6 17.1 %pack.1 = (bf16[8,320,128]{2,1,0:T(8,128)(2,1)}, bf16[256,1024]{1,0:T(8,128)(2,1)}) custom-call(f32[256,128]{1,0:T(8,128)} %state_ref.1, bf16[8,512]{1,0:T(8,128)(2,1)} %keys_ref.1, bf16[8,512]{1,0:T(8,128)(2,1)} %values_ref.1, bf16[256,512]{1,0:T(8,128)(2,1)} %key_ref.1, bf16[256,512]{1,0:T(8,128)(2,1)} %value_ref.1), custom_call_target="tpu_custom_call" | custom-call | tf_op jit(solution)/shard_map/pack/pallas_call | solution.py:430
  17.8 6.2 %all-to-all-start = ((bf16[8,320,128]{2,1,0:T(8,128)(2,1)}), bf16[8,320,128]{2,1,0:T(8,128)(2,1)S(1)}, u32[]{:S(2)}, u32[]{:S(2)}) async-start(bf16[8,320,128]{2,1,0:T(8,128)(2,1)} %get-tuple-element.21), calls=%async_computation | async-start | bytes 1310720 | tf_op jit(solution)/shard_map/all_to_all | solution.py:452
  23.9 1.9 %collective-permute-start.1 = (bf16[256,1024]{1,0:T(8,128)(2,1)}, bf16[256,1024]{1,0:T(8,128)(2,1)S(1)}, u32[]{:S(2)}, u32[]{:S(2)}) collective-permute-start(bf16[256,1024]{1,0:T(8,128)(2,1)} %get-tuple-element.20), channel_id=1, source_target_pairs={{0,1},{1,2},{2,3},{3,4},{4,5},{5,6},{6,7},{7,8},{8,9},{9,10},{10,1... | collective-permute-start | bytes 1572872 | tf_op jit(solution)/shard_map/ppermute | solution.py:378
  25.9 6.0 %tail.1 = (bf16[4224,128]{1,0:T(8,128)(2,1)}, f32[256,128]{1,0:T(8,128)S(1)}, f32[64,256]{1,0:T(8,128)S(1)}, f32[256,128]{1,0:T(8,128)S(1)}, f32[256,128]{1,0:T(8,128)}) custom-call(s32[1,32]{1,0:T(1,128)} %bitcast.7, f32[64,256]{1,0:T(8,128)} %bitcast.5, f32[1,64]{1,0:T(1,128)} %bitcast.8, bf16[256,4096]{1,0:T(8,128)(2,1)} %x_ref.3, bf16[256,512]{1,0:T(8,128)(2,1)} %write_ref.3), custom_call_target="tpu_custom_call" | custom-call | tf_op jit(solution)/shard_map/tail/pallas_call | solution.py:459
  31.9 3.5 %collective-permute-start = (bf16[4224,128]{1,0:T(8,128)(2,1)}, bf16[4224,128]{1,0:T(8,128)(2,1)}, u32[]{:S(2)}, u32[]{:S(2)}) collective-permute-start(bf16[4224,128]{1,0:T(8,128)(2,1)} %get-tuple-element.19), channel_id=1, source_target_pairs={{0,1},{1,2},{2,3},{3,4},{4,5},{5,6},{6,7},{7,8},{8,9},{9,10},{10,1... | collective-permute-start | bytes 3244040 | tf_op jit(solution)/shard_map/ppermute | solution.py:378
  35.4 5.4 %inner.1.inner_ref = bf16[256,4096]{1,0:T(8,128)(2,1)S(1)} custom-call(f32[256,128]{1,0:T(8,128)S(1)} %get-tuple-element.17.start_ref, f32[256,128]{1,0:T(8,128)S(1)} %get-tuple-element.18.level_ref, f32[64,256]{1,0:T(8,128)S(1)} %get-tuple-element.22.column_ref, f32[1,64]{1,0:T(1,128)} %bitcast.9, bf16[256,4096]{1,0:T(8,128)(2,1)} %x_ref.3, ...), custom_call_target="tpu_custom_call" | custom-call | tf_op jit(solution)/shard_map/inner/pallas_call | solution.py:488
  40.8 4.7 %collective-permute-done.1.prior_key_ref.prior_value_ref = bf16[256,1024]{1,0:T(8,128)(2,1)S(1)} collective-permute-done((bf16[256,1024]{1,0:T(8,128)(2,1)}, bf16[256,1024]{1,0:T(8,128)(2,1)S(1)}, u32[]{:S(2)}, u32[]{:S(2)}) %collective-permute-start.1) | collective-permute-done | bytes 524320 | tf_op jit(solution)/shard_map/ppermute | solution.py:378
  45.4 0.0 all-to-all-done.rest_0_
  45.4 0.0 collective-permute-start.2
  45.4 2.1 %collective-permute-done.2.rest_1_ = bf16[8,320,128]{2,1,0:T(8,128)(2,1)S(1)} collective-permute-done((bf16[8,320,128]{2,1,0:T(8,128)(2,1)S(1)}, bf16[8,320,128]{2,1,0:T(8,128)(2,1)S(1)}, u32[]{:S(2)}, u32[]{:S(2)}) %collective-permute-start.2) | collective-permute-done | bytes 655392 | tf_op jit(solution)/shard_map/ppermute | solution.py:507
  47.5 6.3 %attend.1 = bf16[256,2048]{1,0:T(8,128)(2,1)} custom-call(f32[256,128]{1,0:T(8,128)S(1)} %get-tuple-element.17.start_ref, bf16[256,2048]{1,0:T(8,128)(2,1)} %query_ref.1, bf16[256,512]{1,0:T(8,128)(2,1)} %key_ref.1, bf16[256,512]{1,0:T(8,128)(2,1)} %value_ref.1, bf16[256,1024]{1,0:T(8,128)(2,1)S(1)} %collective-permute-done.1.prior_key_ref.prior_value_ref, ...), custom_call_target="tpu_custom_call" | custom-call | tf_op jit(solution)/shard_map/attend/pallas_call | solution.py:510
  53.9 3.2 %collective-permute-done.tail_ref.decay_ref = bf16[4224,128]{1,0:T(8,128)(2,1)} collective-permute-done((bf16[4224,128]{1,0:T(8,128)(2,1)}, bf16[4224,128]{1,0:T(8,128)(2,1)}, u32[]{:S(2)}, u32[]{:S(2)}) %collective-permute-start) | collective-permute-done | bytes 1081376 | tf_op jit(solution)/shard_map/ppermute | solution.py:378
  57.1 6.0 %final.1 = bf16[256,4096]{1,0:T(8,128)(2,1)} custom-call(f32[256,128]{1,0:T(8,128)S(1)} %get-tuple-element.17.start_ref, f32[256,128]{1,0:T(8,128)S(1)} %get-tuple-element.18.level_ref, bf16[4224,128]{1,0:T(8,128)(2,1)} %collective-permute-done.tail_ref.decay_ref, bf16[4224,128]{1,0:T(8,128)(2,1)} %collective-permute-done.tail_ref.decay_ref, ...), custom_call_target="tpu_custom_call" | custom-call | tf_op jit(solution)/shard_map/final/pallas_call | solution.py:536
Async XLA Ops:
  17.8 27.7 %all-to-all-start = ((bf16[8,320,128]{2,1,0:T(8,128)(2,1)}), bf16[8,320,128]{2,1,0:T(8,128)(2,1)S(1)}, u32[]{:S(2)}, u32[]{:S(2)}) async-start(bf16[8,320,128]{2,1,0:T(8,128)(2,1)} %get-tuple-element.21), calls=%async_computation | async-start | bytes 1310720 | tf_op jit(solution)/shard_map/all_to_all | solution.py:452
  23.9 21.5 %collective-permute-start.1 = (bf16[256,1024]{1,0:T(8,128)(2,1)}, bf16[256,1024]{1,0:T(8,128)(2,1)S(1)}, u32[]{:S(2)}, u32[]{:S(2)}) collective-permute-start(bf16[256,1024]{1,0:T(8,128)(2,1)} %get-tuple-element.20), channel_id=1, source_target_pairs={{0,1},{1,2},{2,3},{3,4},{4,5},{5,6},{6,7},{7,8},{8,9},{9,10},{10,1... | collective-permute-start | bytes 1572872 | tf_op jit(solution)/shard_map/ppermute | solution.py:378
  31.9 25.2 %collective-permute-start = (bf16[4224,128]{1,0:T(8,128)(2,1)}, bf16[4224,128]{1,0:T(8,128)(2,1)}, u32[]{:S(2)}, u32[]{:S(2)}) collective-permute-start(bf16[4224,128]{1,0:T(8,128)(2,1)} %get-tuple-element.19), channel_id=1, source_target_pairs={{0,1},{1,2},{2,3},{3,4},{4,5},{5,6},{6,7},{7,8},{8,9},{9,10},{10,1... | collective-permute-start | bytes 3244040 | tf_op jit(solution)/shard_map/ppermute | solution.py:378
  45.4 2.1 %collective-permute-start.2 = (bf16[8,320,128]{2,1,0:T(8,128)(2,1)S(1)}, bf16[8,320,128]{2,1,0:T(8,128)(2,1)S(1)}, u32[]{:S(2)}, u32[]{:S(2)}) collective-permute-start(bf16[8,320,128]{2,1,0:T(8,128)(2,1)S(1)} %all-to-all-done.rest_0_), channel_id=1, source_target_pairs={{0,1},{1,0},{2,3},{3,2},{4,5},{5,4},{6,7},{7,6},{8,9},{9,8},{10,11... | collective-permute-start | bytes 1966088 | tf_op jit(solution)/shard_map/ppermute | solution.py:507

commit v7 on v6

--- a/solution.py
+++ b/solution.py
@@ -45,63 +45,32 @@
 
 
 def spread(value, first, channels):
-    lane = iota(value.shape, 1)
-    source = sum(
-        [jnp.where(lane >= part * channels, 1, 0) for part in range(1, LANES // channels)],
-        jnp.full(value.shape, first, jnp.int32),
-    )
+    lane = iota((8, LANES), 1)
+    source = jnp.full((8, LANES), first, jnp.int32)
+    for part in range(1, LANES // channels):
+        source = source + jnp.where(lane >= part * channels, 1, 0)
+    source = jnp.concatenate([source] * (value.shape[0] // 8), axis=0)
     return jnp.take_along_axis(value, source, axis=1, mode="promise_in_bounds")
 
 
-def pack_kernel(
-    state_ref,
-    keys_ref,
-    values_ref,
-    near_keys_ref,
-    near_values_ref,
-    out_ref,
-    near_ref,
-    own_state_ref,
-    own_keys_ref,
-    own_values_ref,
-    held_ref,
-    in_sems,
-    near_sems,
-    out_sems,
-):
-    width = near_keys_ref.shape[1]
-    loads = [
-        pltpu.make_async_copy(source, target, in_sems.at[place])
-        for place, (source, target) in enumerate(
-            ((state_ref, own_state_ref), (keys_ref, own_keys_ref), (values_ref, own_values_ref))
-        )
-    ]
-    for load in loads:
-        load.start()
-    moves = [
-        pltpu.make_async_copy(ref, near_ref.at[:, part * width : (part + 1) * width], near_sems.at[part])
-        for part, ref in enumerate((near_keys_ref, near_values_ref))
-    ]
-    for move in moves:
-        move.start()
-    for load in loads:
-        load.wait()
-    rows = own_state_ref.shape[0]
-    held_ref[:rows, :] = own_state_ref[...].astype(BF16)
+def join_kernel(keys_ref, values_ref, out_ref):
+    width = keys_ref.shape[1]
+    out_ref[:, :width] = keys_ref[...]
+    out_ref[:, width:] = values_ref[...]
+
+
+def pack_kernel(state_ref, keys_ref, values_ref, out_ref):
+    rows = state_ref.shape[0]
+    state = state_ref[...].astype(BF16)
     parts = []
-    for ref in (own_keys_ref, own_values_ref):
+    for ref in (keys_ref, values_ref):
         wide = ref[...].astype(F32)
         for head in range(wide.shape[1] // HD):
             parts.append(wide[:, head * HD : (head + 1) * HD])
-    held_ref[rows:, :] = jnp.concatenate(parts, axis=0).astype(BF16)
-    copies = [
-        pltpu.make_async_copy(held_ref, out_ref.at[copy], out_sems.at[copy])
-        for copy in range(out_ref.shape[0])
-    ]
-    for copy in copies:
-        copy.start()
-    for move in moves + copies:
-        move.wait()
+    parts = jnp.concatenate(parts, axis=0).astype(BF16)
+    for copy in range(out_ref.shape[0]):
+        out_ref[copy, :rows, :] = state
+        out_ref[copy, rows:, :] = parts
 
 
 def level_part(lengths_ref, raw_ref, rate_ref, level_ref, column_ref, start_ref, weight_ref, tail_ref):
@@ -207,25 +176,28 @@
     both = jnp.where((source.astype(F32) >= wide) & (source <= iota(square, 0)), both, 0.0)
     lanes = level_ref.shape[1]
     level = pltpu.roll(level_ref[...] * LOG2E, lanes - group * per_group, 1)
+    column = column_ref[pl.ds(pl.multiple_of(group * per_group, per_group), per_group), :]
+    begin = pl.multiple_of(group * per_group * channels, per_group * channels)
     skip = jnp.concatenate([skip_ref[...]] * 2, axis=1)
     skip = two_parts(jnp.broadcast_to(skip, (16, 2 * heads)), heads).astype(BF16)
     skip = dot(skip, expander(heads, group, per_group, channels))[:1, :]
     per_tile = LANES // channels
-    lane = iota((tokens, LANES), 1)
+    lane = iota((16, LANES), 1)
+    own = []
+    for part in range(per_tile):
+        mine = (lane >= part * channels) & (lane < (part + 1) * channels)
+        own.append(jnp.concatenate([jnp.where(mine, 1.0, 0.0).astype(BF16)] * (tokens // 16), axis=0))
     for tile in range(per_group // per_tile):
         at = slice(tile * LANES, (tile + 1) * LANES)
-        x = x_ref[:, at].astype(F32)
-        owned = []
-        for part in range(per_tile):
-            mine = (lane >= part * channels) & (lane < (part + 1) * channels)
-            owned.append(jnp.where(mine, x, 0.0).astype(BF16))
+        x = x_ref[:, at]
+        owned = [x * mine for mine in own]
         for block in range(tokens // LANES):
             rows = slice(block * LANES, (block + 1) * LANES)
             reach = (block + 1) * LANES
             mixing = []
             for part in range(per_tile):
                 head = tile * per_tile + part
-                gap = level[rows, head : head + 1] - column_ref[head : head + 1, :reach]
+                gap = level[rows, head : head + 1] - column[head : head + 1, :reach]
                 mixing.append(
                     (jnp.exp2(jnp.minimum(gap, 64.0)) * both[rows, :reach]).astype(BF16)
                 )
@@ -233,7 +205,9 @@
                 jnp.concatenate(mixing, axis=1),
                 jnp.concatenate([value[:reach, :] for value in owned], axis=0),
             )
-            out_ref[rows, at] = (total + skip[:, at] * x[rows, :]).astype(BF16)
+            out_ref[rows, pl.ds(begin + at.start, LANES)] = (
+                total + skip[:, at] * x[rows, :].astype(F32)
+            ).astype(BF16)
 
 
 def attend_kernel(
@@ -241,8 +215,7 @@
     query_ref,
     key_ref,
     value_ref,
-    prior_key_ref,
-    prior_value_ref,
+    prior_ref,
     *rest,
     state_rows,
     prompt_rows,
@@ -277,8 +250,12 @@
         return part.reshape(prompt_count, HD).astype(BF16)
 
     prompt_keys, prompt_values = prompt(0), prompt(1)
-    near_keys = jnp.concatenate([prior_key_ref[...], key_ref[...]], axis=0)
-    near_values = jnp.concatenate([prior_value_ref[...], value_ref[...]], axis=0)
+    prior = [
+        prior_ref[:, pl.ds(pl.multiple_of((which * kv_count + head) * HD, HD), HD)]
+        for which in range(2)
+    ]
+    near_keys = jnp.concatenate([prior[0], key_ref[...]], axis=0)
+    near_values = jnp.concatenate([prior[1], value_ref[...]], axis=0)
     ones = jnp.ones((prompt_count + reach, LANES), BF16)
     for block in range(tokens // LANES):
         rows = slice(block * LANES, (block + 1) * LANES)
@@ -291,10 +268,15 @@
         weights = []
         for query in range(queries):
             own = scores[query * LANES : (query + 1) * LANES, :]
-            far, near = own[:, :prompt_count], own[:, prompt_count:] + bias_ref[rows, :]
-            own = jnp.concatenate([far, near], axis=1)
-            top = jnp.max(own, axis=1, keepdims=True)
-            weights.append(jnp.exp2((own - top) * scale).astype(BF16))
+            far, near = own[:, :prompt_count], own[:, prompt_count:]
+            bias = bias_ref[rows, :]
+            top = jnp.maximum(
+                jnp.max(far, axis=1, keepdims=True), jnp.max(near + bias, axis=1, keepdims=True)
+            )
+            level = top * scale
+            far = jnp.exp2(far * scale - level)
+            near = jnp.exp2(near * scale + (bias - level))
+            weights.append(jnp.concatenate([far, near], axis=1).astype(BF16))
         summed = dot(jnp.concatenate(weights, axis=0), values)
         for query in range(queries):
             own = summed[query * LANES : (query + 1) * LANES, :]
@@ -305,7 +287,6 @@
     start_ref,
     level_ref,
     tail_ref,
-    decay_ref,
     read_ref,
     inner_ref,
     gate_ref,
@@ -326,13 +307,15 @@
     read = read_ref[...].astype(F32)
     read = jnp.concatenate([jnp.where(carried, 0.0, read), jnp.where(carried, read, 0.0)], axis=1)
     read = read.astype(BF16)
-    at = pl.multiple_of(group * per_group, per_group)
-    decay = decay_ref[pl.ds(at, per_group), :].astype(F32)
-    decay = decay + decay_ref[pl.ds(heads + at, per_group), :].astype(F32)
+    falls_at = heads * channels + pl.multiple_of(group * per_group, per_group)
+    decay = tail_ref[pl.ds(falls_at, per_group), :].astype(F32)
+    decay = decay + tail_ref[pl.ds(falls_at + heads, per_group), :].astype(F32)
+    begin = pl.multiple_of(group * width, width)
     own = lax.rem(lax.axis_index("reader"), NEAR)
     seeds = []
-    for run in range(gathered[0].shape[0]):
-        parts = [ref[run, :state_rows, :] for ref in gathered]
+    runs = width // (NEAR * state_rows)
+    for run in range(runs):
+        parts = [ref[group * runs + run, :state_rows, :] for ref in gathered]
         bit = 1
         while bit < NEAR:
             swap = lax.rem(own // bit, 2) == 1
@@ -346,19 +329,20 @@
         tile_heads = range(at.start // channels, at.stop // channels)
         falls = [jnp.broadcast_to(decay[h : h + 1, :], (channels, state)) for h in tile_heads]
         seed = seeds[at, :]
-        entering = seed.astype(F32) * jnp.concatenate(falls, axis=0) + tail_ref[at, :].astype(F32)
+        entering = seed.astype(F32) * jnp.concatenate(falls, axis=0)
+        entering = entering + tail_ref[pl.ds(begin + at.start, WIDE), :].astype(F32)
         states = jnp.concatenate([seed, entering.astype(BF16)], axis=1)
         for block in range(tokens // LANES):
             rows = slice(block * LANES, (block + 1) * LANES)
             inflow = dot(read[rows, :], states, 1, 1)
             falls = [
-                spread(scale[rows, :], (at.start + begin) // channels, channels)
-                for begin in range(0, WIDE, LANES)
+                spread(scale[rows, :], (at.start + offset) // channels, channels)
+                for offset in range(0, WIDE, LANES)
             ]
             inflow = inflow * jnp.concatenate(falls, axis=1)
-            gate = gate_ref[rows, at].astype(F32)
-            gated = inner_ref[rows, at].astype(F32) + inflow
-            gated = gated * (gate * (0.5 + 0.5 * jnp.tanh(0.5 * gate)))
+            half = 0.5 * gate_ref[rows, at].astype(F32)
+            gated = inner_ref[rows, pl.ds(begin + at.start, WIDE)].astype(F32) + inflow
+            gated = gated * (half + half * jnp.tanh(half))
             value_ref[rows, at] = gated
             square = gated * gated
             for part in range(WIDE // LANES):
@@ -417,36 +401,32 @@
     mixer_input, gate_input, state_write, state_read = map(
         in_hbm, (mixer_input, gate_input, state_write, state_read)
     )
-    prompt_state, queries, answer_keys, answer_values, prompt_keys, prompt_values = map(
-        in_hbm, (prompt_state, queries, answer_keys, answer_values, prompt_keys, prompt_values)
+    prompt_state, queries, prompt_keys, prompt_values = map(
+        in_hbm, (prompt_state, queries, prompt_keys, prompt_values)
     )
     lengths, rate, skip, gain = map(
         lambda value: in_hbm(value.reshape(1, -1)),
         (answer_lengths, decay_rate, skip_gain, norm_gain),
     )
+    at_hand = pl.BlockSpec(memory_space=pltpu.VMEM)
     sizes = dict(heads=heads, per_group=per_group, channels=channels)
     packed_rows = state_rows + 2 * prompt_rows * kv_count
 
-    packed, near = pl.pallas_call(
+    packed = pl.pallas_call(
         pack_kernel,
-        out_shape=(
-            jax.ShapeDtypeStruct((devices // NEAR, packed_rows, HD), BF16),
-            jax.ShapeDtypeStruct((tokens, 2 * kv_width), BF16),
-        ),
-        in_specs=[pl.BlockSpec(memory_space=pl.ANY)] * 5,
-        out_specs=(pl.BlockSpec(memory_space=pl.ANY), pl.BlockSpec(memory_space=pl.ANY)),
-        scratch_shapes=[
-            pltpu.VMEM(prompt_state.shape, F32),
-            pltpu.VMEM(prompt_keys.shape, BF16),
-            pltpu.VMEM(prompt_values.shape, BF16),
-            pltpu.VMEM((packed_rows, HD), BF16),
-            pltpu.SemaphoreType.DMA((3,)),
-            pltpu.SemaphoreType.DMA((2,)),
-            pltpu.SemaphoreType.DMA((devices // NEAR,)),
-        ],
+        out_shape=jax.ShapeDtypeStruct((devices // NEAR, packed_rows, HD), BF16),
+        out_specs=at_hand,
         compiler_params=params(),
         name="pack",
-    )(prompt_state, prompt_keys, prompt_values, answer_keys, answer_values)
+    )(prompt_state, prompt_keys, prompt_values)
+    packed, near_keys = lax.optimization_barrier((packed, answer_keys))
+    near = pl.pallas_call(
+        join_kernel,
+        out_shape=jax.ShapeDtypeStruct((tokens, 2 * kv_width), BF16),
+        out_specs=at_hand,
+        compiler_params=params(),
+        name="join",
+    )(in_hbm(near_keys), in_hbm(answer_values))
     packed, raw = lax.optimization_barrier((packed, step_raw.T))
     lines = [list(range(first, devices, NEAR)) for first in range(NEAR)]
     line = lax.all_to_all(packed, "reader", 0, 0, axis_index_groups=lines, tiled=True)
@@ -456,7 +436,7 @@
     small = pl.CostEstimate(flops=0, bytes_accessed=0, transcendentals=0)
     by_group = lambda rows: pl.BlockSpec((rows, state), lambda g: (0, g))
     wide = pl.BlockSpec((tokens, width), lambda g: (0, g))
-    tail, level, column, start, weight = pl.pallas_call(
+    tail, level, column, start = pl.pallas_call(
         functools.partial(tail_kernel, per_group=per_group, channels=channels),
         grid=(groups,),
         in_specs=[
@@ -466,20 +446,14 @@
             wide,
             by_group(tokens),
         ],
-        out_specs=(
-            whole((columns + 2 * heads, state)),
-            whole((tokens, 2 * heads)),
-            whole((heads, tokens)),
-            whole((tokens, LANES)),
-            whole((tokens, 2 * heads)),
-        ),
+        out_specs=(at_hand, at_hand, at_hand, at_hand),
         out_shape=(
             jax.ShapeDtypeStruct((columns + 2 * heads, state), BF16),
             jax.ShapeDtypeStruct((tokens, 2 * heads), F32),
             jax.ShapeDtypeStruct((heads, tokens), F32),
             jax.ShapeDtypeStruct((tokens, LANES), F32),
-            jax.ShapeDtypeStruct((tokens, 2 * heads), F32),
         ),
+        scratch_shapes=[pltpu.VMEM((tokens, 2 * heads), F32)],
         compiler_params=params(),
         cost_estimate=small,
         name="tail",
@@ -489,15 +463,15 @@
         functools.partial(inner_kernel, **sizes),
         grid=(groups,),
         in_specs=[
-            whole((tokens, LANES)),
-            whole((tokens, 2 * heads)),
-            pl.BlockSpec((per_group, tokens), lambda g: (g, 0)),
+            at_hand,
+            at_hand,
+            at_hand,
             whole((1, heads)),
             wide,
             by_group(tokens),
             by_group(tokens),
         ],
-        out_specs=wide,
+        out_specs=at_hand,
         out_shape=jax.ShapeDtypeStruct((tokens, columns), BF16),
         compiler_params=params(),
         cost_estimate=small,
@@ -516,44 +490,42 @@
         ),
         grid=(kv_count,),
         in_specs=[
-            whole((tokens, LANES)),
+            at_hand,
             pl.BlockSpec((tokens, group_size * HD), lambda k: (0, k)),
             pl.BlockSpec((tokens, HD), lambda k: (0, k)),
             pl.BlockSpec((tokens, HD), lambda k: (0, k)),
-            pl.BlockSpec((tokens, HD), lambda k: (0, k)),
-            pl.BlockSpec((tokens, HD), lambda k: (0, kv_count + k)),
+            at_hand,
         ]
-        + [whole((devices // NEAR, packed_rows, HD))] * NEAR,
+        + [at_hand] * NEAR,
         out_specs=pl.BlockSpec((tokens, group_size * HD), lambda k: (0, k)),
         out_shape=jax.ShapeDtypeStruct(queries.shape, BF16),
         scratch_shapes=[pltpu.VMEM((tokens, tokens + LANES), F32)],
         compiler_params=params(),
         cost_estimate=small,
         name="attend",
-    )(start, queries, answer_keys, answer_values, prior, prior, *gathered)
+    )(start, queries, in_hbm(answer_keys), in_hbm(answer_values), prior, *gathered)
 
     inner, attention_out = lax.optimization_barrier((inner, attention_out))
     mixer_out = pl.pallas_call(
         functools.partial(final_kernel, state_rows=state_rows, **sizes),
         grid=(groups,),
         in_specs=[
-            whole((tokens, LANES)),
-            whole((tokens, 2 * heads)),
-            pl.BlockSpec((width, state), lambda g: (g, 0)),
-            pl.BlockSpec((2 * heads, state), lambda g: (columns // (2 * heads), 0)),
+            at_hand,
+            at_hand,
+            at_hand,
             by_group(tokens),
-            wide,
+            at_hand,
             wide,
             pl.BlockSpec((1, width), lambda g: (0, g)),
         ]
-        + [pl.BlockSpec((devices // groups // NEAR, packed_rows, HD), lambda g: (g, 0, 0))] * NEAR,
+        + [at_hand] * NEAR,
         out_specs=wide,
         out_shape=jax.ShapeDtypeStruct((tokens, columns), BF16),
         scratch_shapes=[pltpu.VMEM((tokens, width), F32)],
         compiler_params=params(),
         cost_estimate=small,
         name="final",
-    )(start, level, tail, tail, state_read, inner, gate_input, gain, *gathered)
+    )(start, level, tail, state_read, inner, gate_input, gain, *gathered)
     return (mixer_out, attention_out)
 
 

time: 63.6 us -> 48.4 us (0.76)
  Pallas kernels: 40.9 us -> 27.3 us
  waiting for transfers between devices: 10 us -> 8.44 us
    pallas_call x1 -> x2, Pallas kernels: 17.1 us -> 2.87 us  [the longest x1 1.81 us: local(): pl.pallas_call(pack_kernel, out_shape=jax.ShapeDtypeStruct((devices // NE...]
    ppermute x2, waiting for transfers between devices: 7.92 us -> 6.34 us  [shifted(): return lax.ppermute(value, axis, [(i, i + by) for i in range(length - by)])]
  transfers between devices with their start and end apart: 4 -> 4, of which waited for: 3 -> 3; matrix products, arithmetic and copies ran while one was open for 0% -> 0% of each run, Pallas kernels for 28% -> 40%
where the time goes in v7:
time: 48.4 us; the launch traced here: 47.9 us
  Pallas kernels  27.3 us (56%)
  starting transfers between devices  11.6 us (24%)
  waiting for transfers between devices  8.44 us (17%)
  between operations  0.66 us (1%)
    pallas_call x1, Pallas kernels, local(): pl.pallas_call(functools.partial(attend_kernel, state_rows=state_rows, pr...  6.49 us
    ppermute x2, waiting for transfers between devices, shifted(): return lax.ppermute(value, axis, [(i, i + by) for i in range(length - by)])  6.34 us
    all_to_all x1, starting transfers between devices, local(): lax.all_to_all(packed, 'reader', 0, 0, axis_index_groups=lines, tiled=True)  6.17 us
    pallas_call x1, Pallas kernels, local(): pl.pallas_call(functools.partial(final_kernel, state_rows=state_rows, **s...  6.14 us
    pallas_call x1, Pallas kernels, local(): pl.pallas_call(functools.partial(tail_kernel, per_group=per_group, channe...  6.09 us
    pallas_call x1, Pallas kernels, local(): pl.pallas_call(functools.partial(inner_kernel, **sizes), grid=(groups,),...  5.69 us
    ppermute x2, starting transfers between devices, shifted(): return lax.ppermute(value, axis, [(i, i + by) for i in range(length - by)])  5.38 us
    ppermute x1, waiting for transfers between devices, local(): lax.ppermute(line, 'reader', [(i, i ^ 1) for i in range(devices)])  2.1 us
  transfers between devices with their start and end apart: 4, of which 3 were waited for; matrix products, arithmetic and copies ran while one was open for 0% of the time, Pallas kernels for 40%

profile of v7, /device:TPU:18, one launch (start us, length us, event | category | flops | bytes accessed | tf_op | source)
XLA Modules:
  0.0 47.9 jit_solution(16580787885140534907)
XLA Ops:
  0.6 1.8 %pack.1 = bf16[8,320,128]{2,1,0:T(8,128)(2,1)} custom-call(f32[256,128]{1,0:T(8,128)} %state_ref.1, bf16[8,512]{1,0:T(8,128)(2,1)} %keys_ref.1, bf16[8,512]{1,0:T(8,128)(2,1)} %values_ref.2), custom_call_target="tpu_custom_call" | custom-call | tf_op jit(solution)/shard_map/pack/pallas_call | solution.py:415
  2.4 6.2 %all-to-all-start = ((bf16[8,320,128]{2,1,0:T(8,128)(2,1)}), bf16[8,320,128]{2,1,0:T(8,128)(2,1)S(1)}, u32[]{:S(2)}, u32[]{:S(2)}) async-start(bf16[8,320,128]{2,1,0:T(8,128)(2,1)} %pack.1), calls=%async_computation | async-start | bytes 1310720 | tf_op jit(solution)/shard_map/all_to_all | solution.py:432
  8.6 1.1 %join.1 = bf16[256,1024]{1,0:T(8,128)(2,1)S(1)} custom-call(bf16[256,512]{1,0:T(8,128)(2,1)} %key_ref.1, bf16[256,512]{1,0:T(8,128)(2,1)} %value_ref.1), custom_call_target="tpu_custom_call" | custom-call | tf_op jit(solution)/shard_map/join/pallas_call | solution.py:423
  9.7 1.9 %collective-permute-start.1 = (bf16[256,1024]{1,0:T(8,128)(2,1)S(1)}, bf16[256,1024]{1,0:T(8,128)(2,1)S(1)}, u32[]{:S(2)}, u32[]{:S(2)}) collective-permute-start(bf16[256,1024]{1,0:T(8,128)(2,1)S(1)} %join.1), channel_id=1, source_target_pairs={{0,1},{1,2},{2,3},{3,4},{4,5},{5,6},{6,7},{7,8},{8,9},{9,10},{10,1... | collective-permute-start | bytes 1572872 | tf_op jit(solution)/shard_map/ppermute | solution.py:362
  11.6 6.1 %tail.1 = (bf16[4224,128]{1,0:T(8,128)(2,1)}, f32[256,128]{1,0:T(8,128)S(1)}, f32[64,256]{1,0:T(8,128)S(1)}, f32[256,128]{1,0:T(8,128)S(1)}) custom-call(s32[1,32]{1,0:T(1,128)} %bitcast.7, f32[64,256]{1,0:T(8,128)} %bitcast.5, f32[1,64]{1,0:T(1,128)} %bitcast.8, bf16[256,4096]{1,0:T(8,128)(2,1)} %x_ref.3, bf16[256,512]{1,0:T(8,128)(2,1)} %write_ref.3), custom_call_target="tpu_custom_call" | custom-call | tf_op jit(solution)/shard_map/tail/pallas_call | solution.py:439
  17.7 3.5 %collective-permute-start = (bf16[4224,128]{1,0:T(8,128)(2,1)}, bf16[4224,128]{1,0:T(8,128)(2,1)}, u32[]{:S(2)}, u32[]{:S(2)}) collective-permute-start(bf16[4224,128]{1,0:T(8,128)(2,1)} %get-tuple-element.19), channel_id=1, source_target_pairs={{0,1},{1,2},{2,3},{3,4},{4,5},{5,6},{6,7},{7,8},{8,9},{9,10},{10,1... | collective-permute-start | bytes 3244040 | tf_op jit(solution)/shard_map/ppermute | solution.py:362
  21.2 5.7 %inner.1.inner_ref = bf16[256,4096]{1,0:T(8,128)(2,1)S(1)} custom-call(f32[256,128]{1,0:T(8,128)S(1)} %get-tuple-element.17.start_ref, f32[256,128]{1,0:T(8,128)S(1)} %get-tuple-element.18.level_ref, f32[64,256]{1,0:T(8,128)S(1)} %get-tuple-element.22.column_ref, f32[1,64]{1,0:T(1,128)} %bitcast.9, bf16[256,4096]{1,0:T(8,128)(2,1)} %x_ref.3, ...), custom_call_target="tpu_custom_call" | custom-call | tf_op jit(solution)/shard_map/inner/pallas_call | solution.py:462
  26.9 3.2 %collective-permute-done.1.prior_ref = bf16[256,1024]{1,0:T(8,128)(2,1)S(1)} collective-permute-done((bf16[256,1024]{1,0:T(8,128)(2,1)S(1)}, bf16[256,1024]{1,0:T(8,128)(2,1)S(1)}, u32[]{:S(2)}, u32[]{:S(2)}) %collective-permute-start.1) | collective-permute-done | bytes 524320 | tf_op jit(solution)/shard_map/ppermute | solution.py:362
  30.1 0.0 all-to-all-done.rest_0_
  30.1 0.0 collective-permute-start.2
  30.1 2.1 %collective-permute-done.2.rest_1_ = bf16[8,320,128]{2,1,0:T(8,128)(2,1)S(1)} collective-permute-done((bf16[8,320,128]{2,1,0:T(8,128)(2,1)S(1)}, bf16[8,320,128]{2,1,0:T(8,128)(2,1)S(1)}, u32[]{:S(2)}, u32[]{:S(2)}) %collective-permute-start.2) | collective-permute-done | bytes 655392 | tf_op jit(solution)/shard_map/ppermute | solution.py:481
  32.2 6.5 %attend.1 = bf16[256,2048]{1,0:T(8,128)(2,1)} custom-call(f32[256,128]{1,0:T(8,128)S(1)} %get-tuple-element.17.start_ref, bf16[256,2048]{1,0:T(8,128)(2,1)} %query_ref.1, bf16[256,512]{1,0:T(8,128)(2,1)} %key_ref.1, bf16[256,512]{1,0:T(8,128)(2,1)} %value_ref.1, bf16[256,1024]{1,0:T(8,128)(2,1)S(1)} %collective-permute-done.1.prior_ref, ...), custom_call_target="tpu_custom_call" | custom-call | tf_op jit(solution)/shard_map/attend/pallas_call | solution.py:484
  38.7 3.1 %collective-permute-done.tail_ref = bf16[4224,128]{1,0:T(8,128)(2,1)} collective-permute-done((bf16[4224,128]{1,0:T(8,128)(2,1)}, bf16[4224,128]{1,0:T(8,128)(2,1)}, u32[]{:S(2)}, u32[]{:S(2)}) %collective-permute-start) | collective-permute-done | bytes 1081376 | tf_op jit(solution)/shard_map/ppermute | solution.py:362
  41.8 6.1 %final.1 = bf16[256,4096]{1,0:T(8,128)(2,1)} custom-call(f32[256,128]{1,0:T(8,128)S(1)} %get-tuple-element.17.start_ref, f32[256,128]{1,0:T(8,128)S(1)} %get-tuple-element.18.level_ref, bf16[4224,128]{1,0:T(8,128)(2,1)} %collective-permute-done.tail_ref, bf16[256,512]{1,0:T(8,128)(2,1)} %read_ref.3, bf16[256,4096]{1,0:T(8,128)(2,1)S(1)} %inner.1.inner_ref, ...), custom_call_target="tpu_custom_call" | custom-call | tf_op jit(solution)/shard_map/final/pallas_call | solution.py:509
Async XLA Ops:
  2.4 27.7 %all-to-all-start = ((bf16[8,320,128]{2,1,0:T(8,128)(2,1)}), bf16[8,320,128]{2,1,0:T(8,128)(2,1)S(1)}, u32[]{:S(2)}, u32[]{:S(2)}) async-start(bf16[8,320,128]{2,1,0:T(8,128)(2,1)} %pack.1), calls=%async_computation | async-start | bytes 1310720 | tf_op jit(solution)/shard_map/all_to_all | solution.py:432
  9.7 20.4 %collective-permute-start.1 = (bf16[256,1024]{1,0:T(8,128)(2,1)S(1)}, bf16[256,1024]{1,0:T(8,128)(2,1)S(1)}, u32[]{:S(2)}, u32[]{:S(2)}) collective-permute-start(bf16[256,1024]{1,0:T(8,128)(2,1)S(1)} %join.1), channel_id=1, source_target_pairs={{0,1},{1,2},{2,3},{3,4},{4,5},{5,6},{6,7},{7,8},{8,9},{9,10},{10,1... | collective-permute-start | bytes 1572872 | tf_op jit(solution)/shard_map/ppermute | solution.py:362
  17.7 24.1 %collective-permute-start = (bf16[4224,128]{1,0:T(8,128)(2,1)}, bf16[4224,128]{1,0:T(8,128)(2,1)}, u32[]{:S(2)}, u32[]{:S(2)}) collective-permute-start(bf16[4224,128]{1,0:T(8,128)(2,1)} %get-tuple-element.19), channel_id=1, source_target_pairs={{0,1},{1,2},{2,3},{3,4},{4,5},{5,6},{6,7},{7,8},{8,9},{9,10},{10,1... | collective-permute-start | bytes 3244040 | tf_op jit(solution)/shard_map/ppermute | solution.py:362
  30.1 2.1 %collective-permute-start.2 = (bf16[8,320,128]{2,1,0:T(8,128)(2,1)S(1)}, bf16[8,320,128]{2,1,0:T(8,128)(2,1)S(1)}, u32[]{:S(2)}, u32[]{:S(2)}) collective-permute-start(bf16[8,320,128]{2,1,0:T(8,128)(2,1)S(1)} %all-to-all-done.rest_0_), channel_id=1, source_target_pairs={{0,1},{1,0},{2,3},{3,2},{4,5},{5,4},{6,7},{7,6},{8,9},{9,8},{10,11... | collective-permute-start | bytes 1966088 | tf_op jit(solution)/shard_map/ppermute | solution.py:481

commit v8 on v7

--- a/solution.py
+++ b/solution.py
@@ -114,8 +114,9 @@
     level_ref[...] = jnp.concatenate([level, level], axis=0).T
 
 
-def tail_part(group, at, weight_ref, x_ref, write_ref, tail_ref, per_group, channels):
-    tokens, width = x_ref.shape
+def tail_part(group, weight_ref, x_ref, write_ref, tail_ref, per_group, channels):
+    width = per_group * channels
+    begin = pl.multiple_of(group * width, width)
     weight = to_front(weight_ref[...], group * per_group)
     weighted = []
     for tile in range(width // LANES):
@@ -123,7 +124,7 @@
         x = x_ref[:, tile * LANES : (tile + 1) * LANES].astype(F32)
         weighted.append((x * scale).astype(BF16))
     state = dot(jnp.concatenate(weighted, axis=1), write_ref[...], 0, 0)
-    tail_ref[pl.ds(pl.multiple_of(at, width), width), :] = state.astype(BF16)
+    tail_ref[pl.ds(begin, width), :] = state.astype(BF16)
 
 
 def tail_kernel(
@@ -149,8 +150,7 @@
             lengths_ref, raw_ref, rate_ref, level_ref, column_ref, start_ref, weight_ref, tail_ref
         )
 
-    at = group * x_ref.shape[1]
-    tail_part(group, at, weight_ref, x_ref, write_ref, tail_ref, per_group, channels)
+    tail_part(group, weight_ref, x_ref, write_ref, tail_ref, per_group, channels)
 
 
 def inner_kernel(
@@ -169,7 +169,9 @@
 ):
     group = pl.program_id(0)
     tokens = x_ref.shape[0]
-    both = dot(read_ref[...], write_ref[...], 1, 1)
+    size = read_ref.shape[1] // (heads // per_group)
+    own = pl.ds(pl.multiple_of(group * size, size), size)
+    both = dot(read_ref[:, own], write_ref[:, own], 1, 1)
     square = (tokens, tokens)
     source = iota(square, 1)
     wide = jnp.concatenate([start_ref[...]] * (tokens // LANES), axis=1)
@@ -182,15 +184,14 @@
     skip = two_parts(jnp.broadcast_to(skip, (16, 2 * heads)), heads).astype(BF16)
     skip = dot(skip, expander(heads, group, per_group, channels))[:1, :]
     per_tile = LANES // channels
-    lane = iota((16, LANES), 1)
-    own = []
-    for part in range(per_tile):
-        mine = (lane >= part * channels) & (lane < (part + 1) * channels)
-        own.append(jnp.concatenate([jnp.where(mine, 1.0, 0.0).astype(BF16)] * (tokens // 16), axis=0))
+    lane = iota((tokens, LANES), 1)
     for tile in range(per_group // per_tile):
         at = slice(tile * LANES, (tile + 1) * LANES)
-        x = x_ref[:, at]
-        owned = [x * mine for mine in own]
+        x = x_ref[:, pl.ds(begin + at.start, LANES)].astype(F32)
+        owned = []
+        for part in range(per_tile):
+            mine = (lane >= part * channels) & (lane < (part + 1) * channels)
+            owned.append(jnp.where(mine, x, 0.0).astype(BF16))
         for block in range(tokens // LANES):
             rows = slice(block * LANES, (block + 1) * LANES)
             reach = (block + 1) * LANES
@@ -206,7 +207,7 @@
                 jnp.concatenate([value[:reach, :] for value in owned], axis=0),
             )
             out_ref[rows, pl.ds(begin + at.start, LANES)] = (
-                total + skip[:, at] * x[rows, :].astype(F32)
+                total + skip[:, at] * x[rows, :]
             ).astype(BF16)
 
 
@@ -224,8 +225,9 @@
     gathered, (out_ref, bias_ref) = rest[:-2], rest[-2:]
     head = pl.program_id(0)
     tokens = query_ref.shape[0]
+    own = pl.ds(pl.multiple_of(head * HD, HD), HD)
     prompt_count = len(gathered) * gathered[0].shape[0] * prompt_rows
-    queries = query_ref.shape[1] // HD
+    queries = query_ref.shape[1] // HD // kv_count
     scale = LOG2E / math.sqrt(HD)
     reach = tokens + LANES
 
@@ -254,8 +256,8 @@
         prior_ref[:, pl.ds(pl.multiple_of((which * kv_count + head) * HD, HD), HD)]
         for which in range(2)
     ]
-    near_keys = jnp.concatenate([prior[0], key_ref[...]], axis=0)
-    near_values = jnp.concatenate([prior[1], value_ref[...]], axis=0)
+    near_keys = jnp.concatenate([prior[0], key_ref[:, own]], axis=0)
+    near_values = jnp.concatenate([prior[1], value_ref[:, own]], axis=0)
     ones = jnp.ones((prompt_count + reach, LANES), BF16)
     for block in range(tokens // LANES):
         rows = slice(block * LANES, (block + 1) * LANES)
@@ -263,20 +265,16 @@
         keys = jnp.concatenate([prompt_keys, near_keys[window, :]], axis=0)
         values = jnp.concatenate([prompt_values, near_values[window, :]], axis=0)
         values = jnp.concatenate([values, ones], axis=1)
-        stacked = [query_ref[rows, query * HD : (query + 1) * HD] for query in range(queries)]
+        begin = pl.multiple_of(head * queries * HD, queries * HD)
+        stacked = [query_ref[rows, pl.ds(begin + query * HD, HD)] for query in range(queries)]
         scores = dot(jnp.concatenate(stacked, axis=0), keys, 1, 1)
         weights = []
         for query in range(queries):
             own = scores[query * LANES : (query + 1) * LANES, :]
-            far, near = own[:, :prompt_count], own[:, prompt_count:]
-            bias = bias_ref[rows, :]
-            top = jnp.maximum(
-                jnp.max(far, axis=1, keepdims=True), jnp.max(near + bias, axis=1, keepdims=True)
-            )
-            level = top * scale
-            far = jnp.exp2(far * scale - level)
-            near = jnp.exp2(near * scale + (bias - level))
-            weights.append(jnp.concatenate([far, near], axis=1).astype(BF16))
+            far, near = own[:, :prompt_count], own[:, prompt_count:] + bias_ref[rows, :]
+            own = jnp.concatenate([far, near], axis=1)
+            top = jnp.max(own, axis=1, keepdims=True)
+            weights.append(jnp.exp2((own - top) * scale).astype(BF16))
         summed = dot(jnp.concatenate(weights, axis=0), values)
         for query in range(queries):
             own = summed[query * LANES : (query + 1) * LANES, :]
@@ -299,12 +297,12 @@
 ):
     gathered, (out_ref, value_ref) = rest[:NEAR], rest[-2:]
     group = pl.program_id(0)
-    tokens, state = read_ref.shape
-    width = per_group * channels
+    tokens = read_ref.shape[0]
+    width, state = per_group * channels, tail_ref.shape[1]
 
     scale = to_front(jnp.exp(level_ref[...]), group * per_group)
     carried = start_ref[:, :state] < 0
-    read = read_ref[...].astype(F32)
+    read = read_ref[:, pl.ds(pl.multiple_of(group * state, state), state)].astype(F32)
     read = jnp.concatenate([jnp.where(carried, 0.0, read), jnp.where(carried, read, 0.0)], axis=1)
     read = read.astype(BF16)
     falls_at = heads * channels + pl.multiple_of(group * per_group, per_group)
@@ -340,7 +338,7 @@
                 for offset in range(0, WIDE, LANES)
             ]
             inflow = inflow * jnp.concatenate(falls, axis=1)
-            half = 0.5 * gate_ref[rows, at].astype(F32)
+            half = 0.5 * gate_ref[rows, pl.ds(begin + at.start, WIDE)].astype(F32)
             gated = inner_ref[rows, pl.ds(begin + at.start, WIDE)].astype(F32) + inflow
             gated = gated * (half + half * jnp.tanh(half))
             value_ref[rows, at] = gated
@@ -398,11 +396,8 @@
     kv_count = kv_width // HD
     devices = lax.axis_size("reader")
     in_hbm = lambda value: pltpu.with_memory_space_constraint(value, pltpu.MemorySpace.HBM)
-    mixer_input, gate_input, state_write, state_read = map(
-        in_hbm, (mixer_input, gate_input, state_write, state_read)
-    )
-    prompt_state, queries, prompt_keys, prompt_values = map(
-        in_hbm, (prompt_state, queries, prompt_keys, prompt_values)
+    prompt_state, prompt_keys, prompt_values = map(
+        in_hbm, (prompt_state, prompt_keys, prompt_values)
     )
     lengths, rate, skip, gain = map(
         lambda value: in_hbm(value.reshape(1, -1)),
@@ -434,7 +429,6 @@
     raw = in_hbm(raw)
 
     small = pl.CostEstimate(flops=0, bytes_accessed=0, transcendentals=0)
-    by_group = lambda rows: pl.BlockSpec((rows, state), lambda g: (0, g))
     wide = pl.BlockSpec((tokens, width), lambda g: (0, g))
     tail, level, column, start = pl.pallas_call(
         functools.partial(tail_kernel, per_group=per_group, channels=channels),
@@ -444,7 +438,7 @@
             whole(raw.shape),
             whole((1, heads)),
             wide,
-            by_group(tokens),
+            pl.BlockSpec((tokens, state), lambda g: (0, g)),
         ],
         out_specs=(at_hand, at_hand, at_hand, at_hand),
         out_shape=(
@@ -457,7 +451,7 @@
         compiler_params=params(),
         cost_estimate=small,
         name="tail",
-    )(lengths, raw, rate, mixer_input, state_write)
+    )(lengths, raw, rate, in_hbm(mixer_input), in_hbm(state_write))
     tail = shifted(tail, "reader", 1)
     inner = pl.pallas_call(
         functools.partial(inner_kernel, **sizes),
@@ -467,9 +461,9 @@
             at_hand,
             at_hand,
             whole((1, heads)),
-            wide,
-            by_group(tokens),
-            by_group(tokens),
+            at_hand,
+            at_hand,
+            at_hand,
         ],
         out_specs=at_hand,
         out_shape=jax.ShapeDtypeStruct((tokens, columns), BF16),
@@ -489,13 +483,7 @@
             kv_count=kv_count,
         ),
         grid=(kv_count,),
-        in_specs=[
-            at_hand,
-            pl.BlockSpec((tokens, group_size * HD), lambda k: (0, k)),
-            pl.BlockSpec((tokens, HD), lambda k: (0, k)),
-            pl.BlockSpec((tokens, HD), lambda k: (0, k)),
-            at_hand,
-        ]
+        in_specs=[at_hand] * 5
         + [at_hand] * NEAR,
         out_specs=pl.BlockSpec((tokens, group_size * HD), lambda k: (0, k)),
         out_shape=jax.ShapeDtypeStruct(queries.shape, BF16),
@@ -503,7 +491,7 @@
         compiler_params=params(),
         cost_estimate=small,
         name="attend",
-    )(start, queries, in_hbm(answer_keys), in_hbm(answer_values), prior, *gathered)
+    )(start, queries, answer_keys, answer_values, prior, *gathered)
 
     inner, attention_out = lax.optimization_barrier((inner, attention_out))
     mixer_out = pl.pallas_call(
@@ -513,9 +501,9 @@
             at_hand,
             at_hand,
             at_hand,
-            by_group(tokens),
-            at_hand,
-            wide,
+            at_hand,
+            at_hand,
+            at_hand,
             pl.BlockSpec((1, width), lambda g: (0, g)),
         ]
         + [at_hand] * NEAR,

time: 48.4 us -> 47.8 us (0.988)
  local copies, waits for them, and re-layouts: 0 us -> 4.4 us
  Pallas kernels: 27.3 us -> 24.7 us
  waiting for transfers between devices: 8.44 us -> 5.84 us
    unnamed x0 -> x24, local copies, waits for them, and re-layouts: none -> 4.4 us
    ppermute x2, waiting for transfers between devices: 6.34 us -> 3.75 us  [shifted(): return lax.ppermute(value, axis, [(i, i + by) for i in range(length - by)])]
    pallas_call x1, Pallas kernels: 6.49 us -> 5.25 us  [local(): pl.pallas_call(functools.partial(attend_kernel, state_rows=state_rows, pr...]
    pallas_call x1, Pallas kernels: 6.14 us -> 5.4 us  [local(): pl.pallas_call(functools.partial(final_kernel, state_rows=state_rows, **s...]
    pallas_call x1, Pallas kernels: 5.69 us -> 5.06 us  [local(): pl.pallas_call(functools.partial(inner_kernel, **sizes), grid=(groups,),...]
  transfers between devices with their start and end apart: 4 -> 4, of which waited for: 3 -> 3; matrix products, arithmetic and copies ran while one was open for 0% -> 0% of each run, Pallas kernels for 40% -> 37%
where the time goes in v8:
time: 47.8 us; the launch traced here: 47.3 us
  Pallas kernels  24.7 us (52%)
  starting transfers between devices  11.7 us (24%)
  waiting for transfers between devices  5.84 us (12%)
  local copies, waits for them, and re-layouts  4.4 us (9%)
  between operations  0.73 us (2%)
    all_to_all x1, starting transfers between devices, local(): lax.all_to_all(packed, 'reader', 0, 0, axis_index_groups=lines, tiled=True)  6.3 us
    pallas_call x1, Pallas kernels, local(): pl.pallas_call(functools.partial(tail_kernel, per_group=per_group, channe...  6.05 us
    pallas_call x1, Pallas kernels, local(): pl.pallas_call(functools.partial(final_kernel, state_rows=state_rows, **s...  5.4 us
    ppermute x2, starting transfers between devices, shifted(): return lax.ppermute(value, axis, [(i, i + by) for i in range(length - by)])  5.39 us
    pallas_call x1, Pallas kernels, local(): pl.pallas_call(functools.partial(attend_kernel, state_rows=state_rows, pr...  5.25 us
    pallas_call x1, Pallas kernels, local(): pl.pallas_call(functools.partial(inner_kernel, **sizes), grid=(groups,),...  5.06 us
    unnamed x24, local copies, waits for them, and re-layouts  4.4 us
    ppermute x2, waiting for transfers between devices, shifted(): return lax.ppermute(value, axis, [(i, i + by) for i in range(length - by)])  3.75 us
  transfers between devices with their start and end apart: 4, of which 3 were waited for; matrix products, arithmetic and copies ran while one was open for 0% of the time, Pallas kernels for 37%

profile of v8, /device:TPU:18, one launch (start us, length us, event | category | flops | bytes accessed | tf_op | source)
XLA Modules:
  0.0 47.3 jit_solution(10115254179485977952)
XLA Ops:
  0.6 1.8 %pack.1 = bf16[8,320,128]{2,1,0:T(8,128)(2,1)} custom-call(f32[256,128]{1,0:T(8,128)} %state_ref.1, bf16[8,512]{1,0:T(8,128)(2,1)} %keys_ref.1, bf16[8,512]{1,0:T(8,128)(2,1)} %values_ref.2), custom_call_target="tpu_custom_call" | custom-call | tf_op jit(solution)/shard_map/pack/pallas_call | solution.py:410
  2.4 0.0 copy-start
  2.4 6.3 %all-to-all-start = ((bf16[8,320,128]{2,1,0:T(8,128)(2,1)}), bf16[8,320,128]{2,1,0:T(8,128)(2,1)S(1)}, u32[]{:S(2)}, u32[]{:S(2)}) async-start(bf16[8,320,128]{2,1,0:T(8,128)(2,1)} %pack.1), calls=%async_computation | async-start | bytes 1310720 | tf_op jit(solution)/shard_map/all_to_all | solution.py:427
  8.7 0.0 copy-start.7
  8.7 0.0 copy-start.8
  8.7 1.1 %join.1 = bf16[256,1024]{1,0:T(8,128)(2,1)S(1)} custom-call(bf16[256,512]{1,0:T(8,128)(2,1)} %key_ref.1, bf16[256,512]{1,0:T(8,128)(2,1)} %value_ref.1), custom_call_target="tpu_custom_call" | custom-call | tf_op jit(solution)/shard_map/join/pallas_call | solution.py:418
  9.9 1.9 %collective-permute-start.1 = (bf16[256,1024]{1,0:T(8,128)(2,1)S(1)}, bf16[256,1024]{1,0:T(8,128)(2,1)S(1)}, u32[]{:S(2)}, u32[]{:S(2)}) collective-permute-start(bf16[256,1024]{1,0:T(8,128)(2,1)S(1)} %join.1), channel_id=1, source_target_pairs={{0,1},{1,2},{2,3},{3,4},{4,5},{5,6},{6,7},{7,8},{8,9},{9,10},{10,1... | collective-permute-start | bytes 1572872 | tf_op jit(solution)/shard_map/ppermute | solution.py:360
  11.8 6.0 %tail.1 = (bf16[4224,128]{1,0:T(8,128)(2,1)}, f32[256,128]{1,0:T(8,128)S(1)}, f32[64,256]{1,0:T(8,128)S(1)}, f32[256,128]{1,0:T(8,128)S(1)}) custom-call(s32[1,32]{1,0:T(1,128)} %bitcast.7, f32[64,256]{1,0:T(8,128)} %bitcast.5, f32[1,64]{1,0:T(1,128)} %bitcast.8, bf16[256,4096]{1,0:T(8,128)(2,1)} %x_ref.3, bf16[256,512]{1,0:T(8,128)(2,1)} %write_ref.3), custom_call_target="tpu_custom_call" | custom-call | tf_op jit(solution)/shard_map/tail/pallas_call | solution.py:433
  17.8 3.5 %collective-permute-start = (bf16[4224,128]{1,0:T(8,128)(2,1)}, bf16[4224,128]{1,0:T(8,128)(2,1)}, u32[]{:S(2)}, u32[]{:S(2)}) collective-permute-start(bf16[4224,128]{1,0:T(8,128)(2,1)} %get-tuple-element.19), channel_id=1, source_target_pairs={{0,1},{1,2},{2,3},{3,4},{4,5},{5,6},{6,7},{7,8},{8,9},{9,10},{10,1... | collective-permute-start | bytes 3244040 | tf_op jit(solution)/shard_map/ppermute | solution.py:360
  21.3 0.0 copy-done
  21.3 0.0 copy-done.7
  21.3 0.0 copy-done.8
  21.4 0.0 copy-start.4
  21.4 0.0 copy-start.5
  21.4 5.1 %inner.1.inner_ref = bf16[256,4096]{1,0:T(8,128)(2,1)S(1)} custom-call(f32[256,128]{1,0:T(8,128)S(1)} %get-tuple-element.17.start_ref, f32[256,128]{1,0:T(8,128)S(1)} %get-tuple-element.18.level_ref, f32[64,256]{1,0:T(8,128)S(1)} %get-tuple-element.22.column_ref, f32[1,64]{1,0:T(1,128)} %bitcast.9, bf16[256,4096]{1,0:T(8,128)(2,1)S(1)} %copy-done, ...), custom_call_target="tpu_custom_call" | custom-call | tf_op jit(solution)/shard_map/inner/pallas_call | solution.py:456
  26.4 0.0 copy-start.1
  26.5 1.3 %copy-done.1 = bf16[256,4096]{1,0:T(8,128)(2,1)} copy-done((bf16[256,4096]{1,0:T(8,128)(2,1)}, bf16[256,4096]{1,0:T(8,128)(2,1)S(1)}, u32[]{:S(2)}) %copy-start.1) | copy-done | bytes 2097176
  27.8 2.5 %collective-permute-done.1.prior_ref = bf16[256,1024]{1,0:T(8,128)(2,1)S(1)} collective-permute-done((bf16[256,1024]{1,0:T(8,128)(2,1)S(1)}, bf16[256,1024]{1,0:T(8,128)(2,1)S(1)}, u32[]{:S(2)}, u32[]{:S(2)}) %collective-permute-start.1) | collective-permute-done | bytes 524320 | tf_op jit(solution)/shard_map/ppermute | solution.py:360
  30.2 0.0 copy-start.10
  30.2 0.8 %copy-done.10 = bf16[256,1024]{1,0:T(8,128)(2,1)} copy-done((bf16[256,1024]{1,0:T(8,128)(2,1)}, bf16[256,1024]{1,0:T(8,128)(2,1)S(1)}, u32[]{:S(2)}) %copy-start.10) | copy-done | bytes 524312
  31.0 0.0 copy-start.2
  31.0 0.0 all-to-all-done.rest_0_
  31.0 0.0 copy-start.3
  31.0 0.0 collective-permute-start.2
  31.0 2.1 %collective-permute-done.2.rest_1_ = bf16[8,320,128]{2,1,0:T(8,128)(2,1)S(1)} collective-permute-done((bf16[8,320,128]{2,1,0:T(8,128)(2,1)S(1)}, bf16[8,320,128]{2,1,0:T(8,128)(2,1)S(1)}, u32[]{:S(2)}, u32[]{:S(2)}) %collective-permute-start.2) | collective-permute-done | bytes 655392 | tf_op jit(solution)/shard_map/ppermute | solution.py:475
  33.1 0.0 copy-done.4
  33.1 0.0 copy-done.5
  33.1 0.0 copy-start.6
  33.1 1.2 %copy-done.6 = bf16[256,2048]{1,0:T(8,128)(2,1)S(1)} copy-done((bf16[256,2048]{1,0:T(8,128)(2,1)S(1)}, bf16[256,2048]{1,0:T(8,128)(2,1)}, u32[]{:S(2)}) %copy-start.6) | copy-done | bytes 1048600
  34.4 0.0 copy-start.11
  34.4 1.0 %copy-done.11 = bf16[256,1024]{1,0:T(8,128)(2,1)S(1)} copy-done((bf16[256,1024]{1,0:T(8,128)(2,1)S(1)}, bf16[256,1024]{1,0:T(8,128)(2,1)}, u32[]{:S(2)}) %copy-start.11) | copy-done | bytes 524312
  35.4 0.0 copy-start.9
  35.4 5.2 %attend.1 = bf16[256,2048]{1,0:T(8,128)(2,1)} custom-call(f32[256,128]{1,0:T(8,128)S(1)} %get-tuple-element.17.start_ref, bf16[256,2048]{1,0:T(8,128)(2,1)S(1)} %copy-done.6, bf16[256,512]{1,0:T(8,128)(2,1)S(1)} %copy-done.4, bf16[256,512]{1,0:T(8,128)(2,1)S(1)} %copy-done.5, bf16[256,1024]{1,0:T(8,128)(2,1)S(1)} %copy-done.11, ...), custom_call_target="tpu_custom_call" | custom-call | tf_op jit(solution)/shard_map/attend/pallas_call | solution.py:478
  40.7 1.3 %collective-permute-done.tail_ref = bf16[4224,128]{1,0:T(8,128)(2,1)} collective-permute-done((bf16[4224,128]{1,0:T(8,128)(2,1)}, bf16[4224,128]{1,0:T(8,128)(2,1)}, u32[]{:S(2)}, u32[]{:S(2)}) %collective-permute-start) | collective-permute-done | bytes 1081376 | tf_op jit(solution)/shard_map/ppermute | solution.py:360
  41.9 0.0 copy-done.2
  41.9 0.0 copy-done.3
  41.9 0.0 copy-done.9
  41.9 5.4 %final.1 = bf16[256,4096]{1,0:T(8,128)(2,1)} custom-call(f32[256,128]{1,0:T(8,128)S(1)} %get-tuple-element.17.start_ref, f32[256,128]{1,0:T(8,128)S(1)} %get-tuple-element.18.level_ref, bf16[4224,128]{1,0:T(8,128)(2,1)} %collective-permute-done.tail_ref, bf16[256,512]{1,0:T(8,128)(2,1)S(1)} %copy-done.9, bf16[256,4096]{1,0:T(8,128)(2,1)S(1)} %copy-done.2, ...), custom_call_target="tpu_custom_call" | custom-call | tf_op jit(solution)/shard_map/final/pallas_call | solution.py:497
Async XLA Ops:
  2.4 18.9 %copy-start = (bf16[256,4096]{1,0:T(8,128)(2,1)S(1)}, bf16[256,4096]{1,0:T(8,128)(2,1)}, u32[]{:S(2)}) copy-start(bf16[256,4096]{1,0:T(8,128)(2,1)} %x_ref.3) | copy-start | bytes 6291460
  2.4 28.6 %all-to-all-start = ((bf16[8,320,128]{2,1,0:T(8,128)(2,1)}), bf16[8,320,128]{2,1,0:T(8,128)(2,1)S(1)}, u32[]{:S(2)}, u32[]{:S(2)}) async-start(bf16[8,320,128]{2,1,0:T(8,128)(2,1)} %pack.1), calls=%async_computation | async-start | bytes 1310720 | tf_op jit(solution)/shard_map/all_to_all | solution.py:427
  8.7 12.6 %copy-start.7 = (bf16[256,512]{1,0:T(8,128)(2,1)S(1)}, bf16[256,512]{1,0:T(8,128)(2,1)}, u32[]{:S(2)}) copy-start(bf16[256,512]{1,0:T(8,128)(2,1)} %write_ref.3) | copy-start | bytes 786436
  8.7 12.6 %copy-start.8 = (bf16[256,512]{1,0:T(8,128)(2,1)S(1)}, bf16[256,512]{1,0:T(8,128)(2,1)}, u32[]{:S(2)}) copy-start(bf16[256,512]{1,0:T(8,128)(2,1)} %read_ref.3) | copy-start | bytes 786436
  9.9 20.4 %collective-permute-start.1 = (bf16[256,1024]{1,0:T(8,128)(2,1)S(1)}, bf16[256,1024]{1,0:T(8,128)(2,1)S(1)}, u32[]{:S(2)}, u32[]{:S(2)}) collective-permute-start(bf16[256,1024]{1,0:T(8,128)(2,1)S(1)} %join.1), channel_id=1, source_target_pairs={{0,1},{1,2},{2,3},{3,4},{4,5},{5,6},{6,7},{7,8},{8,9},{9,10},{10,1... | collective-permute-start | bytes 1572872 | tf_op jit(solution)/shard_map/ppermute | solution.py:360
  17.8 24.1 %collective-permute-start = (bf16[4224,128]{1,0:T(8,128)(2,1)}, bf16[4224,128]{1,0:T(8,128)(2,1)}, u32[]{:S(2)}, u32[]{:S(2)}) collective-permute-start(bf16[4224,128]{1,0:T(8,128)(2,1)} %get-tuple-element.19), channel_id=1, source_target_pairs={{0,1},{1,2},{2,3},{3,4},{4,5},{5,6},{6,7},{7,8},{8,9},{9,10},{10,1... | collective-permute-start | bytes 3244040 | tf_op jit(solution)/shard_map/ppermute | solution.py:360
  21.4 11.8 %copy-start.4 = (bf16[256,512]{1,0:T(8,128)(2,1)S(1)}, bf16[256,512]{1,0:T(8,128)(2,1)}, u32[]{:S(2)}) copy-start(bf16[256,512]{1,0:T(8,128)(2,1)} %key_ref.1) | copy-start | bytes 786436
  21.4 11.8 %copy-start.5 = (bf16[256,512]{1,0:T(8,128)(2,1)S(1)}, bf16[256,512]{1,0:T(8,128)(2,1)}, u32[]{:S(2)}) copy-start(bf16[256,512]{1,0:T(8,128)(2,1)} %value_ref.1) | copy-start | bytes 786436
  26.4 1.3 %copy-start.1 = (bf16[256,4096]{1,0:T(8,128)(2,1)}, bf16[256,4096]{1,0:T(8,128)(2,1)S(1)}, u32[]{:S(2)}) copy-start(bf16[256,4096]{1,0:T(8,128)(2,1)S(1)} %inner.1.inner_ref) | copy-start | bytes 6291460
  30.2 0.8 %copy-start.10 = (bf16[256,1024]{1,0:T(8,128)(2,1)}, bf16[256,1024]{1,0:T(8,128)(2,1)S(1)}, u32[]{:S(2)}) copy-start(bf16[256,1024]{1,0:T(8,128)(2,1)S(1)} %collective-permute-done.1.prior_ref) | copy-start | bytes 1572868
  31.0 10.9 %copy-start.2 = (bf16[256,4096]{1,0:T(8,128)(2,1)S(1)}, bf16[256,4096]{1,0:T(8,128)(2,1)}, u32[]{:S(2)}) copy-start(bf16[256,4096]{1,0:T(8,128)(2,1)} %copy-done.1) | copy-start | bytes 6291460
  31.0 10.9 %copy-start.3 = (bf16[256,4096]{1,0:T(8,128)(2,1)S(1)}, bf16[256,4096]{1,0:T(8,128)(2,1)}, u32[]{:S(2)}) copy-start(bf16[256,4096]{1,0:T(8,128)(2,1)} %gate_ref.1) | copy-start | bytes 6291460
  31.0 2.1 %collective-permute-start.2 = (bf16[8,320,128]{2,1,0:T(8,128)(2,1)S(1)}, bf16[8,320,128]{2,1,0:T(8,128)(2,1)S(1)}, u32[]{:S(2)}, u32[]{:S(2)}) collective-permute-start(bf16[8,320,128]{2,1,0:T(8,128)(2,1)S(1)} %all-to-all-done.rest_0_), channel_id=1, source_target_pairs={{0,1},{1,0},{2,3},{3,2},{4,5},{5,4},{6,7},{7,6},{8,9},{9,8},{10,11... | collective-permute-start | bytes 1966088 | tf_op jit(solution)/shard_map/ppermute | solution.py:475
  33.1 1.2 %copy-start.6 = (bf16[256,2048]{1,0:T(8,128)(2,1)S(1)}, bf16[256,2048]{1,0:T(8,128)(2,1)}, u32[]{:S(2)}) copy-start(bf16[256,2048]{1,0:T(8,128)(2,1)} %query_ref.1) | copy-start | bytes 3145732
  34.4 1.0 %copy-start.11 = (bf16[256,1024]{1,0:T(8,128)(2,1)S(1)}, bf16[256,1024]{1,0:T(8,128)(2,1)}, u32[]{:S(2)}) copy-start(bf16[256,1024]{1,0:T(8,128)(2,1)} %copy-done.10) | copy-start | bytes 1572868
  35.4 6.5 %copy-start.9 = (bf16[256,512]{1,0:T(8,128)(2,1)S(1)}, bf16[256,512]{1,0:T(8,128)(2,1)}, u32[]{:S(2)}) copy-start(bf16[256,512]{1,0:T(8,128)(2,1)} %read_ref.3) | copy-start | bytes 786436

commit v9 on v8

--- a/solution.py
+++ b/solution.py
@@ -162,6 +162,7 @@
     write_ref,
     read_ref,
     out_ref,
+    mark_ref,
     *,
     heads,
     per_group,
@@ -169,6 +170,7 @@
 ):
     group = pl.program_id(0)
     tokens = x_ref.shape[0]
+    mark_ref[...] = jnp.zeros_like(mark_ref)
     size = read_ref.shape[1] // (heads // per_group)
     own = pl.ds(pl.multiple_of(group * size, size), size)
     both = dot(read_ref[:, own], write_ref[:, own], 1, 1)
@@ -222,12 +224,13 @@
     prompt_rows,
     kv_count,
 ):
-    gathered, (out_ref, bias_ref) = rest[:-2], rest[-2:]
+    gathered, (out_ref, mark_ref, bias_ref) = rest[:NEAR], rest[-3:]
     head = pl.program_id(0)
+    mark_ref[...] = jnp.zeros_like(mark_ref)
     tokens = query_ref.shape[0]
     own = pl.ds(pl.multiple_of(head * HD, HD), HD)
     prompt_count = len(gathered) * gathered[0].shape[0] * prompt_rows
-    queries = query_ref.shape[1] // HD // kv_count
+    queries = query_ref.shape[1] // HD
     scale = LOG2E / math.sqrt(HD)
     reach = tokens + LANES
 
@@ -265,8 +268,7 @@
         keys = jnp.concatenate([prompt_keys, near_keys[window, :]], axis=0)
         values = jnp.concatenate([prompt_values, near_values[window, :]], axis=0)
         values = jnp.concatenate([values, ones], axis=1)
-        begin = pl.multiple_of(head * queries * HD, queries * HD)
-        stacked = [query_ref[rows, pl.ds(begin + query * HD, HD)] for query in range(queries)]
+        stacked = [query_ref[rows, query * HD : (query + 1) * HD] for query in range(queries)]
         scores = dot(jnp.concatenate(stacked, axis=0), keys, 1, 1)
         weights = []
         for query in range(queries):
@@ -453,7 +455,7 @@
         name="tail",
     )(lengths, raw, rate, in_hbm(mixer_input), in_hbm(state_write))
     tail = shifted(tail, "reader", 1)
-    inner = pl.pallas_call(
+    inner, mark = pl.pallas_call(
         functools.partial(inner_kernel, **sizes),
         grid=(groups,),
         in_specs=[
@@ -465,17 +467,20 @@
             at_hand,
             at_hand,
         ],
-        out_specs=at_hand,
-        out_shape=jax.ShapeDtypeStruct((tokens, columns), BF16),
+        out_specs=(at_hand, at_hand),
+        out_shape=(
+            jax.ShapeDtypeStruct((tokens, columns), BF16),
+            jax.ShapeDtypeStruct((8, LANES), F32),
+        ),
         compiler_params=params(),
         cost_estimate=small,
         name="inner",
     )(start, level, column, skip, mixer_input, state_write, state_read)
-    prior, line, inner = lax.optimization_barrier((prior, line, inner))
+    prior, line, mark = lax.optimization_barrier((prior, line, mark))
     gathered = (line, lax.ppermute(line, "reader", [(i, i ^ 1) for i in range(devices)]))
 
     group_size = queries.shape[1] // kv_width
-    attention_out = pl.pallas_call(
+    attention_out, mark = pl.pallas_call(
         functools.partial(
             attend_kernel,
             state_rows=state_rows,
@@ -483,17 +488,26 @@
             kv_count=kv_count,
         ),
         grid=(kv_count,),
-        in_specs=[at_hand] * 5
-        + [at_hand] * NEAR,
-        out_specs=pl.BlockSpec((tokens, group_size * HD), lambda k: (0, k)),
-        out_shape=jax.ShapeDtypeStruct(queries.shape, BF16),
+        in_specs=[
+            at_hand,
+            pl.BlockSpec((tokens, group_size * HD), lambda k: (0, k)),
+            at_hand,
+            at_hand,
+            at_hand,
+        ]
+        + [at_hand] * NEAR
+        + [pl.BlockSpec(memory_space=pl.ANY)],
+        out_specs=(pl.BlockSpec((tokens, group_size * HD), lambda k: (0, k)), at_hand),
+        out_shape=(
+            jax.ShapeDtypeStruct(queries.shape, BF16),
+            jax.ShapeDtypeStruct((8, LANES), F32),
+        ),
         scratch_shapes=[pltpu.VMEM((tokens, tokens + LANES), F32)],
         compiler_params=params(),
         cost_estimate=small,
         name="attend",
-    )(start, queries, answer_keys, answer_values, prior, *gathered)
-
-    inner, attention_out = lax.optimization_barrier((inner, attention_out))
+    )(start, in_hbm(queries), answer_keys, answer_values, prior, *gathered, mark)
+
     mixer_out = pl.pallas_call(
         functools.partial(final_kernel, state_rows=state_rows, **sizes),
         grid=(groups,),
@@ -506,14 +520,15 @@
             at_hand,
             pl.BlockSpec((1, width), lambda g: (0, g)),
         ]
-        + [at_hand] * NEAR,
+        + [at_hand] * NEAR
+        + [pl.BlockSpec(memory_space=pl.ANY)],
         out_specs=wide,
         out_shape=jax.ShapeDtypeStruct((tokens, columns), BF16),
         scratch_shapes=[pltpu.VMEM((tokens, width), F32)],
         compiler_params=params(),
         cost_estimate=small,
         name="final",
-    )(start, level, tail, state_read, inner, gate_input, gain, *gathered)
+    )(start, level, tail, state_read, inner, gate_input, gain, *gathered, mark)
     return (mixer_out, attention_out)
 
 

time: 47.8 us -> 50.2 us (1.050)
  local copies, waits for them, and re-layouts: 4.4 us -> 6.64 us
  waiting for transfers between devices: 5.84 us -> 4.71 us
  Pallas kernels: 24.7 us -> 25.5 us
    unnamed x24 -> x20, local copies, waits for them, and re-layouts: 4.4 us -> 6.64 us
    ppermute x2, waiting for transfers between devices: 3.75 us -> 2.61 us  [shifted(): return lax.ppermute(value, axis, [(i, i + by) for i in range(length - by)])]
    pallas_call x1, Pallas kernels: 5.25 us -> 6.17 us  [local(): pl.pallas_call(functools.partial(attend_kernel, state_rows=state_rows, pr...]
  transfers between devices with their start and end apart: 4 -> 4, of which waited for: 3 -> 2; matrix products, arithmetic and copies ran while one was open for 0% -> 0% of each run, Pallas kernels for 37% -> 37%
where the time goes in v9:
time: 50.2 us; the launch traced here: 49.3 us
  Pallas kernels  25.5 us (51%)
  starting transfers between devices  11.8 us (24%)
  local copies, waits for them, and re-layouts  6.64 us (13%)
  waiting for transfers between devices  4.71 us (9%)
  between operations  0.71 us (1%)
    unnamed x20, local copies, waits for them, and re-layouts  6.64 us
    all_to_all x1, starting transfers between devices, local(): lax.all_to_all(packed, 'reader', 0, 0, axis_index_groups=lines, tiled=True)  6.43 us
    pallas_call x1, Pallas kernels, local(): pl.pallas_call(functools.partial(attend_kernel, state_rows=state_rows, pr...  6.17 us
    pallas_call x1, Pallas kernels, local(): pl.pallas_call(functools.partial(tail_kernel, per_group=per_group, channe...  6.05 us
    ppermute x2, starting transfers between devices, shifted(): return lax.ppermute(value, axis, [(i, i + by) for i in range(length - by)])  5.38 us
    pallas_call x1, Pallas kernels, local(): pl.pallas_call(functools.partial(final_kernel, state_rows=state_rows, **s...  5.36 us
    pallas_call x1, Pallas kernels, local(): pl.pallas_call(functools.partial(inner_kernel, **sizes), grid=(groups,),...  5.01 us
    ppermute x2, waiting for transfers between devices, shifted(): return lax.ppermute(value, axis, [(i, i + by) for i in range(length - by)])  2.61 us
  transfers between devices with their start and end apart: 4, of which 2 were waited for; matrix products, arithmetic and copies ran while one was open for 0% of the time, Pallas kernels for 37%

profile of v9, /device:TPU:18, one launch (start us, length us, event | category | flops | bytes accessed | tf_op | source)
XLA Modules:
  0.0 49.3 jit_solution(2994582834131990150)
XLA Ops:
  0.6 1.8 %pack.1 = bf16[8,320,128]{2,1,0:T(8,128)(2,1)} custom-call(f32[256,128]{1,0:T(8,128)} %state_ref.1, bf16[8,512]{1,0:T(8,128)(2,1)} %keys_ref.1, bf16[8,512]{1,0:T(8,128)(2,1)} %values_ref.2), custom_call_target="tpu_custom_call" | custom-call | tf_op jit(solution)/shard_map/pack/pallas_call | solution.py:412
  2.4 0.0 copy-start
  2.4 0.0 copy-start.4
  2.4 0.0 copy-start.5
  2.4 6.4 %all-to-all-start = ((bf16[8,320,128]{2,1,0:T(8,128)(2,1)}), bf16[8,320,128]{2,1,0:T(8,128)(2,1)S(1)}, u32[]{:S(2)}, u32[]{:S(2)}) async-start(bf16[8,320,128]{2,1,0:T(8,128)(2,1)} %pack.1), calls=%async_computation | async-start | bytes 1310720 | tf_op jit(solution)/shard_map/all_to_all | solution.py:429
  8.9 1.1 %join.1 = bf16[256,1024]{1,0:T(8,128)(2,1)S(1)} custom-call(bf16[256,512]{1,0:T(8,128)(2,1)} %key_ref.1, bf16[256,512]{1,0:T(8,128)(2,1)} %value_ref.1), custom_call_target="tpu_custom_call" | custom-call | tf_op jit(solution)/shard_map/join/pallas_call | solution.py:420
  9.9 1.9 %collective-permute-start.1 = (bf16[256,1024]{1,0:T(8,128)(2,1)S(1)}, bf16[256,1024]{1,0:T(8,128)(2,1)S(1)}, u32[]{:S(2)}, u32[]{:S(2)}) collective-permute-start(bf16[256,1024]{1,0:T(8,128)(2,1)S(1)} %join.1), channel_id=1, source_target_pairs={{0,1},{1,2},{2,3},{3,4},{4,5},{5,6},{6,7},{7,8},{8,9},{9,10},{10,1... | collective-permute-start | bytes 1572872 | tf_op jit(solution)/shard_map/ppermute | solution.py:362
  11.9 6.0 %tail.1 = (bf16[4224,128]{1,0:T(8,128)(2,1)}, f32[256,128]{1,0:T(8,128)S(1)}, f32[64,256]{1,0:T(8,128)S(1)}, f32[256,128]{1,0:T(8,128)S(1)}) custom-call(s32[1,32]{1,0:T(1,128)} %bitcast.7, f32[64,256]{1,0:T(8,128)} %bitcast.5, f32[1,64]{1,0:T(1,128)} %bitcast.8, bf16[256,4096]{1,0:T(8,128)(2,1)} %x_ref.3, bf16[256,512]{1,0:T(8,128)(2,1)} %write_ref.3), custom_call_target="tpu_custom_call" | custom-call | tf_op jit(solution)/shard_map/tail/pallas_call | solution.py:435
  17.9 3.5 %collective-permute-start = (bf16[4224,128]{1,0:T(8,128)(2,1)}, bf16[4224,128]{1,0:T(8,128)(2,1)}, u32[]{:S(2)}, u32[]{:S(2)}) collective-permute-start(bf16[4224,128]{1,0:T(8,128)(2,1)} %get-tuple-element.21), channel_id=1, source_target_pairs={{0,1},{1,2},{2,3},{3,4},{4,5},{5,6},{6,7},{7,8},{8,9},{9,10},{10,1... | collective-permute-start | bytes 3244040 | tf_op jit(solution)/shard_map/ppermute | solution.py:362
  21.4 0.0 copy-done
  21.4 0.0 copy-done.4
  21.4 0.0 copy-done.5
  21.4 5.0 %inner.1 = (bf16[256,4096]{1,0:T(8,128)(2,1)S(1)}, f32[8,128]{1,0:T(8,128)S(1)}) custom-call(f32[256,128]{1,0:T(8,128)S(1)} %get-tuple-element.19.start_ref, f32[256,128]{1,0:T(8,128)S(1)} %get-tuple-element.20.level_ref, f32[64,256]{1,0:T(8,128)S(1)} %get-tuple-element.22.column_ref, f32[1,64]{1,0:T(1,128)} %bitcast.9, bf16[256,4096]{1,0:T(8,128)(2,1)S(1)} %copy-done, ...), custom_call_target="tpu_custom_call" | custom-call | tf_op jit(solution)/shard_map/inner/pallas_call | solution.py:458
  26.4 0.0 copy-start.2
  26.5 1.3 %copy-done.2 = bf16[256,4096]{1,0:T(8,128)(2,1)} copy-done((bf16[256,4096]{1,0:T(8,128)(2,1)}, bf16[256,4096]{1,0:T(8,128)(2,1)S(1)}, u32[]{:S(2)}) %copy-start.2) | copy-done | bytes 2097176
  27.8 0.0 copy-start.1
  27.8 2.6 %collective-permute-done.1.prior_ref = bf16[256,1024]{1,0:T(8,128)(2,1)S(1)} collective-permute-done((bf16[256,1024]{1,0:T(8,128)(2,1)S(1)}, bf16[256,1024]{1,0:T(8,128)(2,1)S(1)}, u32[]{:S(2)}, u32[]{:S(2)}) %collective-permute-start.1) | collective-permute-done | bytes 524320 | tf_op jit(solution)/shard_map/ppermute | solution.py:362
  30.4 0.0 copy-start.8
  30.4 0.8 %copy-done.8 = bf16[256,1024]{1,0:T(8,128)(2,1)} copy-done((bf16[256,1024]{1,0:T(8,128)(2,1)}, bf16[256,1024]{1,0:T(8,128)(2,1)S(1)}, u32[]{:S(2)}) %copy-start.8) | copy-done | bytes 524312
  31.2 0.0 all-to-all-done.rest_0_
  31.2 0.0 collective-permute-start.2
  31.2 2.1 %collective-permute-done.2.rest_1_ = bf16[8,320,128]{2,1,0:T(8,128)(2,1)S(1)} collective-permute-done((bf16[8,320,128]{2,1,0:T(8,128)(2,1)S(1)}, bf16[8,320,128]{2,1,0:T(8,128)(2,1)S(1)}, u32[]{:S(2)}, u32[]{:S(2)}) %collective-permute-start.2) | collective-permute-done | bytes 655392 | tf_op jit(solution)/shard_map/ppermute | solution.py:480
  33.3 0.0 copy-start.6
  33.3 0.9 %copy-done.6 = bf16[256,512]{1,0:T(8,128)(2,1)S(1)} copy-done((bf16[256,512]{1,0:T(8,128)(2,1)S(1)}, bf16[256,512]{1,0:T(8,128)(2,1)}, u32[]{:S(2)}) %copy-start.6) | copy-done | bytes 262168
  34.2 0.0 copy-start.7
  34.2 0.9 %copy-done.7 = bf16[256,512]{1,0:T(8,128)(2,1)S(1)} copy-done((bf16[256,512]{1,0:T(8,128)(2,1)S(1)}, bf16[256,512]{1,0:T(8,128)(2,1)}, u32[]{:S(2)}) %copy-start.7) | copy-done | bytes 262168
  35.2 0.0 copy-start.9
  35.2 1.0 %copy-done.9 = bf16[256,1024]{1,0:T(8,128)(2,1)S(1)} copy-done((bf16[256,1024]{1,0:T(8,128)(2,1)S(1)}, bf16[256,1024]{1,0:T(8,128)(2,1)}, u32[]{:S(2)}) %copy-start.9) | copy-done | bytes 524312
  36.2 6.2 %attend.1 = (bf16[256,2048]{1,0:T(8,128)(2,1)}, f32[8,128]{1,0:T(8,128)S(1)}) custom-call(f32[256,128]{1,0:T(8,128)S(1)} %get-tuple-element.19.start_ref, bf16[256,2048]{1,0:T(8,128)(2,1)} %query_ref.1, bf16[256,512]{1,0:T(8,128)(2,1)S(1)} %copy-done.6, bf16[256,512]{1,0:T(8,128)(2,1)S(1)} %copy-done.7, bf16[256,1024]{1,0:T(8,128)(2,1)S(1)} %copy-done.9, ...), custom_call_target="tpu_custom_call" | custom-call | tf_op jit(solution)/shard_map/attend/pallas_call | solution.py:483
  42.4 0.0 collective-permute-done.tail_ref
  42.4 0.0 copy-done.1
  42.4 0.0 copy-start.3
  42.4 1.6 %copy-done.3 = bf16[256,4096]{1,0:T(8,128)(2,1)S(1)} copy-done((bf16[256,4096]{1,0:T(8,128)(2,1)S(1)}, bf16[256,4096]{1,0:T(8,128)(2,1)}, u32[]{:S(2)}) %copy-start.3) | copy-done | bytes 2097176
  44.0 5.4 %final.1 = bf16[256,4096]{1,0:T(8,128)(2,1)} custom-call(f32[256,128]{1,0:T(8,128)S(1)} %get-tuple-element.19.start_ref, f32[256,128]{1,0:T(8,128)S(1)} %get-tuple-element.20.level_ref, bf16[4224,128]{1,0:T(8,128)(2,1)} %collective-permute-done.tail_ref, bf16[256,512]{1,0:T(8,128)(2,1)S(1)} %copy-done.5, bf16[256,4096]{1,0:T(8,128)(2,1)S(1)} %copy-done.3, ...), custom_call_target="tpu_custom_call" | custom-call | tf_op jit(solution)/shard_map/final/pallas_call | solution.py:511
Async XLA Ops:
  2.4 19.0 %copy-start = (bf16[256,4096]{1,0:T(8,128)(2,1)S(1)}, bf16[256,4096]{1,0:T(8,128)(2,1)}, u32[]{:S(2)}) copy-start(bf16[256,4096]{1,0:T(8,128)(2,1)} %x_ref.3) | copy-start | bytes 6291460
  2.4 19.0 %copy-start.4 = (bf16[256,512]{1,0:T(8,128)(2,1)S(1)}, bf16[256,512]{1,0:T(8,128)(2,1)}, u32[]{:S(2)}) copy-start(bf16[256,512]{1,0:T(8,128)(2,1)} %write_ref.3) | copy-start | bytes 786436
  2.4 19.0 %copy-start.5 = (bf16[256,512]{1,0:T(8,128)(2,1)S(1)}, bf16[256,512]{1,0:T(8,128)(2,1)}, u32[]{:S(2)}) copy-start(bf16[256,512]{1,0:T(8,128)(2,1)} %read_ref.3) | copy-start | bytes 786436
  2.4 28.7 %all-to-all-start = ((bf16[8,320,128]{2,1,0:T(8,128)(2,1)}), bf16[8,320,128]{2,1,0:T(8,128)(2,1)S(1)}, u32[]{:S(2)}, u32[]{:S(2)}) async-start(bf16[8,320,128]{2,1,0:T(8,128)(2,1)} %pack.1), calls=%async_computation | async-start | bytes 1310720 | tf_op jit(solution)/shard_map/all_to_all | solution.py:429
  9.9 20.4 %collective-permute-start.1 = (bf16[256,1024]{1,0:T(8,128)(2,1)S(1)}, bf16[256,1024]{1,0:T(8,128)(2,1)S(1)}, u32[]{:S(2)}, u32[]{:S(2)}) collective-permute-start(bf16[256,1024]{1,0:T(8,128)(2,1)S(1)} %join.1), channel_id=1, source_target_pairs={{0,1},{1,2},{2,3},{3,4},{4,5},{5,6},{6,7},{7,8},{8,9},{9,10},{10,1... | collective-permute-start | bytes 1572872 | tf_op jit(solution)/shard_map/ppermute | solution.py:362
  17.9 24.5 %collective-permute-start = (bf16[4224,128]{1,0:T(8,128)(2,1)}, bf16[4224,128]{1,0:T(8,128)(2,1)}, u32[]{:S(2)}, u32[]{:S(2)}) collective-permute-start(bf16[4224,128]{1,0:T(8,128)(2,1)} %get-tuple-element.21), channel_id=1, source_target_pairs={{0,1},{1,2},{2,3},{3,4},{4,5},{5,6},{6,7},{7,8},{8,9},{9,10},{10,1... | collective-permute-start | bytes 3244040 | tf_op jit(solution)/shard_map/ppermute | solution.py:362
  26.4 1.3 %copy-start.2 = (bf16[256,4096]{1,0:T(8,128)(2,1)}, bf16[256,4096]{1,0:T(8,128)(2,1)S(1)}, u32[]{:S(2)}) copy-start(bf16[256,4096]{1,0:T(8,128)(2,1)S(1)} %get-tuple-element.23.inner_ref) | copy-start | bytes 6291460
  27.8 14.6 %copy-start.1 = (bf16[256,4096]{1,0:T(8,128)(2,1)S(1)}, bf16[256,4096]{1,0:T(8,128)(2,1)}, u32[]{:S(2)}) copy-start(bf16[256,4096]{1,0:T(8,128)(2,1)} %gate_ref.1) | copy-start | bytes 6291460
  30.4 0.8 %copy-start.8 = (bf16[256,1024]{1,0:T(8,128)(2,1)}, bf16[256,1024]{1,0:T(8,128)(2,1)S(1)}, u32[]{:S(2)}) copy-start(bf16[256,1024]{1,0:T(8,128)(2,1)S(1)} %collective-permute-done.1.prior_ref) | copy-start | bytes 1572868
  31.2 2.1 %collective-permute-start.2 = (bf16[8,320,128]{2,1,0:T(8,128)(2,1)S(1)}, bf16[8,320,128]{2,1,0:T(8,128)(2,1)S(1)}, u32[]{:S(2)}, u32[]{:S(2)}) collective-permute-start(bf16[8,320,128]{2,1,0:T(8,128)(2,1)S(1)} %all-to-all-done.rest_0_), channel_id=1, source_target_pairs={{0,1},{1,0},{2,3},{3,2},{4,5},{5,4},{6,7},{7,6},{8,9},{9,8},{10,11... | collective-permute-start | bytes 1966088 | tf_op jit(solution)/shard_map/ppermute | solution.py:480
  33.3 1.0 %copy-start.6 = (bf16[256,512]{1,0:T(8,128)(2,1)S(1)}, bf16[256,512]{1,0:T(8,128)(2,1)}, u32[]{:S(2)}) copy-start(bf16[256,512]{1,0:T(8,128)(2,1)} %key_ref.1) | copy-start | bytes 786436
  34.2 0.9 %copy-start.7 = (bf16[256,512]{1,0:T(8,128)(2,1)S(1)}, bf16[256,512]{1,0:T(8,128)(2,1)}, u32[]{:S(2)}) copy-start(bf16[256,512]{1,0:T(8,128)(2,1)} %value_ref.1) | copy-start | bytes 786436
  35.2 1.0 %copy-start.9 = (bf16[256,1024]{1,0:T(8,128)(2,1)S(1)}, bf16[256,1024]{1,0:T(8,128)(2,1)}, u32[]{:S(2)}) copy-start(bf16[256,1024]{1,0:T(8,128)(2,1)} %copy-done.8) | copy-start | bytes 1572868
  42.4 1.6 %copy-start.3 = (bf16[256,4096]{1,0:T(8,128)(2,1)S(1)}, bf16[256,4096]{1,0:T(8,128)(2,1)}, u32[]{:S(2)}) copy-start(bf16[256,4096]{1,0:T(8,128)(2,1)} %copy-done.2) | copy-start | bytes 6291460

commit v10 on v9

--- a/solution.py
+++ b/solution.py
@@ -218,7 +218,8 @@
     query_ref,
     key_ref,
     value_ref,
-    prior_ref,
+    prior_key_ref,
+    prior_value_ref,
     *rest,
     state_rows,
     prompt_rows,
@@ -228,7 +229,6 @@
     head = pl.program_id(0)
     mark_ref[...] = jnp.zeros_like(mark_ref)
     tokens = query_ref.shape[0]
-    own = pl.ds(pl.multiple_of(head * HD, HD), HD)
     prompt_count = len(gathered) * gathered[0].shape[0] * prompt_rows
     queries = query_ref.shape[1] // HD
     scale = LOG2E / math.sqrt(HD)
@@ -255,12 +255,8 @@
         return part.reshape(prompt_count, HD).astype(BF16)
 
     prompt_keys, prompt_values = prompt(0), prompt(1)
-    prior = [
-        prior_ref[:, pl.ds(pl.multiple_of((which * kv_count + head) * HD, HD), HD)]
-        for which in range(2)
-    ]
-    near_keys = jnp.concatenate([prior[0], key_ref[:, own]], axis=0)
-    near_values = jnp.concatenate([prior[1], value_ref[:, own]], axis=0)
+    near_keys = jnp.concatenate([prior_key_ref[...], key_ref[...]], axis=0)
+    near_values = jnp.concatenate([prior_value_ref[...], value_ref[...]], axis=0)
     ones = jnp.ones((prompt_count + reach, LANES), BF16)
     for block in range(tokens // LANES):
         rows = slice(block * LANES, (block + 1) * LANES)
@@ -287,6 +283,7 @@
     start_ref,
     level_ref,
     tail_ref,
+    decay_ref,
     read_ref,
     inner_ref,
     gate_ref,
@@ -304,12 +301,12 @@
 
     scale = to_front(jnp.exp(level_ref[...]), group * per_group)
     carried = start_ref[:, :state] < 0
-    read = read_ref[:, pl.ds(pl.multiple_of(group * state, state), state)].astype(F32)
+    read = read_ref[...].astype(F32)
     read = jnp.concatenate([jnp.where(carried, 0.0, read), jnp.where(carried, read, 0.0)], axis=1)
     read = read.astype(BF16)
-    falls_at = heads * channels + pl.multiple_of(group * per_group, per_group)
-    decay = tail_ref[pl.ds(falls_at, per_group), :].astype(F32)
-    decay = decay + tail_ref[pl.ds(falls_at + heads, per_group), :].astype(F32)
+    falls_at = pl.multiple_of(group * per_group, per_group)
+    decay = decay_ref[pl.ds(falls_at, per_group), :].astype(F32)
+    decay = decay + decay_ref[pl.ds(falls_at + heads, per_group), :].astype(F32)
     begin = pl.multiple_of(group * width, width)
     own = lax.rem(lax.axis_index("reader"), NEAR)
     seeds = []
@@ -330,7 +327,7 @@
         falls = [jnp.broadcast_to(decay[h : h + 1, :], (channels, state)) for h in tile_heads]
         seed = seeds[at, :]
         entering = seed.astype(F32) * jnp.concatenate(falls, axis=0)
-        entering = entering + tail_ref[pl.ds(begin + at.start, WIDE), :].astype(F32)
+        entering = entering + tail_ref[at, :].astype(F32)
         states = jnp.concatenate([seed, entering.astype(BF16)], axis=1)
         for block in range(tokens // LANES):
             rows = slice(block * LANES, (block + 1) * LANES)
@@ -340,7 +337,7 @@
                 for offset in range(0, WIDE, LANES)
             ]
             inflow = inflow * jnp.concatenate(falls, axis=1)
-            half = 0.5 * gate_ref[rows, pl.ds(begin + at.start, WIDE)].astype(F32)
+            half = 0.5 * gate_ref[rows, at].astype(F32)
             gated = inner_ref[rows, pl.ds(begin + at.start, WIDE)].astype(F32) + inflow
             gated = gated * (half + half * jnp.tanh(half))
             value_ref[rows, at] = gated
@@ -491,9 +488,10 @@
         in_specs=[
             at_hand,
             pl.BlockSpec((tokens, group_size * HD), lambda k: (0, k)),
-            at_hand,
-            at_hand,
-            at_hand,
+            pl.BlockSpec((tokens, HD), lambda k: (0, k)),
+            pl.BlockSpec((tokens, HD), lambda k: (0, k)),
+            pl.BlockSpec((tokens, HD), lambda k: (0, k)),
+            pl.BlockSpec((tokens, HD), lambda k: (0, kv_count + k)),
         ]
         + [at_hand] * NEAR
         + [pl.BlockSpec(memory_space=pl.ANY)],
@@ -506,7 +504,7 @@
         compiler_params=params(),
         cost_estimate=small,
         name="attend",
-    )(start, in_hbm(queries), answer_keys, answer_values, prior, *gathered, mark)
+    )(start, *map(in_hbm, (queries, answer_keys, answer_values)), prior, prior, *gathered, mark)
 
     mixer_out = pl.pallas_call(
         functools.partial(final_kernel, state_rows=state_rows, **sizes),
@@ -514,10 +512,11 @@
         in_specs=[
             at_hand,
             at_hand,
-            at_hand,
-            at_hand,
-            at_hand,
-            at_hand,
+            pl.BlockSpec((width, state), lambda g: (g, 0)),
+            pl.BlockSpec((2 * heads, state), lambda g: (columns // (2 * heads), 0)),
+            pl.BlockSpec((tokens, state), lambda g: (0, g)),
+            at_hand,
+            wide,
             pl.BlockSpec((1, width), lambda g: (0, g)),
         ]
         + [at_hand] * NEAR
@@ -528,7 +527,7 @@
         compiler_params=params(),
         cost_estimate=small,
         name="final",
-    )(start, level, tail, state_read, inner, gate_input, gain, *gathered, mark)
+    )(start, level, tail, tail, in_hbm(state_read), inner, in_hbm(gate_input), gain, *gathered, mark)
     return (mixer_out, attention_out)
 
 

time: 50.2 us -> 48.2 us (0.960)
  local copies, waits for them, and re-layouts: 6.64 us -> 1.33 us
  waiting for transfers between devices: 4.71 us -> 7.88 us
  Pallas kernels: 25.5 us -> 26.2 us
    unnamed x20 -> x10, local copies, waits for them, and re-layouts: 6.64 us -> 1.33 us
    ppermute x2, waiting for transfers between devices: 2.61 us -> 5.78 us  [shifted(): return lax.ppermute(value, axis, [(i, i + by) for i in range(length - by)])]
  transfers between devices with their start and end apart: 4 -> 4, of which waited for: 2 -> 3; matrix products, arithmetic and copies ran while one was open for 0% -> 0% of each run, Pallas kernels for 37% -> 39%
where the time goes in v10:
time: 48.2 us; the launch traced here: 47.8 us
  Pallas kernels  26.2 us (54%)
  starting transfers between devices  11.7 us (24%)
  waiting for transfers between devices  7.88 us (16%)
  local copies, waits for them, and re-layouts  1.33 us (3%)
  between operations  0.7 us (1%)
    pallas_call x1, Pallas kernels, local(): pl.pallas_call(functools.partial(attend_kernel, state_rows=state_rows, pr...  6.35 us
    all_to_all x1, starting transfers between devices, local(): lax.all_to_all(packed, 'reader', 0, 0, axis_index_groups=lines, tiled=True)  6.3 us
    pallas_call x1, Pallas kernels, local(): pl.pallas_call(functools.partial(tail_kernel, per_group=per_group, channe...  6.05 us
    pallas_call x1, Pallas kernels, local(): pl.pallas_call(functools.partial(final_kernel, state_rows=state_rows, **s...  5.85 us
    ppermute x2, waiting for transfers between devices, shifted(): return lax.ppermute(value, axis, [(i, i + by) for i in range(length - by)])  5.78 us
    ppermute x2, starting transfers between devices, shifted(): return lax.ppermute(value, axis, [(i, i + by) for i in range(length - by)])  5.39 us
    pallas_call x1, Pallas kernels, local(): pl.pallas_call(functools.partial(inner_kernel, **sizes), grid=(groups,),...  5.01 us
    ppermute x1, waiting for transfers between devices, local(): lax.ppermute(line, 'reader', [(i, i ^ 1) for i in range(devices)])  2.09 us
  transfers between devices with their start and end apart: 4, of which 3 were waited for; matrix products, arithmetic and copies ran while one was open for 0% of the time, Pallas kernels for 39%

profile of v10, /device:TPU:18, one launch (start us, length us, event | category | flops | bytes accessed | tf_op | source)
XLA Modules:
  0.0 47.8 jit_solution(12877654031446657997)
XLA Ops:
  0.6 1.8 %pack.1 = bf16[8,320,128]{2,1,0:T(8,128)(2,1)} custom-call(f32[256,128]{1,0:T(8,128)} %state_ref.1, bf16[8,512]{1,0:T(8,128)(2,1)} %keys_ref.1, bf16[8,512]{1,0:T(8,128)(2,1)} %values_ref.2), custom_call_target="tpu_custom_call" | custom-call | tf_op jit(solution)/shard_map/pack/pallas_call | solution.py:409
  2.4 0.0 copy-start
  2.4 6.3 %all-to-all-start = ((bf16[8,320,128]{2,1,0:T(8,128)(2,1)}), bf16[8,320,128]{2,1,0:T(8,128)(2,1)S(1)}, u32[]{:S(2)}, u32[]{:S(2)}) async-start(bf16[8,320,128]{2,1,0:T(8,128)(2,1)} %pack.1), calls=%async_computation | async-start | bytes 1310720 | tf_op jit(solution)/shard_map/all_to_all | solution.py:426
  8.7 0.0 copy-start.3
  8.7 0.0 copy-start.4
  8.7 1.1 %join.1 = bf16[256,1024]{1,0:T(8,128)(2,1)S(1)} custom-call(bf16[256,512]{1,0:T(8,128)(2,1)} %key_ref.1, bf16[256,512]{1,0:T(8,128)(2,1)} %value_ref.1), custom_call_target="tpu_custom_call" | custom-call | tf_op jit(solution)/shard_map/join/pallas_call | solution.py:417
  9.9 1.9 %collective-permute-start.1 = (bf16[256,1024]{1,0:T(8,128)(2,1)S(1)}, bf16[256,1024]{1,0:T(8,128)(2,1)S(1)}, u32[]{:S(2)}, u32[]{:S(2)}) collective-permute-start(bf16[256,1024]{1,0:T(8,128)(2,1)S(1)} %join.1), channel_id=1, source_target_pairs={{0,1},{1,2},{2,3},{3,4},{4,5},{5,6},{6,7},{7,8},{8,9},{9,10},{10,1... | collective-permute-start | bytes 1572872 | tf_op jit(solution)/shard_map/ppermute | solution.py:359
  11.8 6.0 %tail.1 = (bf16[4224,128]{1,0:T(8,128)(2,1)}, f32[256,128]{1,0:T(8,128)S(1)}, f32[64,256]{1,0:T(8,128)S(1)}, f32[256,128]{1,0:T(8,128)S(1)}) custom-call(s32[1,32]{1,0:T(1,128)} %bitcast.7, f32[64,256]{1,0:T(8,128)} %bitcast.5, f32[1,64]{1,0:T(1,128)} %bitcast.8, bf16[256,4096]{1,0:T(8,128)(2,1)} %x_ref.3, bf16[256,512]{1,0:T(8,128)(2,1)} %write_ref.3), custom_call_target="tpu_custom_call" | custom-call | tf_op jit(solution)/shard_map/tail/pallas_call | solution.py:432
  17.9 3.5 %collective-permute-start = (bf16[4224,128]{1,0:T(8,128)(2,1)}, bf16[4224,128]{1,0:T(8,128)(2,1)}, u32[]{:S(2)}, u32[]{:S(2)}) collective-permute-start(bf16[4224,128]{1,0:T(8,128)(2,1)} %get-tuple-element.21), channel_id=1, source_target_pairs={{0,1},{1,2},{2,3},{3,4},{4,5},{5,6},{6,7},{7,8},{8,9},{9,10},{10,1... | collective-permute-start | bytes 3244040 | tf_op jit(solution)/shard_map/ppermute | solution.py:359
  21.3 0.0 copy-done
  21.3 0.0 copy-done.3
  21.3 0.0 copy-done.4
  21.4 5.0 %inner.1 = (bf16[256,4096]{1,0:T(8,128)(2,1)S(1)}, f32[8,128]{1,0:T(8,128)S(1)}) custom-call(f32[256,128]{1,0:T(8,128)S(1)} %get-tuple-element.19.start_ref, f32[256,128]{1,0:T(8,128)S(1)} %get-tuple-element.20.level_ref, f32[64,256]{1,0:T(8,128)S(1)} %get-tuple-element.22.column_ref, f32[1,64]{1,0:T(1,128)} %bitcast.9, bf16[256,4096]{1,0:T(8,128)(2,1)S(1)} %copy-done, ...), custom_call_target="tpu_custom_call" | custom-call | tf_op jit(solution)/shard_map/inner/pallas_call | solution.py:455
  26.4 0.0 copy-start.1
  26.4 1.3 %copy-done.1 = bf16[256,4096]{1,0:T(8,128)(2,1)} copy-done((bf16[256,4096]{1,0:T(8,128)(2,1)}, bf16[256,4096]{1,0:T(8,128)(2,1)S(1)}, u32[]{:S(2)}) %copy-start.1) | copy-done | bytes 2097176
  27.7 2.5 %collective-permute-done.1.prior_key_ref.prior_value_ref = bf16[256,1024]{1,0:T(8,128)(2,1)S(1)} collective-permute-done((bf16[256,1024]{1,0:T(8,128)(2,1)S(1)}, bf16[256,1024]{1,0:T(8,128)(2,1)S(1)}, u32[]{:S(2)}, u32[]{:S(2)}) %collective-permute-start.1) | collective-permute-done | bytes 524320 | tf_op jit(solution)/shard_map/ppermute | solution.py:359
  30.2 0.0 copy-start.2
  30.2 0.0 all-to-all-done.rest_0_
  30.2 0.0 collective-permute-start.2
  30.3 2.1 %collective-permute-done.2.rest_1_ = bf16[8,320,128]{2,1,0:T(8,128)(2,1)S(1)} collective-permute-done((bf16[8,320,128]{2,1,0:T(8,128)(2,1)S(1)}, bf16[8,320,128]{2,1,0:T(8,128)(2,1)S(1)}, u32[]{:S(2)}, u32[]{:S(2)}) %collective-permute-start.2) | collective-permute-done | bytes 655392 | tf_op jit(solution)/shard_map/ppermute | solution.py:477
  32.3 6.3 %attend.1 = (bf16[256,2048]{1,0:T(8,128)(2,1)}, f32[8,128]{1,0:T(8,128)S(1)}) custom-call(f32[256,128]{1,0:T(8,128)S(1)} %get-tuple-element.19.start_ref, bf16[256,2048]{1,0:T(8,128)(2,1)} %query_ref.1, bf16[256,512]{1,0:T(8,128)(2,1)} %key_ref.1, bf16[256,512]{1,0:T(8,128)(2,1)} %value_ref.1, ...), custom_call_target="tpu_custom_call" | custom-call | tf_op jit(solution)/shard_map/attend/pallas_call | solution.py:480
  38.7 3.2 %collective-permute-done.tail_ref.decay_ref = bf16[4224,128]{1,0:T(8,128)(2,1)} collective-permute-done((bf16[4224,128]{1,0:T(8,128)(2,1)}, bf16[4224,128]{1,0:T(8,128)(2,1)}, u32[]{:S(2)}, u32[]{:S(2)}) %collective-permute-start) | collective-permute-done | bytes 1081376 | tf_op jit(solution)/shard_map/ppermute | solution.py:359
  41.9 0.0 copy-done.2
  41.9 5.8 %final.1 = bf16[256,4096]{1,0:T(8,128)(2,1)} custom-call(f32[256,128]{1,0:T(8,128)S(1)} %get-tuple-element.19.start_ref, f32[256,128]{1,0:T(8,128)S(1)} %get-tuple-element.20.level_ref, bf16[4224,128]{1,0:T(8,128)(2,1)} %collective-permute-done.tail_ref.decay_ref, bf16[4224,128]{1,0:T(8,128)(2,1)} %collective-permute-done.tail_ref.decay_ref, ...), custom_call_target="tpu_custom_call" | custom-call | tf_op jit(solution)/shard_map/final/pallas_call | solution.py:509
Async XLA Ops:
  2.4 18.9 %copy-start = (bf16[256,4096]{1,0:T(8,128)(2,1)S(1)}, bf16[256,4096]{1,0:T(8,128)(2,1)}, u32[]{:S(2)}) copy-start(bf16[256,4096]{1,0:T(8,128)(2,1)} %x_ref.3) | copy-start | bytes 6291460
  2.4 27.8 %all-to-all-start = ((bf16[8,320,128]{2,1,0:T(8,128)(2,1)}), bf16[8,320,128]{2,1,0:T(8,128)(2,1)S(1)}, u32[]{:S(2)}, u32[]{:S(2)}) async-start(bf16[8,320,128]{2,1,0:T(8,128)(2,1)} %pack.1), calls=%async_computation | async-start | bytes 1310720 | tf_op jit(solution)/shard_map/all_to_all | solution.py:426
  8.7 12.6 %copy-start.3 = (bf16[256,512]{1,0:T(8,128)(2,1)S(1)}, bf16[256,512]{1,0:T(8,128)(2,1)}, u32[]{:S(2)}) copy-start(bf16[256,512]{1,0:T(8,128)(2,1)} %write_ref.3) | copy-start | bytes 786436
  8.7 12.6 %copy-start.4 = (bf16[256,512]{1,0:T(8,128)(2,1)S(1)}, bf16[256,512]{1,0:T(8,128)(2,1)}, u32[]{:S(2)}) copy-start(bf16[256,512]{1,0:T(8,128)(2,1)} %read_ref.3) | copy-start | bytes 786436
  9.9 20.4 %collective-permute-start.1 = (bf16[256,1024]{1,0:T(8,128)(2,1)S(1)}, bf16[256,1024]{1,0:T(8,128)(2,1)S(1)}, u32[]{:S(2)}, u32[]{:S(2)}) collective-permute-start(bf16[256,1024]{1,0:T(8,128)(2,1)S(1)} %join.1), channel_id=1, source_target_pairs={{0,1},{1,2},{2,3},{3,4},{4,5},{5,6},{6,7},{7,8},{8,9},{9,10},{10,1... | collective-permute-start | bytes 1572872 | tf_op jit(solution)/shard_map/ppermute | solution.py:359
  17.9 24.1 %collective-permute-start = (bf16[4224,128]{1,0:T(8,128)(2,1)}, bf16[4224,128]{1,0:T(8,128)(2,1)}, u32[]{:S(2)}, u32[]{:S(2)}) collective-permute-start(bf16[4224,128]{1,0:T(8,128)(2,1)} %get-tuple-element.21), channel_id=1, source_target_pairs={{0,1},{1,2},{2,3},{3,4},{4,5},{5,6},{6,7},{7,8},{8,9},{9,10},{10,1... | collective-permute-start | bytes 3244040 | tf_op jit(solution)/shard_map/ppermute | solution.py:359
  26.4 1.3 %copy-start.1 = (bf16[256,4096]{1,0:T(8,128)(2,1)}, bf16[256,4096]{1,0:T(8,128)(2,1)S(1)}, u32[]{:S(2)}) copy-start(bf16[256,4096]{1,0:T(8,128)(2,1)S(1)} %get-tuple-element.23.inner_ref) | copy-start | bytes 6291460
  30.2 11.7 %copy-start.2 = (bf16[256,4096]{1,0:T(8,128)(2,1)S(1)}, bf16[256,4096]{1,0:T(8,128)(2,1)}, u32[]{:S(2)}) copy-start(bf16[256,4096]{1,0:T(8,128)(2,1)} %copy-done.1) | copy-start | bytes 6291460
  30.2 2.1 %collective-permute-start.2 = (bf16[8,320,128]{2,1,0:T(8,128)(2,1)S(1)}, bf16[8,320,128]{2,1,0:T(8,128)(2,1)S(1)}, u32[]{:S(2)}, u32[]{:S(2)}) collective-permute-start(bf16[8,320,128]{2,1,0:T(8,128)(2,1)S(1)} %all-to-all-done.rest_0_), channel_id=1, source_target_pairs={{0,1},{1,0},{2,3},{3,2},{4,5},{5,4},{6,7},{7,6},{8,9},{9,8},{10,11... | collective-permute-start | bytes 1966088 | tf_op jit(solution)/shard_map/ppermute | solution.py:477

commit v11 on v8

--- a/solution.py
+++ b/solution.py
@@ -285,6 +285,7 @@
     start_ref,
     level_ref,
     tail_ref,
+    decay_ref,
     read_ref,
     inner_ref,
     gate_ref,
@@ -305,9 +306,9 @@
     read = read_ref[:, pl.ds(pl.multiple_of(group * state, state), state)].astype(F32)
     read = jnp.concatenate([jnp.where(carried, 0.0, read), jnp.where(carried, read, 0.0)], axis=1)
     read = read.astype(BF16)
-    falls_at = heads * channels + pl.multiple_of(group * per_group, per_group)
-    decay = tail_ref[pl.ds(falls_at, per_group), :].astype(F32)
-    decay = decay + tail_ref[pl.ds(falls_at + heads, per_group), :].astype(F32)
+    falls_at = pl.multiple_of(group * per_group, per_group)
+    decay = decay_ref[pl.ds(falls_at, per_group), :].astype(F32)
+    decay = decay + decay_ref[pl.ds(falls_at + heads, per_group), :].astype(F32)
     begin = pl.multiple_of(group * width, width)
     own = lax.rem(lax.axis_index("reader"), NEAR)
     seeds = []
@@ -328,7 +329,7 @@
         falls = [jnp.broadcast_to(decay[h : h + 1, :], (channels, state)) for h in tile_heads]
         seed = seeds[at, :]
         entering = seed.astype(F32) * jnp.concatenate(falls, axis=0)
-        entering = entering + tail_ref[pl.ds(begin + at.start, WIDE), :].astype(F32)
+        entering = entering + tail_ref[at, :].astype(F32)
         states = jnp.concatenate([seed, entering.astype(BF16)], axis=1)
         for block in range(tokens // LANES):
             rows = slice(block * LANES, (block + 1) * LANES)
@@ -500,7 +501,8 @@
         in_specs=[
             at_hand,
             at_hand,
-            at_hand,
+            pl.BlockSpec((width, state), lambda g: (g, 0)),
+            pl.BlockSpec((2 * heads, state), lambda g: (columns // (2 * heads), 0)),
             at_hand,
             at_hand,
             at_hand,
@@ -513,7 +515,7 @@
         compiler_params=params(),
         cost_estimate=small,
         name="final",
-    )(start, level, tail, state_read, inner, gate_input, gain, *gathered)
+    )(start, level, tail, tail, state_read, inner, gate_input, gain, *gathered)
     return (mixer_out, attention_out)
 
 

time: 47.8 us -> 47.7 us (level)
  local copies, waits for them, and re-layouts: 4.4 us -> 3.12 us
  waiting for transfers between devices: 5.84 us -> 7.05 us
    unnamed x24 -> x20, local copies, waits for them, and re-layouts: 4.4 us -> 3.12 us
    ppermute x2, waiting for transfers between devices: 3.75 us -> 4.95 us  [shifted(): return lax.ppermute(value, axis, [(i, i + by) for i in range(length - by)])]
where the time goes in v11:
time: 47.7 us; the launch traced here: 47.2 us
  Pallas kernels  24.8 us (52%)
  starting transfers between devices  11.6 us (24%)
  waiting for transfers between devices  7.05 us (15%)
  local copies, waits for them, and re-layouts  3.12 us (7%)
  between operations  0.72 us (2%)
    all_to_all x1, starting transfers between devices, local(): lax.all_to_all(packed, 'reader', 0, 0, axis_index_groups=lines, tiled=True)  6.17 us
    pallas_call x1, Pallas kernels, local(): pl.pallas_call(functools.partial(tail_kernel, per_group=per_group, channe...  6.04 us
    pallas_call x1, Pallas kernels, local(): pl.pallas_call(functools.partial(final_kernel, state_rows=state_rows, **s...  5.4 us
    ppermute x2, starting transfers between devices, shifted(): return lax.ppermute(value, axis, [(i, i + by) for i in range(length - by)])  5.39 us
    pallas_call x1, Pallas kernels, local(): pl.pallas_call(functools.partial(attend_kernel, state_rows=state_rows, pr...  5.24 us
    pallas_call x1, Pallas kernels, local(): pl.pallas_call(functools.partial(inner_kernel, **sizes), grid=(groups,),...  5.06 us
    ppermute x2, waiting for transfers between devices, shifted(): return lax.ppermute(value, axis, [(i, i + by) for i in range(length - by)])  4.95 us
    unnamed x20, local copies, waits for them, and re-layouts  3.12 us
  transfers between devices with their start and end apart: 4, of which 3 were waited for; matrix products, arithmetic and copies ran while one was open for 0% of the time, Pallas kernels for 37%

profile of v11, /device:TPU:18, one launch (start us, length us, event | category | flops | bytes accessed | tf_op | source)
XLA Modules:
  0.0 47.2 jit_solution(10448418554819140624)
XLA Ops:
  0.6 1.8 %pack.1 = bf16[8,320,128]{2,1,0:T(8,128)(2,1)} custom-call(f32[256,128]{1,0:T(8,128)} %state_ref.1, bf16[8,512]{1,0:T(8,128)(2,1)} %keys_ref.1, bf16[8,512]{1,0:T(8,128)(2,1)} %values_ref.2), custom_call_target="tpu_custom_call" | custom-call | tf_op jit(solution)/shard_map/pack/pallas_call | solution.py:411
  2.4 6.2 %all-to-all-start = ((bf16[8,320,128]{2,1,0:T(8,128)(2,1)}), bf16[8,320,128]{2,1,0:T(8,128)(2,1)S(1)}, u32[]{:S(2)}, u32[]{:S(2)}) async-start(bf16[8,320,128]{2,1,0:T(8,128)(2,1)} %pack.1), calls=%async_computation | async-start | bytes 1310720 | tf_op jit(solution)/shard_map/all_to_all | solution.py:428
  8.6 0.0 copy-start
  8.6 0.0 copy-start.5
  8.6 0.0 copy-start.6
  8.6 1.2 %join.1 = bf16[256,1024]{1,0:T(8,128)(2,1)S(1)} custom-call(bf16[256,512]{1,0:T(8,128)(2,1)} %key_ref.1, bf16[256,512]{1,0:T(8,128)(2,1)} %value_ref.1), custom_call_target="tpu_custom_call" | custom-call | tf_op jit(solution)/shard_map/join/pallas_call | solution.py:419
  9.8 1.9 %collective-permute-start.1 = (bf16[256,1024]{1,0:T(8,128)(2,1)S(1)}, bf16[256,1024]{1,0:T(8,128)(2,1)S(1)}, u32[]{:S(2)}, u32[]{:S(2)}) collective-permute-start(bf16[256,1024]{1,0:T(8,128)(2,1)S(1)} %join.1), channel_id=1, source_target_pairs={{0,1},{1,2},{2,3},{3,4},{4,5},{5,6},{6,7},{7,8},{8,9},{9,10},{10,1... | collective-permute-start | bytes 1572872 | tf_op jit(solution)/shard_map/ppermute | solution.py:361
  11.8 6.0 %tail.1 = (bf16[4224,128]{1,0:T(8,128)(2,1)}, f32[256,128]{1,0:T(8,128)S(1)}, f32[64,256]{1,0:T(8,128)S(1)}, f32[256,128]{1,0:T(8,128)S(1)}) custom-call(s32[1,32]{1,0:T(1,128)} %bitcast.7, f32[64,256]{1,0:T(8,128)} %bitcast.5, f32[1,64]{1,0:T(1,128)} %bitcast.8, bf16[256,4096]{1,0:T(8,128)(2,1)} %x_ref.3, bf16[256,512]{1,0:T(8,128)(2,1)} %write_ref.3), custom_call_target="tpu_custom_call" | custom-call | tf_op jit(solution)/shard_map/tail/pallas_call | solution.py:434
  17.8 3.5 %collective-permute-start = (bf16[4224,128]{1,0:T(8,128)(2,1)}, bf16[4224,128]{1,0:T(8,128)(2,1)}, u32[]{:S(2)}, u32[]{:S(2)}) collective-permute-start(bf16[4224,128]{1,0:T(8,128)(2,1)} %get-tuple-element.19), channel_id=1, source_target_pairs={{0,1},{1,2},{2,3},{3,4},{4,5},{5,6},{6,7},{7,8},{8,9},{9,10},{10,1... | collective-permute-start | bytes 3244040 | tf_op jit(solution)/shard_map/ppermute | solution.py:361
  21.3 0.0 copy-done
  21.3 0.0 copy-done.5
  21.3 0.0 copy-done.6
  21.3 0.0 copy-start.2
  21.3 0.0 copy-start.3
  21.3 5.1 %inner.1.inner_ref = bf16[256,4096]{1,0:T(8,128)(2,1)S(1)} custom-call(f32[256,128]{1,0:T(8,128)S(1)} %get-tuple-element.17.start_ref, f32[256,128]{1,0:T(8,128)S(1)} %get-tuple-element.18.level_ref, f32[64,256]{1,0:T(8,128)S(1)} %get-tuple-element.22.column_ref, f32[1,64]{1,0:T(1,128)} %bitcast.9, bf16[256,4096]{1,0:T(8,128)(2,1)S(1)} %copy-done, ...), custom_call_target="tpu_custom_call" | custom-call | tf_op jit(solution)/shard_map/inner/pallas_call | solution.py:457
  26.4 3.7 %collective-permute-done.1.prior_ref = bf16[256,1024]{1,0:T(8,128)(2,1)S(1)} collective-permute-done((bf16[256,1024]{1,0:T(8,128)(2,1)S(1)}, bf16[256,1024]{1,0:T(8,128)(2,1)S(1)}, u32[]{:S(2)}, u32[]{:S(2)}) %collective-permute-start.1) | collective-permute-done | bytes 524320 | tf_op jit(solution)/shard_map/ppermute | solution.py:361
  30.1 0.0 copy-start.8
  30.1 0.8 %copy-done.8 = bf16[256,1024]{1,0:T(8,128)(2,1)} copy-done((bf16[256,1024]{1,0:T(8,128)(2,1)}, bf16[256,1024]{1,0:T(8,128)(2,1)S(1)}, u32[]{:S(2)}) %copy-start.8) | copy-done | bytes 524312
  30.9 0.0 all-to-all-done.rest_0_
  30.9 0.0 copy-start.1
  30.9 0.0 collective-permute-start.2
  30.9 2.1 %collective-permute-done.2.rest_1_ = bf16[8,320,128]{2,1,0:T(8,128)(2,1)S(1)} collective-permute-done((bf16[8,320,128]{2,1,0:T(8,128)(2,1)S(1)}, bf16[8,320,128]{2,1,0:T(8,128)(2,1)S(1)}, u32[]{:S(2)}, u32[]{:S(2)}) %collective-permute-start.2) | collective-permute-done | bytes 655392 | tf_op jit(solution)/shard_map/ppermute | solution.py:476
  33.0 0.0 copy-done.2
  33.0 0.0 copy-done.3
  33.0 0.0 copy-start.4
  33.0 1.2 %copy-done.4 = bf16[256,2048]{1,0:T(8,128)(2,1)S(1)} copy-done((bf16[256,2048]{1,0:T(8,128)(2,1)S(1)}, bf16[256,2048]{1,0:T(8,128)(2,1)}, u32[]{:S(2)}) %copy-start.4) | copy-done | bytes 1048600
  34.3 0.0 copy-start.9
  34.3 1.0 %copy-done.9 = bf16[256,1024]{1,0:T(8,128)(2,1)S(1)} copy-done((bf16[256,1024]{1,0:T(8,128)(2,1)S(1)}, bf16[256,1024]{1,0:T(8,128)(2,1)}, u32[]{:S(2)}) %copy-start.9) | copy-done | bytes 524312
  35.3 0.0 copy-start.7
  35.3 5.2 %attend.1 = bf16[256,2048]{1,0:T(8,128)(2,1)} custom-call(f32[256,128]{1,0:T(8,128)S(1)} %get-tuple-element.17.start_ref, bf16[256,2048]{1,0:T(8,128)(2,1)S(1)} %copy-done.4, bf16[256,512]{1,0:T(8,128)(2,1)S(1)} %copy-done.2, bf16[256,512]{1,0:T(8,128)(2,1)S(1)} %copy-done.3, bf16[256,1024]{1,0:T(8,128)(2,1)S(1)} %copy-done.9, ...), custom_call_target="tpu_custom_call" | custom-call | tf_op jit(solution)/shard_map/attend/pallas_call | solution.py:479
  40.6 1.2 %collective-permute-done.tail_ref.decay_ref = bf16[4224,128]{1,0:T(8,128)(2,1)} collective-permute-done((bf16[4224,128]{1,0:T(8,128)(2,1)}, bf16[4224,128]{1,0:T(8,128)(2,1)}, u32[]{:S(2)}, u32[]{:S(2)}) %collective-permute-start) | collective-permute-done | bytes 1081376 | tf_op jit(solution)/shard_map/ppermute | solution.py:361
  41.8 0.0 copy-done.1
  41.8 0.0 copy-done.7
  41.8 5.4 %final.1 = bf16[256,4096]{1,0:T(8,128)(2,1)} custom-call(f32[256,128]{1,0:T(8,128)S(1)} %get-tuple-element.17.start_ref, f32[256,128]{1,0:T(8,128)S(1)} %get-tuple-element.18.level_ref, bf16[4224,128]{1,0:T(8,128)(2,1)} %collective-permute-done.tail_ref.decay_ref, bf16[4224,128]{1,0:T(8,128)(2,1)} %collective-permute-done.tail_ref.decay_ref, ...), custom_call_target="tpu_custom_call" | custom-call | tf_op jit(solution)/shard_map/final/pallas_call | solution.py:498
Async XLA Ops:
  2.4 28.5 %all-to-all-start = ((bf16[8,320,128]{2,1,0:T(8,128)(2,1)}), bf16[8,320,128]{2,1,0:T(8,128)(2,1)S(1)}, u32[]{:S(2)}, u32[]{:S(2)}) async-start(bf16[8,320,128]{2,1,0:T(8,128)(2,1)} %pack.1), calls=%async_computation | async-start | bytes 1310720 | tf_op jit(solution)/shard_map/all_to_all | solution.py:428
  8.6 12.7 %copy-start = (bf16[256,4096]{1,0:T(8,128)(2,1)S(1)}, bf16[256,4096]{1,0:T(8,128)(2,1)}, u32[]{:S(2)}) copy-start(bf16[256,4096]{1,0:T(8,128)(2,1)} %x_ref.3) | copy-start | bytes 6291460
  8.6 12.7 %copy-start.5 = (bf16[256,512]{1,0:T(8,128)(2,1)S(1)}, bf16[256,512]{1,0:T(8,128)(2,1)}, u32[]{:S(2)}) copy-start(bf16[256,512]{1,0:T(8,128)(2,1)} %write_ref.3) | copy-start | bytes 786436
  8.6 12.7 %copy-start.6 = (bf16[256,512]{1,0:T(8,128)(2,1)S(1)}, bf16[256,512]{1,0:T(8,128)(2,1)}, u32[]{:S(2)}) copy-start(bf16[256,512]{1,0:T(8,128)(2,1)} %read_ref.3) | copy-start | bytes 786436
  9.8 20.3 %collective-permute-start.1 = (bf16[256,1024]{1,0:T(8,128)(2,1)S(1)}, bf16[256,1024]{1,0:T(8,128)(2,1)S(1)}, u32[]{:S(2)}, u32[]{:S(2)}) collective-permute-start(bf16[256,1024]{1,0:T(8,128)(2,1)S(1)} %join.1), channel_id=1, source_target_pairs={{0,1},{1,2},{2,3},{3,4},{4,5},{5,6},{6,7},{7,8},{8,9},{9,10},{10,1... | collective-permute-start | bytes 1572872 | tf_op jit(solution)/shard_map/ppermute | solution.py:361
  17.8 24.0 %collective-permute-start = (bf16[4224,128]{1,0:T(8,128)(2,1)}, bf16[4224,128]{1,0:T(8,128)(2,1)}, u32[]{:S(2)}, u32[]{:S(2)}) collective-permute-start(bf16[4224,128]{1,0:T(8,128)(2,1)} %get-tuple-element.19), channel_id=1, source_target_pairs={{0,1},{1,2},{2,3},{3,4},{4,5},{5,6},{6,7},{7,8},{8,9},{9,10},{10,1... | collective-permute-start | bytes 3244040 | tf_op jit(solution)/shard_map/ppermute | solution.py:361
  21.3 11.7 %copy-start.2 = (bf16[256,512]{1,0:T(8,128)(2,1)S(1)}, bf16[256,512]{1,0:T(8,128)(2,1)}, u32[]{:S(2)}) copy-start(bf16[256,512]{1,0:T(8,128)(2,1)} %key_ref.1) | copy-start | bytes 786436
  21.3 11.7 %copy-start.3 = (bf16[256,512]{1,0:T(8,128)(2,1)S(1)}, bf16[256,512]{1,0:T(8,128)(2,1)}, u32[]{:S(2)}) copy-start(bf16[256,512]{1,0:T(8,128)(2,1)} %value_ref.1) | copy-start | bytes 786436
  30.1 0.8 %copy-start.8 = (bf16[256,1024]{1,0:T(8,128)(2,1)}, bf16[256,1024]{1,0:T(8,128)(2,1)S(1)}, u32[]{:S(2)}) copy-start(bf16[256,1024]{1,0:T(8,128)(2,1)S(1)} %collective-permute-done.1.prior_ref) | copy-start | bytes 1572868
  30.9 10.9 %copy-start.1 = (bf16[256,4096]{1,0:T(8,128)(2,1)S(1)}, bf16[256,4096]{1,0:T(8,128)(2,1)}, u32[]{:S(2)}) copy-start(bf16[256,4096]{1,0:T(8,128)(2,1)} %gate_ref.1) | copy-start | bytes 6291460
  30.9 2.1 %collective-permute-start.2 = (bf16[8,320,128]{2,1,0:T(8,128)(2,1)S(1)}, bf16[8,320,128]{2,1,0:T(8,128)(2,1)S(1)}, u32[]{:S(2)}, u32[]{:S(2)}) collective-permute-start(bf16[8,320,128]{2,1,0:T(8,128)(2,1)S(1)} %all-to-all-done.rest_0_), channel_id=1, source_target_pairs={{0,1},{1,0},{2,3},{3,2},{4,5},{5,4},{6,7},{7,6},{8,9},{9,8},{10,11... | collective-permute-start | bytes 1966088 | tf_op jit(solution)/shard_map/ppermute | solution.py:476
  33.0 1.2 %copy-start.4 = (bf16[256,2048]{1,0:T(8,128)(2,1)S(1)}, bf16[256,2048]{1,0:T(8,128)(2,1)}, u32[]{:S(2)}) copy-start(bf16[256,2048]{1,0:T(8,128)(2,1)} %query_ref.1) | copy-start | bytes 3145732
  34.3 1.0 %copy-start.9 = (bf16[256,1024]{1,0:T(8,128)(2,1)S(1)}, bf16[256,1024]{1,0:T(8,128)(2,1)}, u32[]{:S(2)}) copy-start(bf16[256,1024]{1,0:T(8,128)(2,1)} %copy-done.8) | copy-start | bytes 1572868
  35.3 6.5 %copy-start.7 = (bf16[256,512]{1,0:T(8,128)(2,1)S(1)}, bf16[256,512]{1,0:T(8,128)(2,1)}, u32[]{:S(2)}) copy-start(bf16[256,512]{1,0:T(8,128)(2,1)} %read_ref.3) | copy-start | bytes 786436

commit v12 on v11

--- a/solution.py
+++ b/solution.py
@@ -304,56 +304,62 @@
     scale = to_front(jnp.exp(level_ref[...]), group * per_group)
     carried = start_ref[:, :state] < 0
     read = read_ref[:, pl.ds(pl.multiple_of(group * state, state), state)].astype(F32)
-    read = jnp.concatenate([jnp.where(carried, 0.0, read), jnp.where(carried, read, 0.0)], axis=1)
-    read = read.astype(BF16)
+    fresh = jnp.where(carried, 0.0, read).astype(BF16)
+    kept = jnp.where(carried, read, 0.0).astype(BF16)
+    read = jnp.concatenate([fresh, kept, kept], axis=1)
     falls_at = pl.multiple_of(group * per_group, per_group)
     decay = decay_ref[pl.ds(falls_at, per_group), :].astype(F32)
     decay = decay + decay_ref[pl.ds(falls_at + heads, per_group), :].astype(F32)
     begin = pl.multiple_of(group * width, width)
-    own = lax.rem(lax.axis_index("reader"), NEAR)
-    seeds = []
     runs = width // (NEAR * state_rows)
-    for run in range(runs):
-        parts = [ref[group * runs + run, :state_rows, :] for ref in gathered]
-        bit = 1
-        while bit < NEAR:
-            swap = lax.rem(own // bit, 2) == 1
-            parts = [jnp.where(swap, parts[i ^ bit], parts[i]) for i in range(NEAR)]
-            bit *= 2
-        seeds += parts
-    seeds = jnp.concatenate(seeds, axis=0)
-    squares = [None] * (tokens // LANES)
-    for tile in range(width // WIDE):
-        at = slice(tile * WIDE, (tile + 1) * WIDE)
-        tile_heads = range(at.start // channels, at.stop // channels)
-        falls = [jnp.broadcast_to(decay[h : h + 1, :], (channels, state)) for h in tile_heads]
-        seed = seeds[at, :]
-        entering = seed.astype(F32) * jnp.concatenate(falls, axis=0)
-        entering = entering + tail_ref[at, :].astype(F32)
-        states = jnp.concatenate([seed, entering.astype(BF16)], axis=1)
+
+    def finish(in_order):
+        seeds = [
+            ref[group * runs + run, :state_rows, :] for run in range(runs) for ref in in_order
+        ]
+        seeds = jnp.concatenate(seeds, axis=0)
+        squares = [None] * (tokens // LANES)
+        for tile in range(width // WIDE):
+            at = slice(tile * WIDE, (tile + 1) * WIDE)
+            tile_heads = range(at.start // channels, at.stop // channels)
+            falls = [jnp.broadcast_to(decay[h : h + 1, :], (channels, state)) for h in tile_heads]
+            seed = seeds[at, :]
+            faded = (seed.astype(F32) * jnp.concatenate(falls, axis=0)).astype(BF16)
+            states = jnp.concatenate([seed, faded, tail_ref[at, :]], axis=1)
+            for block in range(tokens // LANES):
+                rows = slice(block * LANES, (block + 1) * LANES)
+                inflow = dot(read[rows, :], states, 1, 1)
+                falls = [
+                    spread(scale[rows, :], (at.start + offset) // channels, channels)
+                    for offset in range(0, WIDE, LANES)
+                ]
+                inflow = inflow * jnp.concatenate(falls, axis=1)
+                own = pl.ds(begin + at.start, WIDE)
+                half = 0.5 * gate_ref[rows, own].astype(F32)
+                gated = inner_ref[rows, own].astype(F32) + inflow
+                gated = gated * (half + half * jnp.tanh(half))
+                value_ref[rows, at] = gated
+                square = gated * gated
+                for part in range(WIDE // LANES):
+                    piece = square[:, part * LANES : (part + 1) * LANES]
+                    squares[block] = piece if squares[block] is None else squares[block] + piece
         for block in range(tokens // LANES):
             rows = slice(block * LANES, (block + 1) * LANES)
-            inflow = dot(read[rows, :], states, 1, 1)
-            falls = [
-                spread(scale[rows, :], (at.start + offset) // channels, channels)
-                for offset in range(0, WIDE, LANES)
-            ]
-            inflow = inflow * jnp.concatenate(falls, axis=1)
-            half = 0.5 * gate_ref[rows, pl.ds(begin + at.start, WIDE)].astype(F32)
-            gated = inner_ref[rows, pl.ds(begin + at.start, WIDE)].astype(F32) + inflow
-            gated = gated * (half + half * jnp.tanh(half))
-            value_ref[rows, at] = gated
-            square = gated * gated
-            for part in range(WIDE // LANES):
-                piece = square[:, part * LANES : (part + 1) * LANES]
-                squares[block] = piece if squares[block] is None else squares[block] + piece
-    for block in range(tokens // LANES):
-        rows = slice(block * LANES, (block + 1) * LANES)
-        mean = jnp.sum(squares[block], axis=1, keepdims=True) * (1.0 / width)
-        norm = lax.rsqrt(mean + 1e-05)
-        for tile in range(width // WIDE):
-            at = slice(tile * WIDE, (tile + 1) * WIDE)
-            out_ref[rows, at] = (value_ref[rows, at] * norm * gain_ref[:, at]).astype(BF16)
+            mean = jnp.sum(squares[block], axis=1, keepdims=True) * (1.0 / width)
+            norm = lax.rsqrt(mean + 1e-05)
+            for tile in range(width // WIDE):
+                at = slice(tile * WIDE, (tile + 1) * WIDE)
+                out_ref[rows, at] = (value_ref[rows, at] * norm * gain_ref[:, at]).astype(BF16)
+
+    place = lax.rem(lax.axis_index("reader"), NEAR)
+
+    @pl.when(place == 0)
+    def _():
+        finish(gathered)
+
+    @pl.when(place == 1)
+    def _():
+        finish(gathered[::-1])
 
 
 def shifted(value, axis, by):

time: 47.7 us -> 48.2 us (1.010)
  Pallas kernels: 24.8 us -> 25.3 us
    pallas_call x1, Pallas kernels: 5.4 us -> 5.94 us  [local(): pl.pallas_call(functools.partial(final_kernel, state_rows=state_rows, **s...]
where the time goes in v12:
time: 48.2 us; the launch traced here: 47.7 us
  Pallas kernels  25.3 us (52%)
  starting transfers between devices  11.6 us (24%)
  waiting for transfers between devices  7.05 us (15%)
  local copies, waits for them, and re-layouts  3.12 us (6%)
  between operations  0.72 us (1%)
    all_to_all x1, starting transfers between devices, local(): lax.all_to_all(packed, 'reader', 0, 0, axis_index_groups=lines, tiled=True)  6.17 us
    pallas_call x1, Pallas kernels, local(): pl.pallas_call(functools.partial(tail_kernel, per_group=per_group, channe...  6.04 us
    pallas_call x1, Pallas kernels, local(): pl.pallas_call(functools.partial(final_kernel, state_rows=state_rows, **s...  5.94 us
    ppermute x2, starting transfers between devices, shifted(): return lax.ppermute(value, axis, [(i, i + by) for i in range(length - by)])  5.39 us
    pallas_call x1, Pallas kernels, local(): pl.pallas_call(functools.partial(attend_kernel, state_rows=state_rows, pr...  5.24 us
    pallas_call x1, Pallas kernels, local(): pl.pallas_call(functools.partial(inner_kernel, **sizes), grid=(groups,),...  5.06 us
    ppermute x2, waiting for transfers between devices, shifted(): return lax.ppermute(value, axis, [(i, i + by) for i in range(length - by)])  4.95 us
    unnamed x20, local copies, waits for them, and re-layouts  3.12 us
  transfers between devices with their start and end apart: 4, of which 3 were waited for; matrix products, arithmetic and copies ran while one was open for 0% of the time, Pallas kernels for 37%

profile of v12, /device:TPU:18, one launch (start us, length us, event | category | flops | bytes accessed | tf_op | source)
XLA Modules:
  0.0 47.7 jit_solution(1033215762421019769)
XLA Ops:
  0.6 1.8 %pack.1 = bf16[8,320,128]{2,1,0:T(8,128)(2,1)} custom-call(f32[256,128]{1,0:T(8,128)} %state_ref.1, bf16[8,512]{1,0:T(8,128)(2,1)} %keys_ref.1, bf16[8,512]{1,0:T(8,128)(2,1)} %values_ref.2), custom_call_target="tpu_custom_call" | custom-call | tf_op jit(solution)/shard_map/pack/pallas_call | solution.py:417
  2.4 6.2 %all-to-all-start = ((bf16[8,320,128]{2,1,0:T(8,128)(2,1)}), bf16[8,320,128]{2,1,0:T(8,128)(2,1)S(1)}, u32[]{:S(2)}, u32[]{:S(2)}) async-start(bf16[8,320,128]{2,1,0:T(8,128)(2,1)} %pack.1), calls=%async_computation | async-start | bytes 1310720 | tf_op jit(solution)/shard_map/all_to_all | solution.py:434
  8.6 0.0 copy-start
  8.6 0.0 copy-start.5
  8.6 0.0 copy-start.6
  8.6 1.2 %join.1 = bf16[256,1024]{1,0:T(8,128)(2,1)S(1)} custom-call(bf16[256,512]{1,0:T(8,128)(2,1)} %key_ref.1, bf16[256,512]{1,0:T(8,128)(2,1)} %value_ref.1), custom_call_target="tpu_custom_call" | custom-call | tf_op jit(solution)/shard_map/join/pallas_call | solution.py:425
  9.8 1.9 %collective-permute-start.1 = (bf16[256,1024]{1,0:T(8,128)(2,1)S(1)}, bf16[256,1024]{1,0:T(8,128)(2,1)S(1)}, u32[]{:S(2)}, u32[]{:S(2)}) collective-permute-start(bf16[256,1024]{1,0:T(8,128)(2,1)S(1)} %join.1), channel_id=1, source_target_pairs={{0,1},{1,2},{2,3},{3,4},{4,5},{5,6},{6,7},{7,8},{8,9},{9,10},{10,1... | collective-permute-start | bytes 1572872 | tf_op jit(solution)/shard_map/ppermute | solution.py:367
  11.8 6.0 %tail.1 = (bf16[4224,128]{1,0:T(8,128)(2,1)}, f32[256,128]{1,0:T(8,128)S(1)}, f32[64,256]{1,0:T(8,128)S(1)}, f32[256,128]{1,0:T(8,128)S(1)}) custom-call(s32[1,32]{1,0:T(1,128)} %bitcast.7, f32[64,256]{1,0:T(8,128)} %bitcast.5, f32[1,64]{1,0:T(1,128)} %bitcast.8, bf16[256,4096]{1,0:T(8,128)(2,1)} %x_ref.3, bf16[256,512]{1,0:T(8,128)(2,1)} %write_ref.3), custom_call_target="tpu_custom_call" | custom-call | tf_op jit(solution)/shard_map/tail/pallas_call | solution.py:440
  17.8 3.5 %collective-permute-start = (bf16[4224,128]{1,0:T(8,128)(2,1)}, bf16[4224,128]{1,0:T(8,128)(2,1)}, u32[]{:S(2)}, u32[]{:S(2)}) collective-permute-start(bf16[4224,128]{1,0:T(8,128)(2,1)} %get-tuple-element.19), channel_id=1, source_target_pairs={{0,1},{1,2},{2,3},{3,4},{4,5},{5,6},{6,7},{7,8},{8,9},{9,10},{10,1... | collective-permute-start | bytes 3244040 | tf_op jit(solution)/shard_map/ppermute | solution.py:367
  21.3 0.0 copy-done
  21.3 0.0 copy-done.5
  21.3 0.0 copy-done.6
  21.3 0.0 copy-start.2
  21.3 0.0 copy-start.3
  21.3 5.1 %inner.1.inner_ref = bf16[256,4096]{1,0:T(8,128)(2,1)S(1)} custom-call(f32[256,128]{1,0:T(8,128)S(1)} %get-tuple-element.17.start_ref, f32[256,128]{1,0:T(8,128)S(1)} %get-tuple-element.18.level_ref, f32[64,256]{1,0:T(8,128)S(1)} %get-tuple-element.22.column_ref, f32[1,64]{1,0:T(1,128)} %bitcast.9, bf16[256,4096]{1,0:T(8,128)(2,1)S(1)} %copy-done, ...), custom_call_target="tpu_custom_call" | custom-call | tf_op jit(solution)/shard_map/inner/pallas_call | solution.py:463
  26.4 3.7 %collective-permute-done.1.prior_ref = bf16[256,1024]{1,0:T(8,128)(2,1)S(1)} collective-permute-done((bf16[256,1024]{1,0:T(8,128)(2,1)S(1)}, bf16[256,1024]{1,0:T(8,128)(2,1)S(1)}, u32[]{:S(2)}, u32[]{:S(2)}) %collective-permute-start.1) | collective-permute-done | bytes 524320 | tf_op jit(solution)/shard_map/ppermute | solution.py:367
  30.1 0.0 copy-start.8
  30.1 0.8 %copy-done.8 = bf16[256,1024]{1,0:T(8,128)(2,1)} copy-done((bf16[256,1024]{1,0:T(8,128)(2,1)}, bf16[256,1024]{1,0:T(8,128)(2,1)S(1)}, u32[]{:S(2)}) %copy-start.8) | copy-done | bytes 524312
  30.9 0.0 all-to-all-done.rest_0_
  30.9 0.0 copy-start.1
  30.9 0.0 collective-permute-start.2
  30.9 2.1 %collective-permute-done.2.rest_1_ = bf16[8,320,128]{2,1,0:T(8,128)(2,1)S(1)} collective-permute-done((bf16[8,320,128]{2,1,0:T(8,128)(2,1)S(1)}, bf16[8,320,128]{2,1,0:T(8,128)(2,1)S(1)}, u32[]{:S(2)}, u32[]{:S(2)}) %collective-permute-start.2) | collective-permute-done | bytes 655392 | tf_op jit(solution)/shard_map/ppermute | solution.py:482
  33.0 0.0 copy-done.2
  33.0 0.0 copy-done.3
  33.0 0.0 copy-start.4
  33.0 1.2 %copy-done.4 = bf16[256,2048]{1,0:T(8,128)(2,1)S(1)} copy-done((bf16[256,2048]{1,0:T(8,128)(2,1)S(1)}, bf16[256,2048]{1,0:T(8,128)(2,1)}, u32[]{:S(2)}) %copy-start.4) | copy-done | bytes 1048600
  34.3 0.0 copy-start.9
  34.3 1.0 %copy-done.9 = bf16[256,1024]{1,0:T(8,128)(2,1)S(1)} copy-done((bf16[256,1024]{1,0:T(8,128)(2,1)S(1)}, bf16[256,1024]{1,0:T(8,128)(2,1)}, u32[]{:S(2)}) %copy-start.9) | copy-done | bytes 524312
  35.3 0.0 copy-start.7
  35.3 5.2 %attend.1 = bf16[256,2048]{1,0:T(8,128)(2,1)} custom-call(f32[256,128]{1,0:T(8,128)S(1)} %get-tuple-element.17.start_ref, bf16[256,2048]{1,0:T(8,128)(2,1)S(1)} %copy-done.4, bf16[256,512]{1,0:T(8,128)(2,1)S(1)} %copy-done.2, bf16[256,512]{1,0:T(8,128)(2,1)S(1)} %copy-done.3, bf16[256,1024]{1,0:T(8,128)(2,1)S(1)} %copy-done.9, ...), custom_call_target="tpu_custom_call" | custom-call | tf_op jit(solution)/shard_map/attend/pallas_call | solution.py:485
  40.6 1.2 %collective-permute-done.tail_ref.decay_ref = bf16[4224,128]{1,0:T(8,128)(2,1)} collective-permute-done((bf16[4224,128]{1,0:T(8,128)(2,1)}, bf16[4224,128]{1,0:T(8,128)(2,1)}, u32[]{:S(2)}, u32[]{:S(2)}) %collective-permute-start) | collective-permute-done | bytes 1081376 | tf_op jit(solution)/shard_map/ppermute | solution.py:367
  41.8 0.0 copy-done.1
  41.8 0.0 copy-done.7
  41.8 5.9 %final.1 = bf16[256,4096]{1,0:T(8,128)(2,1)} custom-call(f32[256,128]{1,0:T(8,128)S(1)} %get-tuple-element.17.start_ref, f32[256,128]{1,0:T(8,128)S(1)} %get-tuple-element.18.level_ref, bf16[4224,128]{1,0:T(8,128)(2,1)} %collective-permute-done.tail_ref.decay_ref, bf16[4224,128]{1,0:T(8,128)(2,1)} %collective-permute-done.tail_ref.decay_ref, ...), custom_call_target="tpu_custom_call" | custom-call | tf_op jit(solution)/shard_map/final/pallas_call | solution.py:504
Async XLA Ops:
  2.4 28.5 %all-to-all-start = ((bf16[8,320,128]{2,1,0:T(8,128)(2,1)}), bf16[8,320,128]{2,1,0:T(8,128)(2,1)S(1)}, u32[]{:S(2)}, u32[]{:S(2)}) async-start(bf16[8,320,128]{2,1,0:T(8,128)(2,1)} %pack.1), calls=%async_computation | async-start | bytes 1310720 | tf_op jit(solution)/shard_map/all_to_all | solution.py:434
  8.6 12.7 %copy-start = (bf16[256,4096]{1,0:T(8,128)(2,1)S(1)}, bf16[256,4096]{1,0:T(8,128)(2,1)}, u32[]{:S(2)}) copy-start(bf16[256,4096]{1,0:T(8,128)(2,1)} %x_ref.3) | copy-start | bytes 6291460
  8.6 12.7 %copy-start.5 = (bf16[256,512]{1,0:T(8,128)(2,1)S(1)}, bf16[256,512]{1,0:T(8,128)(2,1)}, u32[]{:S(2)}) copy-start(bf16[256,512]{1,0:T(8,128)(2,1)} %write_ref.3) | copy-start | bytes 786436
  8.6 12.7 %copy-start.6 = (bf16[256,512]{1,0:T(8,128)(2,1)S(1)}, bf16[256,512]{1,0:T(8,128)(2,1)}, u32[]{:S(2)}) copy-start(bf16[256,512]{1,0:T(8,128)(2,1)} %read_ref.3) | copy-start | bytes 786436
  9.8 20.3 %collective-permute-start.1 = (bf16[256,1024]{1,0:T(8,128)(2,1)S(1)}, bf16[256,1024]{1,0:T(8,128)(2,1)S(1)}, u32[]{:S(2)}, u32[]{:S(2)}) collective-permute-start(bf16[256,1024]{1,0:T(8,128)(2,1)S(1)} %join.1), channel_id=1, source_target_pairs={{0,1},{1,2},{2,3},{3,4},{4,5},{5,6},{6,7},{7,8},{8,9},{9,10},{10,1... | collective-permute-start | bytes 1572872 | tf_op jit(solution)/shard_map/ppermute | solution.py:367
  17.8 24.0 %collective-permute-start = (bf16[4224,128]{1,0:T(8,128)(2,1)}, bf16[4224,128]{1,0:T(8,128)(2,1)}, u32[]{:S(2)}, u32[]{:S(2)}) collective-permute-start(bf16[4224,128]{1,0:T(8,128)(2,1)} %get-tuple-element.19), channel_id=1, source_target_pairs={{0,1},{1,2},{2,3},{3,4},{4,5},{5,6},{6,7},{7,8},{8,9},{9,10},{10,1... | collective-permute-start | bytes 3244040 | tf_op jit(solution)/shard_map/ppermute | solution.py:367
  21.3 11.7 %copy-start.2 = (bf16[256,512]{1,0:T(8,128)(2,1)S(1)}, bf16[256,512]{1,0:T(8,128)(2,1)}, u32[]{:S(2)}) copy-start(bf16[256,512]{1,0:T(8,128)(2,1)} %key_ref.1) | copy-start | bytes 786436
  21.3 11.7 %copy-start.3 = (bf16[256,512]{1,0:T(8,128)(2,1)S(1)}, bf16[256,512]{1,0:T(8,128)(2,1)}, u32[]{:S(2)}) copy-start(bf16[256,512]{1,0:T(8,128)(2,1)} %value_ref.1) | copy-start | bytes 786436
  30.1 0.8 %copy-start.8 = (bf16[256,1024]{1,0:T(8,128)(2,1)}, bf16[256,1024]{1,0:T(8,128)(2,1)S(1)}, u32[]{:S(2)}) copy-start(bf16[256,1024]{1,0:T(8,128)(2,1)S(1)} %collective-permute-done.1.prior_ref) | copy-start | bytes 1572868
  30.9 10.9 %copy-start.1 = (bf16[256,4096]{1,0:T(8,128)(2,1)S(1)}, bf16[256,4096]{1,0:T(8,128)(2,1)}, u32[]{:S(2)}) copy-start(bf16[256,4096]{1,0:T(8,128)(2,1)} %gate_ref.1) | copy-start | bytes 6291460
  30.9 2.1 %collective-permute-start.2 = (bf16[8,320,128]{2,1,0:T(8,128)(2,1)S(1)}, bf16[8,320,128]{2,1,0:T(8,128)(2,1)S(1)}, u32[]{:S(2)}, u32[]{:S(2)}) collective-permute-start(bf16[8,320,128]{2,1,0:T(8,128)(2,1)S(1)} %all-to-all-done.rest_0_), channel_id=1, source_target_pairs={{0,1},{1,0},{2,3},{3,2},{4,5},{5,4},{6,7},{7,6},{8,9},{9,8},{10,11... | collective-permute-start | bytes 1966088 | tf_op jit(solution)/shard_map/ppermute | solution.py:482
  33.0 1.2 %copy-start.4 = (bf16[256,2048]{1,0:T(8,128)(2,1)S(1)}, bf16[256,2048]{1,0:T(8,128)(2,1)}, u32[]{:S(2)}) copy-start(bf16[256,2048]{1,0:T(8,128)(2,1)} %query_ref.1) | copy-start | bytes 3145732
  34.3 1.0 %copy-start.9 = (bf16[256,1024]{1,0:T(8,128)(2,1)S(1)}, bf16[256,1024]{1,0:T(8,128)(2,1)}, u32[]{:S(2)}) copy-start(bf16[256,1024]{1,0:T(8,128)(2,1)} %copy-done.8) | copy-start | bytes 1572868
  35.3 6.5 %copy-start.7 = (bf16[256,512]{1,0:T(8,128)(2,1)S(1)}, bf16[256,512]{1,0:T(8,128)(2,1)}, u32[]{:S(2)}) copy-start(bf16[256,512]{1,0:T(8,128)(2,1)} %read_ref.3) | copy-start | bytes 786436

commit v13 on v12

--- a/solution.py
+++ b/solution.py
@@ -326,14 +326,14 @@
             seed = seeds[at, :]
             faded = (seed.astype(F32) * jnp.concatenate(falls, axis=0)).astype(BF16)
             states = jnp.concatenate([seed, faded, tail_ref[at, :]], axis=1)
+            inflows = dot(read, states, 1, 1)
             for block in range(tokens // LANES):
                 rows = slice(block * LANES, (block + 1) * LANES)
-                inflow = dot(read[rows, :], states, 1, 1)
                 falls = [
                     spread(scale[rows, :], (at.start + offset) // channels, channels)
                     for offset in range(0, WIDE, LANES)
                 ]
-                inflow = inflow * jnp.concatenate(falls, axis=1)
+                inflow = inflows[rows, :] * jnp.concatenate(falls, axis=1)
                 own = pl.ds(begin + at.start, WIDE)
                 half = 0.5 * gate_ref[rows, own].astype(F32)
                 gated = inner_ref[rows, own].astype(F32) + inflow

time: 48.2 us -> 47.8 us (level)
  no operation moved by 1% of the time
where the time goes in v13:
time: 47.8 us; the launch traced here: 47.3 us
  Pallas kernels  24.9 us (52%)
  starting transfers between devices  11.6 us (24%)
  waiting for transfers between devices  7.05 us (15%)
  local copies, waits for them, and re-layouts  3.12 us (7%)
  between operations  0.72 us (2%)
    all_to_all x1, starting transfers between devices, local(): lax.all_to_all(packed, 'reader', 0, 0, axis_index_groups=lines, tiled=True)  6.17 us
    pallas_call x1, Pallas kernels, local(): pl.pallas_call(functools.partial(tail_kernel, per_group=per_group, channe...  6.04 us
    pallas_call x1, Pallas kernels, local(): pl.pallas_call(functools.partial(final_kernel, state_rows=state_rows, **s...  5.51 us
    ppermute x2, starting transfers between devices, shifted(): return lax.ppermute(value, axis, [(i, i + by) for i in range(length - by)])  5.39 us
    pallas_call x1, Pallas kernels, local(): pl.pallas_call(functools.partial(attend_kernel, state_rows=state_rows, pr...  5.24 us
    pallas_call x1, Pallas kernels, local(): pl.pallas_call(functools.partial(inner_kernel, **sizes), grid=(groups,),...  5.06 us
    ppermute x2, waiting for transfers between devices, shifted(): return lax.ppermute(value, axis, [(i, i + by) for i in range(length - by)])  4.95 us
    unnamed x20, local copies, waits for them, and re-layouts  3.12 us
  transfers between devices with their start and end apart: 4, of which 3 were waited for; matrix products, arithmetic and copies ran while one was open for 0% of the time, Pallas kernels for 37%

profile of v13, /device:TPU:18, one launch (start us, length us, event | category | flops | bytes accessed | tf_op | source)
XLA Modules:
  0.0 47.3 jit_solution(5573273710862892294)
XLA Ops:
  0.6 1.8 %pack.1 = bf16[8,320,128]{2,1,0:T(8,128)(2,1)} custom-call(f32[256,128]{1,0:T(8,128)} %state_ref.1, bf16[8,512]{1,0:T(8,128)(2,1)} %keys_ref.1, bf16[8,512]{1,0:T(8,128)(2,1)} %values_ref.2), custom_call_target="tpu_custom_call" | custom-call | tf_op jit(solution)/shard_map/pack/pallas_call | solution.py:417
  2.4 6.2 %all-to-all-start = ((bf16[8,320,128]{2,1,0:T(8,128)(2,1)}), bf16[8,320,128]{2,1,0:T(8,128)(2,1)S(1)}, u32[]{:S(2)}, u32[]{:S(2)}) async-start(bf16[8,320,128]{2,1,0:T(8,128)(2,1)} %pack.1), calls=%async_computation | async-start | bytes 1310720 | tf_op jit(solution)/shard_map/all_to_all | solution.py:434
  8.6 0.0 copy-start
  8.6 0.0 copy-start.5
  8.6 0.0 copy-start.6
  8.6 1.2 %join.1 = bf16[256,1024]{1,0:T(8,128)(2,1)S(1)} custom-call(bf16[256,512]{1,0:T(8,128)(2,1)} %key_ref.1, bf16[256,512]{1,0:T(8,128)(2,1)} %value_ref.1), custom_call_target="tpu_custom_call" | custom-call | tf_op jit(solution)/shard_map/join/pallas_call | solution.py:425
  9.8 1.9 %collective-permute-start.1 = (bf16[256,1024]{1,0:T(8,128)(2,1)S(1)}, bf16[256,1024]{1,0:T(8,128)(2,1)S(1)}, u32[]{:S(2)}, u32[]{:S(2)}) collective-permute-start(bf16[256,1024]{1,0:T(8,128)(2,1)S(1)} %join.1), channel_id=1, source_target_pairs={{0,1},{1,2},{2,3},{3,4},{4,5},{5,6},{6,7},{7,8},{8,9},{9,10},{10,1... | collective-permute-start | bytes 1572872 | tf_op jit(solution)/shard_map/ppermute | solution.py:367
  11.8 6.0 %tail.1 = (bf16[4224,128]{1,0:T(8,128)(2,1)}, f32[256,128]{1,0:T(8,128)S(1)}, f32[64,256]{1,0:T(8,128)S(1)}, f32[256,128]{1,0:T(8,128)S(1)}) custom-call(s32[1,32]{1,0:T(1,128)} %bitcast.7, f32[64,256]{1,0:T(8,128)} %bitcast.5, f32[1,64]{1,0:T(1,128)} %bitcast.8, bf16[256,4096]{1,0:T(8,128)(2,1)} %x_ref.3, bf16[256,512]{1,0:T(8,128)(2,1)} %write_ref.3), custom_call_target="tpu_custom_call" | custom-call | tf_op jit(solution)/shard_map/tail/pallas_call | solution.py:440
  17.8 3.5 %collective-permute-start = (bf16[4224,128]{1,0:T(8,128)(2,1)}, bf16[4224,128]{1,0:T(8,128)(2,1)}, u32[]{:S(2)}, u32[]{:S(2)}) collective-permute-start(bf16[4224,128]{1,0:T(8,128)(2,1)} %get-tuple-element.19), channel_id=1, source_target_pairs={{0,1},{1,2},{2,3},{3,4},{4,5},{5,6},{6,7},{7,8},{8,9},{9,10},{10,1... | collective-permute-start | bytes 3244040 | tf_op jit(solution)/shard_map/ppermute | solution.py:367
  21.3 0.0 copy-done
  21.3 0.0 copy-done.5
  21.3 0.0 copy-done.6
  21.3 0.0 copy-start.2
  21.3 0.0 copy-start.3
  21.3 5.1 %inner.1.inner_ref = bf16[256,4096]{1,0:T(8,128)(2,1)S(1)} custom-call(f32[256,128]{1,0:T(8,128)S(1)} %get-tuple-element.17.start_ref, f32[256,128]{1,0:T(8,128)S(1)} %get-tuple-element.18.level_ref, f32[64,256]{1,0:T(8,128)S(1)} %get-tuple-element.22.column_ref, f32[1,64]{1,0:T(1,128)} %bitcast.9, bf16[256,4096]{1,0:T(8,128)(2,1)S(1)} %copy-done, ...), custom_call_target="tpu_custom_call" | custom-call | tf_op jit(solution)/shard_map/inner/pallas_call | solution.py:463
  26.4 3.7 %collective-permute-done.1.prior_ref = bf16[256,1024]{1,0:T(8,128)(2,1)S(1)} collective-permute-done((bf16[256,1024]{1,0:T(8,128)(2,1)S(1)}, bf16[256,1024]{1,0:T(8,128)(2,1)S(1)}, u32[]{:S(2)}, u32[]{:S(2)}) %collective-permute-start.1) | collective-permute-done | bytes 524320 | tf_op jit(solution)/shard_map/ppermute | solution.py:367
  30.1 0.0 copy-start.8
  30.1 0.8 %copy-done.8 = bf16[256,1024]{1,0:T(8,128)(2,1)} copy-done((bf16[256,1024]{1,0:T(8,128)(2,1)}, bf16[256,1024]{1,0:T(8,128)(2,1)S(1)}, u32[]{:S(2)}) %copy-start.8) | copy-done | bytes 524312
  30.9 0.0 all-to-all-done.rest_0_
  30.9 0.0 copy-start.1
  30.9 0.0 collective-permute-start.2
  30.9 2.1 %collective-permute-done.2.rest_1_ = bf16[8,320,128]{2,1,0:T(8,128)(2,1)S(1)} collective-permute-done((bf16[8,320,128]{2,1,0:T(8,128)(2,1)S(1)}, bf16[8,320,128]{2,1,0:T(8,128)(2,1)S(1)}, u32[]{:S(2)}, u32[]{:S(2)}) %collective-permute-start.2) | collective-permute-done | bytes 655392 | tf_op jit(solution)/shard_map/ppermute | solution.py:482
  33.0 0.0 copy-done.2
  33.0 0.0 copy-done.3
  33.0 0.0 copy-start.4
  33.0 1.2 %copy-done.4 = bf16[256,2048]{1,0:T(8,128)(2,1)S(1)} copy-done((bf16[256,2048]{1,0:T(8,128)(2,1)S(1)}, bf16[256,2048]{1,0:T(8,128)(2,1)}, u32[]{:S(2)}) %copy-start.4) | copy-done | bytes 1048600
  34.3 0.0 copy-start.9
  34.3 1.0 %copy-done.9 = bf16[256,1024]{1,0:T(8,128)(2,1)S(1)} copy-done((bf16[256,1024]{1,0:T(8,128)(2,1)S(1)}, bf16[256,1024]{1,0:T(8,128)(2,1)}, u32[]{:S(2)}) %copy-start.9) | copy-done | bytes 524312
  35.3 0.0 copy-start.7
  35.3 5.2 %attend.1 = bf16[256,2048]{1,0:T(8,128)(2,1)} custom-call(f32[256,128]{1,0:T(8,128)S(1)} %get-tuple-element.17.start_ref, bf16[256,2048]{1,0:T(8,128)(2,1)S(1)} %copy-done.4, bf16[256,512]{1,0:T(8,128)(2,1)S(1)} %copy-done.2, bf16[256,512]{1,0:T(8,128)(2,1)S(1)} %copy-done.3, bf16[256,1024]{1,0:T(8,128)(2,1)S(1)} %copy-done.9, ...), custom_call_target="tpu_custom_call" | custom-call | tf_op jit(solution)/shard_map/attend/pallas_call | solution.py:485
  40.6 1.2 %collective-permute-done.tail_ref.decay_ref = bf16[4224,128]{1,0:T(8,128)(2,1)} collective-permute-done((bf16[4224,128]{1,0:T(8,128)(2,1)}, bf16[4224,128]{1,0:T(8,128)(2,1)}, u32[]{:S(2)}, u32[]{:S(2)}) %collective-permute-start) | collective-permute-done | bytes 1081376 | tf_op jit(solution)/shard_map/ppermute | solution.py:367
  41.8 0.0 copy-done.1
  41.8 0.0 copy-done.7
  41.8 5.5 %final.1 = bf16[256,4096]{1,0:T(8,128)(2,1)} custom-call(f32[256,128]{1,0:T(8,128)S(1)} %get-tuple-element.17.start_ref, f32[256,128]{1,0:T(8,128)S(1)} %get-tuple-element.18.level_ref, bf16[4224,128]{1,0:T(8,128)(2,1)} %collective-permute-done.tail_ref.decay_ref, bf16[4224,128]{1,0:T(8,128)(2,1)} %collective-permute-done.tail_ref.decay_ref, ...), custom_call_target="tpu_custom_call" | custom-call | tf_op jit(solution)/shard_map/final/pallas_call | solution.py:504
Async XLA Ops:
  2.4 28.5 %all-to-all-start = ((bf16[8,320,128]{2,1,0:T(8,128)(2,1)}), bf16[8,320,128]{2,1,0:T(8,128)(2,1)S(1)}, u32[]{:S(2)}, u32[]{:S(2)}) async-start(bf16[8,320,128]{2,1,0:T(8,128)(2,1)} %pack.1), calls=%async_computation | async-start | bytes 1310720 | tf_op jit(solution)/shard_map/all_to_all | solution.py:434
  8.6 12.7 %copy-start = (bf16[256,4096]{1,0:T(8,128)(2,1)S(1)}, bf16[256,4096]{1,0:T(8,128)(2,1)}, u32[]{:S(2)}) copy-start(bf16[256,4096]{1,0:T(8,128)(2,1)} %x_ref.3) | copy-start | bytes 6291460
  8.6 12.7 %copy-start.5 = (bf16[256,512]{1,0:T(8,128)(2,1)S(1)}, bf16[256,512]{1,0:T(8,128)(2,1)}, u32[]{:S(2)}) copy-start(bf16[256,512]{1,0:T(8,128)(2,1)} %write_ref.3) | copy-start | bytes 786436
  8.6 12.7 %copy-start.6 = (bf16[256,512]{1,0:T(8,128)(2,1)S(1)}, bf16[256,512]{1,0:T(8,128)(2,1)}, u32[]{:S(2)}) copy-start(bf16[256,512]{1,0:T(8,128)(2,1)} %read_ref.3) | copy-start | bytes 786436
  9.8 20.3 %collective-permute-start.1 = (bf16[256,1024]{1,0:T(8,128)(2,1)S(1)}, bf16[256,1024]{1,0:T(8,128)(2,1)S(1)}, u32[]{:S(2)}, u32[]{:S(2)}) collective-permute-start(bf16[256,1024]{1,0:T(8,128)(2,1)S(1)} %join.1), channel_id=1, source_target_pairs={{0,1},{1,2},{2,3},{3,4},{4,5},{5,6},{6,7},{7,8},{8,9},{9,10},{10,1... | collective-permute-start | bytes 1572872 | tf_op jit(solution)/shard_map/ppermute | solution.py:367
  17.8 24.0 %collective-permute-start = (bf16[4224,128]{1,0:T(8,128)(2,1)}, bf16[4224,128]{1,0:T(8,128)(2,1)}, u32[]{:S(2)}, u32[]{:S(2)}) collective-permute-start(bf16[4224,128]{1,0:T(8,128)(2,1)} %get-tuple-element.19), channel_id=1, source_target_pairs={{0,1},{1,2},{2,3},{3,4},{4,5},{5,6},{6,7},{7,8},{8,9},{9,10},{10,1... | collective-permute-start | bytes 3244040 | tf_op jit(solution)/shard_map/ppermute | solution.py:367
  21.3 11.7 %copy-start.2 = (bf16[256,512]{1,0:T(8,128)(2,1)S(1)}, bf16[256,512]{1,0:T(8,128)(2,1)}, u32[]{:S(2)}) copy-start(bf16[256,512]{1,0:T(8,128)(2,1)} %key_ref.1) | copy-start | bytes 786436
  21.3 11.7 %copy-start.3 = (bf16[256,512]{1,0:T(8,128)(2,1)S(1)}, bf16[256,512]{1,0:T(8,128)(2,1)}, u32[]{:S(2)}) copy-start(bf16[256,512]{1,0:T(8,128)(2,1)} %value_ref.1) | copy-start | bytes 786436
  30.1 0.8 %copy-start.8 = (bf16[256,1024]{1,0:T(8,128)(2,1)}, bf16[256,1024]{1,0:T(8,128)(2,1)S(1)}, u32[]{:S(2)}) copy-start(bf16[256,1024]{1,0:T(8,128)(2,1)S(1)} %collective-permute-done.1.prior_ref) | copy-start | bytes 1572868
  30.9 10.9 %copy-start.1 = (bf16[256,4096]{1,0:T(8,128)(2,1)S(1)}, bf16[256,4096]{1,0:T(8,128)(2,1)}, u32[]{:S(2)}) copy-start(bf16[256,4096]{1,0:T(8,128)(2,1)} %gate_ref.1) | copy-start | bytes 6291460
  30.9 2.1 %collective-permute-start.2 = (bf16[8,320,128]{2,1,0:T(8,128)(2,1)S(1)}, bf16[8,320,128]{2,1,0:T(8,128)(2,1)S(1)}, u32[]{:S(2)}, u32[]{:S(2)}) collective-permute-start(bf16[8,320,128]{2,1,0:T(8,128)(2,1)S(1)} %all-to-all-done.rest_0_), channel_id=1, source_target_pairs={{0,1},{1,0},{2,3},{3,2},{4,5},{5,4},{6,7},{7,6},{8,9},{9,8},{10,11... | collective-permute-start | bytes 1966088 | tf_op jit(solution)/shard_map/ppermute | solution.py:482
  33.0 1.2 %copy-start.4 = (bf16[256,2048]{1,0:T(8,128)(2,1)S(1)}, bf16[256,2048]{1,0:T(8,128)(2,1)}, u32[]{:S(2)}) copy-start(bf16[256,2048]{1,0:T(8,128)(2,1)} %query_ref.1) | copy-start | bytes 3145732
  34.3 1.0 %copy-start.9 = (bf16[256,1024]{1,0:T(8,128)(2,1)S(1)}, bf16[256,1024]{1,0:T(8,128)(2,1)}, u32[]{:S(2)}) copy-start(bf16[256,1024]{1,0:T(8,128)(2,1)} %copy-done.8) | copy-start | bytes 1572868
  35.3 6.5 %copy-start.7 = (bf16[256,512]{1,0:T(8,128)(2,1)S(1)}, bf16[256,512]{1,0:T(8,128)(2,1)}, u32[]{:S(2)}) copy-start(bf16[256,512]{1,0:T(8,128)(2,1)} %read_ref.3) | copy-start | bytes 786436

commit v14 on v13

--- a/solution.py
+++ b/solution.py
@@ -59,18 +59,23 @@
     out_ref[:, width:] = values_ref[...]
 
 
-def pack_kernel(state_ref, keys_ref, values_ref, out_ref):
+def pack_kernel(state_ref, keys_ref, values_ref, out_ref, held_ref, sems):
     rows = state_ref.shape[0]
-    state = state_ref[...].astype(BF16)
+    held_ref[:rows, :] = state_ref[...].astype(BF16)
     parts = []
     for ref in (keys_ref, values_ref):
         wide = ref[...].astype(F32)
         for head in range(wide.shape[1] // HD):
             parts.append(wide[:, head * HD : (head + 1) * HD])
-    parts = jnp.concatenate(parts, axis=0).astype(BF16)
-    for copy in range(out_ref.shape[0]):
-        out_ref[copy, :rows, :] = state
-        out_ref[copy, rows:, :] = parts
+    held_ref[rows:, :] = jnp.concatenate(parts, axis=0).astype(BF16)
+    copies = [
+        pltpu.make_async_copy(held_ref, out_ref.at[place], sems.at[place])
+        for place in range(out_ref.shape[0])
+    ]
+    for copy in copies:
+        copy.start()
+    for copy in copies:
+        copy.wait()
 
 
 def level_part(lengths_ref, raw_ref, rate_ref, level_ref, column_ref, start_ref, weight_ref, tail_ref):
@@ -417,7 +422,11 @@
     packed = pl.pallas_call(
         pack_kernel,
         out_shape=jax.ShapeDtypeStruct((devices // NEAR, packed_rows, HD), BF16),
-        out_specs=at_hand,
+        out_specs=pl.BlockSpec(memory_space=pl.ANY),
+        scratch_shapes=[
+            pltpu.VMEM((packed_rows, HD), BF16),
+            pltpu.SemaphoreType.DMA((devices // NEAR,)),
+        ],
         compiler_params=params(),
         name="pack",
     )(prompt_state, prompt_keys, prompt_values)

time: 47.8 us -> 47.8 us (level)
  no operation moved by 1% of the time
where the time goes in v14:
time: 47.8 us; the launch traced here: 47.3 us
  Pallas kernels  24.9 us (52%)
  starting transfers between devices  11.6 us (24%)
  waiting for transfers between devices  7.05 us (15%)
  local copies, waits for them, and re-layouts  3.12 us (7%)
  between operations  0.73 us (2%)
    all_to_all x1, starting transfers between devices, local(): lax.all_to_all(packed, 'reader', 0, 0, axis_index_groups=lines, tiled=True)  6.18 us
    pallas_call x1, Pallas kernels, local(): pl.pallas_call(functools.partial(tail_kernel, per_group=per_group, channe...  6.04 us
    pallas_call x1, Pallas kernels, local(): pl.pallas_call(functools.partial(final_kernel, state_rows=state_rows, **s...  5.51 us
    ppermute x2, starting transfers between devices, shifted(): return lax.ppermute(value, axis, [(i, i + by) for i in range(length - by)])  5.39 us
    pallas_call x1, Pallas kernels, local(): pl.pallas_call(functools.partial(attend_kernel, state_rows=state_rows, pr...  5.24 us
    pallas_call x1, Pallas kernels, local(): pl.pallas_call(functools.partial(inner_kernel, **sizes), grid=(groups,),...  5.06 us
    ppermute x2, waiting for transfers between devices, shifted(): return lax.ppermute(value, axis, [(i, i + by) for i in range(length - by)])  4.95 us
    unnamed x20, local copies, waits for them, and re-layouts  3.12 us
  transfers between devices with their start and end apart: 4, of which 3 were waited for; matrix products, arithmetic and copies ran while one was open for 0% of the time, Pallas kernels for 37%

profile of v14, /device:TPU:18, one launch (start us, length us, event | category | flops | bytes accessed | tf_op | source)
XLA Modules:
  0.0 47.3 jit_solution(13279841666138161004)
XLA Ops:
  0.6 1.8 %pack.1 = bf16[8,320,128]{2,1,0:T(8,128)(2,1)} custom-call(f32[256,128]{1,0:T(8,128)} %state_ref.1, bf16[8,512]{1,0:T(8,128)(2,1)} %keys_ref.1, bf16[8,512]{1,0:T(8,128)(2,1)} %values_ref.2), custom_call_target="tpu_custom_call" | custom-call | tf_op jit(solution)/shard_map/pack/pallas_call | solution.py:422
  2.5 6.2 %all-to-all-start = ((bf16[8,320,128]{2,1,0:T(8,128)(2,1)}), bf16[8,320,128]{2,1,0:T(8,128)(2,1)S(1)}, u32[]{:S(2)}, u32[]{:S(2)}) async-start(bf16[8,320,128]{2,1,0:T(8,128)(2,1)} %pack.1), calls=%async_computation | async-start | bytes 1310720 | tf_op jit(solution)/shard_map/all_to_all | solution.py:443
  8.6 0.0 copy-start
  8.6 0.0 copy-start.5
  8.6 0.0 copy-start.6
  8.7 1.2 %join.1 = bf16[256,1024]{1,0:T(8,128)(2,1)S(1)} custom-call(bf16[256,512]{1,0:T(8,128)(2,1)} %key_ref.1, bf16[256,512]{1,0:T(8,128)(2,1)} %value_ref.1), custom_call_target="tpu_custom_call" | custom-call | tf_op jit(solution)/shard_map/join/pallas_call | solution.py:434
  9.9 1.9 %collective-permute-start.1 = (bf16[256,1024]{1,0:T(8,128)(2,1)S(1)}, bf16[256,1024]{1,0:T(8,128)(2,1)S(1)}, u32[]{:S(2)}, u32[]{:S(2)}) collective-permute-start(bf16[256,1024]{1,0:T(8,128)(2,1)S(1)} %join.1), channel_id=1, source_target_pairs={{0,1},{1,2},{2,3},{3,4},{4,5},{5,6},{6,7},{7,8},{8,9},{9,10},{10,1... | collective-permute-start | bytes 1572872 | tf_op jit(solution)/shard_map/ppermute | solution.py:372
  11.8 6.0 %tail.1 = (bf16[4224,128]{1,0:T(8,128)(2,1)}, f32[256,128]{1,0:T(8,128)S(1)}, f32[64,256]{1,0:T(8,128)S(1)}, f32[256,128]{1,0:T(8,128)S(1)}) custom-call(s32[1,32]{1,0:T(1,128)} %bitcast.7, f32[64,256]{1,0:T(8,128)} %bitcast.5, f32[1,64]{1,0:T(1,128)} %bitcast.8, bf16[256,4096]{1,0:T(8,128)(2,1)} %x_ref.3, bf16[256,512]{1,0:T(8,128)(2,1)} %write_ref.3), custom_call_target="tpu_custom_call" | custom-call | tf_op jit(solution)/shard_map/tail/pallas_call | solution.py:449
  17.8 3.5 %collective-permute-start = (bf16[4224,128]{1,0:T(8,128)(2,1)}, bf16[4224,128]{1,0:T(8,128)(2,1)}, u32[]{:S(2)}, u32[]{:S(2)}) collective-permute-start(bf16[4224,128]{1,0:T(8,128)(2,1)} %get-tuple-element.19), channel_id=1, source_target_pairs={{0,1},{1,2},{2,3},{3,4},{4,5},{5,6},{6,7},{7,8},{8,9},{9,10},{10,1... | collective-permute-start | bytes 3244040 | tf_op jit(solution)/shard_map/ppermute | solution.py:372
  21.3 0.0 copy-done
  21.3 0.0 copy-done.5
  21.3 0.0 copy-done.6
  21.3 0.0 copy-start.2
  21.4 0.0 copy-start.3
  21.4 5.1 %inner.1.inner_ref = bf16[256,4096]{1,0:T(8,128)(2,1)S(1)} custom-call(f32[256,128]{1,0:T(8,128)S(1)} %get-tuple-element.17.start_ref, f32[256,128]{1,0:T(8,128)S(1)} %get-tuple-element.18.level_ref, f32[64,256]{1,0:T(8,128)S(1)} %get-tuple-element.22.column_ref, f32[1,64]{1,0:T(1,128)} %bitcast.9, bf16[256,4096]{1,0:T(8,128)(2,1)S(1)} %copy-done, ...), custom_call_target="tpu_custom_call" | custom-call | tf_op jit(solution)/shard_map/inner/pallas_call | solution.py:472
  26.4 3.7 %collective-permute-done.1.prior_ref = bf16[256,1024]{1,0:T(8,128)(2,1)S(1)} collective-permute-done((bf16[256,1024]{1,0:T(8,128)(2,1)S(1)}, bf16[256,1024]{1,0:T(8,128)(2,1)S(1)}, u32[]{:S(2)}, u32[]{:S(2)}) %collective-permute-start.1) | collective-permute-done | bytes 524320 | tf_op jit(solution)/shard_map/ppermute | solution.py:372
  30.1 0.0 copy-start.8
  30.1 0.8 %copy-done.8 = bf16[256,1024]{1,0:T(8,128)(2,1)} copy-done((bf16[256,1024]{1,0:T(8,128)(2,1)}, bf16[256,1024]{1,0:T(8,128)(2,1)S(1)}, u32[]{:S(2)}) %copy-start.8) | copy-done | bytes 524312
  31.0 0.0 all-to-all-done.rest_0_
  31.0 0.0 copy-start.1
  31.0 0.0 collective-permute-start.2
  31.0 2.1 %collective-permute-done.2.rest_1_ = bf16[8,320,128]{2,1,0:T(8,128)(2,1)S(1)} collective-permute-done((bf16[8,320,128]{2,1,0:T(8,128)(2,1)S(1)}, bf16[8,320,128]{2,1,0:T(8,128)(2,1)S(1)}, u32[]{:S(2)}, u32[]{:S(2)}) %collective-permute-start.2) | collective-permute-done | bytes 655392 | tf_op jit(solution)/shard_map/ppermute | solution.py:491
  33.1 0.0 copy-done.2
  33.1 0.0 copy-done.3
  33.1 0.0 copy-start.4
  33.1 1.2 %copy-done.4 = bf16[256,2048]{1,0:T(8,128)(2,1)S(1)} copy-done((bf16[256,2048]{1,0:T(8,128)(2,1)S(1)}, bf16[256,2048]{1,0:T(8,128)(2,1)}, u32[]{:S(2)}) %copy-start.4) | copy-done | bytes 1048600
  34.3 0.0 copy-start.9
  34.3 1.0 %copy-done.9 = bf16[256,1024]{1,0:T(8,128)(2,1)S(1)} copy-done((bf16[256,1024]{1,0:T(8,128)(2,1)S(1)}, bf16[256,1024]{1,0:T(8,128)(2,1)}, u32[]{:S(2)}) %copy-start.9) | copy-done | bytes 524312
  35.3 0.0 copy-start.7
  35.3 5.2 %attend.1 = bf16[256,2048]{1,0:T(8,128)(2,1)} custom-call(f32[256,128]{1,0:T(8,128)S(1)} %get-tuple-element.17.start_ref, bf16[256,2048]{1,0:T(8,128)(2,1)S(1)} %copy-done.4, bf16[256,512]{1,0:T(8,128)(2,1)S(1)} %copy-done.2, bf16[256,512]{1,0:T(8,128)(2,1)S(1)} %copy-done.3, bf16[256,1024]{1,0:T(8,128)(2,1)S(1)} %copy-done.9, ...), custom_call_target="tpu_custom_call" | custom-call | tf_op jit(solution)/shard_map/attend/pallas_call | solution.py:494
  40.6 1.2 %collective-permute-done.tail_ref.decay_ref = bf16[4224,128]{1,0:T(8,128)(2,1)} collective-permute-done((bf16[4224,128]{1,0:T(8,128)(2,1)}, bf16[4224,128]{1,0:T(8,128)(2,1)}, u32[]{:S(2)}, u32[]{:S(2)}) %collective-permute-start) | collective-permute-done | bytes 1081376 | tf_op jit(solution)/shard_map/ppermute | solution.py:372
  41.8 0.0 copy-done.1
  41.8 0.0 copy-done.7
  41.8 5.5 %final.1 = bf16[256,4096]{1,0:T(8,128)(2,1)} custom-call(f32[256,128]{1,0:T(8,128)S(1)} %get-tuple-element.17.start_ref, f32[256,128]{1,0:T(8,128)S(1)} %get-tuple-element.18.level_ref, bf16[4224,128]{1,0:T(8,128)(2,1)} %collective-permute-done.tail_ref.decay_ref, bf16[4224,128]{1,0:T(8,128)(2,1)} %collective-permute-done.tail_ref.decay_ref, ...), custom_call_target="tpu_custom_call" | custom-call | tf_op jit(solution)/shard_map/final/pallas_call | solution.py:513
Async XLA Ops:
  2.5 28.5 %all-to-all-start = ((bf16[8,320,128]{2,1,0:T(8,128)(2,1)}), bf16[8,320,128]{2,1,0:T(8,128)(2,1)S(1)}, u32[]{:S(2)}, u32[]{:S(2)}) async-start(bf16[8,320,128]{2,1,0:T(8,128)(2,1)} %pack.1), calls=%async_computation | async-start | bytes 1310720 | tf_op jit(solution)/shard_map/all_to_all | solution.py:443
  8.6 12.7 %copy-start = (bf16[256,4096]{1,0:T(8,128)(2,1)S(1)}, bf16[256,4096]{1,0:T(8,128)(2,1)}, u32[]{:S(2)}) copy-start(bf16[256,4096]{1,0:T(8,128)(2,1)} %x_ref.3) | copy-start | bytes 6291460
  8.6 12.7 %copy-start.5 = (bf16[256,512]{1,0:T(8,128)(2,1)S(1)}, bf16[256,512]{1,0:T(8,128)(2,1)}, u32[]{:S(2)}) copy-start(bf16[256,512]{1,0:T(8,128)(2,1)} %write_ref.3) | copy-start | bytes 786436
  8.6 12.7 %copy-start.6 = (bf16[256,512]{1,0:T(8,128)(2,1)S(1)}, bf16[256,512]{1,0:T(8,128)(2,1)}, u32[]{:S(2)}) copy-start(bf16[256,512]{1,0:T(8,128)(2,1)} %read_ref.3) | copy-start | bytes 786436
  9.9 20.3 %collective-permute-start.1 = (bf16[256,1024]{1,0:T(8,128)(2,1)S(1)}, bf16[256,1024]{1,0:T(8,128)(2,1)S(1)}, u32[]{:S(2)}, u32[]{:S(2)}) collective-permute-start(bf16[256,1024]{1,0:T(8,128)(2,1)S(1)} %join.1), channel_id=1, source_target_pairs={{0,1},{1,2},{2,3},{3,4},{4,5},{5,6},{6,7},{7,8},{8,9},{9,10},{10,1... | collective-permute-start | bytes 1572872 | tf_op jit(solution)/shard_map/ppermute | solution.py:372
  17.8 24.0 %collective-permute-start = (bf16[4224,128]{1,0:T(8,128)(2,1)}, bf16[4224,128]{1,0:T(8,128)(2,1)}, u32[]{:S(2)}, u32[]{:S(2)}) collective-permute-start(bf16[4224,128]{1,0:T(8,128)(2,1)} %get-tuple-element.19), channel_id=1, source_target_pairs={{0,1},{1,2},{2,3},{3,4},{4,5},{5,6},{6,7},{7,8},{8,9},{9,10},{10,1... | collective-permute-start | bytes 3244040 | tf_op jit(solution)/shard_map/ppermute | solution.py:372
  21.3 11.7 %copy-start.2 = (bf16[256,512]{1,0:T(8,128)(2,1)S(1)}, bf16[256,512]{1,0:T(8,128)(2,1)}, u32[]{:S(2)}) copy-start(bf16[256,512]{1,0:T(8,128)(2,1)} %key_ref.1) | copy-start | bytes 786436
  21.4 11.7 %copy-start.3 = (bf16[256,512]{1,0:T(8,128)(2,1)S(1)}, bf16[256,512]{1,0:T(8,128)(2,1)}, u32[]{:S(2)}) copy-start(bf16[256,512]{1,0:T(8,128)(2,1)} %value_ref.1) | copy-start | bytes 786436
  30.1 0.8 %copy-start.8 = (bf16[256,1024]{1,0:T(8,128)(2,1)}, bf16[256,1024]{1,0:T(8,128)(2,1)S(1)}, u32[]{:S(2)}) copy-start(bf16[256,1024]{1,0:T(8,128)(2,1)S(1)} %collective-permute-done.1.prior_ref) | copy-start | bytes 1572868
  31.0 10.9 %copy-start.1 = (bf16[256,4096]{1,0:T(8,128)(2,1)S(1)}, bf16[256,4096]{1,0:T(8,128)(2,1)}, u32[]{:S(2)}) copy-start(bf16[256,4096]{1,0:T(8,128)(2,1)} %gate_ref.1) | copy-start | bytes 6291460
  31.0 2.1 %collective-permute-start.2 = (bf16[8,320,128]{2,1,0:T(8,128)(2,1)S(1)}, bf16[8,320,128]{2,1,0:T(8,128)(2,1)S(1)}, u32[]{:S(2)}, u32[]{:S(2)}) collective-permute-start(bf16[8,320,128]{2,1,0:T(8,128)(2,1)S(1)} %all-to-all-done.rest_0_), channel_id=1, source_target_pairs={{0,1},{1,0},{2,3},{3,2},{4,5},{5,4},{6,7},{7,6},{8,9},{9,8},{10,11... | collective-permute-start | bytes 1966088 | tf_op jit(solution)/shard_map/ppermute | solution.py:491
  33.1 1.2 %copy-start.4 = (bf16[256,2048]{1,0:T(8,128)(2,1)S(1)}, bf16[256,2048]{1,0:T(8,128)(2,1)}, u32[]{:S(2)}) copy-start(bf16[256,2048]{1,0:T(8,128)(2,1)} %query_ref.1) | copy-start | bytes 3145732
  34.3 1.0 %copy-start.9 = (bf16[256,1024]{1,0:T(8,128)(2,1)S(1)}, bf16[256,1024]{1,0:T(8,128)(2,1)}, u32[]{:S(2)}) copy-start(bf16[256,1024]{1,0:T(8,128)(2,1)} %copy-done.8) | copy-start | bytes 1572868
  35.3 6.5 %copy-start.7 = (bf16[256,512]{1,0:T(8,128)(2,1)S(1)}, bf16[256,512]{1,0:T(8,128)(2,1)}, u32[]{:S(2)}) copy-start(bf16[256,512]{1,0:T(8,128)(2,1)} %read_ref.3) | copy-start | bytes 786436

commit v15 on v14

--- a/solution.py
+++ b/solution.py
@@ -10,7 +10,7 @@
 
 HD = 128
 LANES = 128
-WIDE = 256
+WIDE = 512
 NEAR = 2
 LOG2E = 1.4426950408889634
 F32 = jnp.float32

time: 47.8 us -> 47.8 us (level)
  no operation moved by 1% of the time
where the time goes in v15:
time: 47.8 us; the launch traced here: 47.3 us
  Pallas kernels  24.9 us (52%)
  starting transfers between devices  11.6 us (24%)
  waiting for transfers between devices  7.05 us (15%)
  local copies, waits for them, and re-layouts  3.12 us (7%)
  between operations  0.73 us (2%)
    all_to_all x1, starting transfers between devices, local(): lax.all_to_all(packed, 'reader', 0, 0, axis_index_groups=lines, tiled=True)  6.18 us
    pallas_call x1, Pallas kernels, local(): pl.pallas_call(functools.partial(tail_kernel, per_group=per_group, channe...  6.04 us
    pallas_call x1, Pallas kernels, local(): pl.pallas_call(functools.partial(final_kernel, state_rows=state_rows, **s...  5.5 us
    ppermute x2, starting transfers between devices, shifted(): return lax.ppermute(value, axis, [(i, i + by) for i in range(length - by)])  5.39 us
    pallas_call x1, Pallas kernels, local(): pl.pallas_call(functools.partial(attend_kernel, state_rows=state_rows, pr...  5.24 us
    pallas_call x1, Pallas kernels, local(): pl.pallas_call(functools.partial(inner_kernel, **sizes), grid=(groups,),...  5.06 us
    ppermute x2, waiting for transfers between devices, shifted(): return lax.ppermute(value, axis, [(i, i + by) for i in range(length - by)])  4.95 us
    unnamed x20, local copies, waits for them, and re-layouts  3.12 us
  transfers between devices with their start and end apart: 4, of which 3 were waited for; matrix products, arithmetic and copies ran while one was open for 0% of the time, Pallas kernels for 37%

profile of v15, /device:TPU:18, one launch (start us, length us, event | category | flops | bytes accessed | tf_op | source)
XLA Modules:
  0.0 47.3 jit_solution(16528267134450442485)
XLA Ops:
  0.6 1.8 %pack.1 = bf16[8,320,128]{2,1,0:T(8,128)(2,1)} custom-call(f32[256,128]{1,0:T(8,128)} %state_ref.1, bf16[8,512]{1,0:T(8,128)(2,1)} %keys_ref.1, bf16[8,512]{1,0:T(8,128)(2,1)} %values_ref.2), custom_call_target="tpu_custom_call" | custom-call | tf_op jit(solution)/shard_map/pack/pallas_call | solution.py:422
  2.5 6.2 %all-to-all-start = ((bf16[8,320,128]{2,1,0:T(8,128)(2,1)}), bf16[8,320,128]{2,1,0:T(8,128)(2,1)S(1)}, u32[]{:S(2)}, u32[]{:S(2)}) async-start(bf16[8,320,128]{2,1,0:T(8,128)(2,1)} %pack.1), calls=%async_computation | async-start | bytes 1310720 | tf_op jit(solution)/shard_map/all_to_all | solution.py:443
  8.6 0.0 copy-start
  8.6 0.0 copy-start.5
  8.6 0.0 copy-start.6
  8.7 1.2 %join.1 = bf16[256,1024]{1,0:T(8,128)(2,1)S(1)} custom-call(bf16[256,512]{1,0:T(8,128)(2,1)} %key_ref.1, bf16[256,512]{1,0:T(8,128)(2,1)} %value_ref.1), custom_call_target="tpu_custom_call" | custom-call | tf_op jit(solution)/shard_map/join/pallas_call | solution.py:434
  9.9 1.9 %collective-permute-start.1 = (bf16[256,1024]{1,0:T(8,128)(2,1)S(1)}, bf16[256,1024]{1,0:T(8,128)(2,1)S(1)}, u32[]{:S(2)}, u32[]{:S(2)}) collective-permute-start(bf16[256,1024]{1,0:T(8,128)(2,1)S(1)} %join.1), channel_id=1, source_target_pairs={{0,1},{1,2},{2,3},{3,4},{4,5},{5,6},{6,7},{7,8},{8,9},{9,10},{10,1... | collective-permute-start | bytes 1572872 | tf_op jit(solution)/shard_map/ppermute | solution.py:372
  11.8 6.0 %tail.1 = (bf16[4224,128]{1,0:T(8,128)(2,1)}, f32[256,128]{1,0:T(8,128)S(1)}, f32[64,256]{1,0:T(8,128)S(1)}, f32[256,128]{1,0:T(8,128)S(1)}) custom-call(s32[1,32]{1,0:T(1,128)} %bitcast.7, f32[64,256]{1,0:T(8,128)} %bitcast.5, f32[1,64]{1,0:T(1,128)} %bitcast.8, bf16[256,4096]{1,0:T(8,128)(2,1)} %x_ref.3, bf16[256,512]{1,0:T(8,128)(2,1)} %write_ref.3), custom_call_target="tpu_custom_call" | custom-call | tf_op jit(solution)/shard_map/tail/pallas_call | solution.py:449
  17.8 3.5 %collective-permute-start = (bf16[4224,128]{1,0:T(8,128)(2,1)}, bf16[4224,128]{1,0:T(8,128)(2,1)}, u32[]{:S(2)}, u32[]{:S(2)}) collective-permute-start(bf16[4224,128]{1,0:T(8,128)(2,1)} %get-tuple-element.19), channel_id=1, source_target_pairs={{0,1},{1,2},{2,3},{3,4},{4,5},{5,6},{6,7},{7,8},{8,9},{9,10},{10,1... | collective-permute-start | bytes 3244040 | tf_op jit(solution)/shard_map/ppermute | solution.py:372
  21.3 0.0 copy-done
  21.3 0.0 copy-done.5
  21.3 0.0 copy-done.6
  21.3 0.0 copy-start.2
  21.4 0.0 copy-start.3
  21.4 5.1 %inner.1.inner_ref = bf16[256,4096]{1,0:T(8,128)(2,1)S(1)} custom-call(f32[256,128]{1,0:T(8,128)S(1)} %get-tuple-element.17.start_ref, f32[256,128]{1,0:T(8,128)S(1)} %get-tuple-element.18.level_ref, f32[64,256]{1,0:T(8,128)S(1)} %get-tuple-element.22.column_ref, f32[1,64]{1,0:T(1,128)} %bitcast.9, bf16[256,4096]{1,0:T(8,128)(2,1)S(1)} %copy-done, ...), custom_call_target="tpu_custom_call" | custom-call | tf_op jit(solution)/shard_map/inner/pallas_call | solution.py:472
  26.4 3.7 %collective-permute-done.1.prior_ref = bf16[256,1024]{1,0:T(8,128)(2,1)S(1)} collective-permute-done((bf16[256,1024]{1,0:T(8,128)(2,1)S(1)}, bf16[256,1024]{1,0:T(8,128)(2,1)S(1)}, u32[]{:S(2)}, u32[]{:S(2)}) %collective-permute-start.1) | collective-permute-done | bytes 524320 | tf_op jit(solution)/shard_map/ppermute | solution.py:372
  30.1 0.0 copy-start.8
  30.1 0.8 %copy-done.8 = bf16[256,1024]{1,0:T(8,128)(2,1)} copy-done((bf16[256,1024]{1,0:T(8,128)(2,1)}, bf16[256,1024]{1,0:T(8,128)(2,1)S(1)}, u32[]{:S(2)}) %copy-start.8) | copy-done | bytes 524312
  31.0 0.0 all-to-all-done.rest_0_
  31.0 0.0 copy-start.1
  31.0 0.0 collective-permute-start.2
  31.0 2.1 %collective-permute-done.2.rest_1_ = bf16[8,320,128]{2,1,0:T(8,128)(2,1)S(1)} collective-permute-done((bf16[8,320,128]{2,1,0:T(8,128)(2,1)S(1)}, bf16[8,320,128]{2,1,0:T(8,128)(2,1)S(1)}, u32[]{:S(2)}, u32[]{:S(2)}) %collective-permute-start.2) | collective-permute-done | bytes 655392 | tf_op jit(solution)/shard_map/ppermute | solution.py:491
  33.1 0.0 copy-done.2
  33.1 0.0 copy-done.3
  33.1 0.0 copy-start.4
  33.1 1.2 %copy-done.4 = bf16[256,2048]{1,0:T(8,128)(2,1)S(1)} copy-done((bf16[256,2048]{1,0:T(8,128)(2,1)S(1)}, bf16[256,2048]{1,0:T(8,128)(2,1)}, u32[]{:S(2)}) %copy-start.4) | copy-done | bytes 1048600
  34.3 0.0 copy-start.9
  34.3 1.0 %copy-done.9 = bf16[256,1024]{1,0:T(8,128)(2,1)S(1)} copy-done((bf16[256,1024]{1,0:T(8,128)(2,1)S(1)}, bf16[256,1024]{1,0:T(8,128)(2,1)}, u32[]{:S(2)}) %copy-start.9) | copy-done | bytes 524312
  35.3 0.0 copy-start.7
  35.3 5.2 %attend.1 = bf16[256,2048]{1,0:T(8,128)(2,1)} custom-call(f32[256,128]{1,0:T(8,128)S(1)} %get-tuple-element.17.start_ref, bf16[256,2048]{1,0:T(8,128)(2,1)S(1)} %copy-done.4, bf16[256,512]{1,0:T(8,128)(2,1)S(1)} %copy-done.2, bf16[256,512]{1,0:T(8,128)(2,1)S(1)} %copy-done.3, bf16[256,1024]{1,0:T(8,128)(2,1)S(1)} %copy-done.9, ...), custom_call_target="tpu_custom_call" | custom-call | tf_op jit(solution)/shard_map/attend/pallas_call | solution.py:494
  40.6 1.2 %collective-permute-done.tail_ref.decay_ref = bf16[4224,128]{1,0:T(8,128)(2,1)} collective-permute-done((bf16[4224,128]{1,0:T(8,128)(2,1)}, bf16[4224,128]{1,0:T(8,128)(2,1)}, u32[]{:S(2)}, u32[]{:S(2)}) %collective-permute-start) | collective-permute-done | bytes 1081376 | tf_op jit(solution)/shard_map/ppermute | solution.py:372
  41.8 0.0 copy-done.1
  41.8 0.0 copy-done.7
  41.8 5.5 %final.1 = bf16[256,4096]{1,0:T(8,128)(2,1)} custom-call(f32[256,128]{1,0:T(8,128)S(1)} %get-tuple-element.17.start_ref, f32[256,128]{1,0:T(8,128)S(1)} %get-tuple-element.18.level_ref, bf16[4224,128]{1,0:T(8,128)(2,1)} %collective-permute-done.tail_ref.decay_ref, bf16[4224,128]{1,0:T(8,128)(2,1)} %collective-permute-done.tail_ref.decay_ref, ...), custom_call_target="tpu_custom_call" | custom-call | tf_op jit(solution)/shard_map/final/pallas_call | solution.py:513
Async XLA Ops:
  2.5 28.5 %all-to-all-start = ((bf16[8,320,128]{2,1,0:T(8,128)(2,1)}), bf16[8,320,128]{2,1,0:T(8,128)(2,1)S(1)}, u32[]{:S(2)}, u32[]{:S(2)}) async-start(bf16[8,320,128]{2,1,0:T(8,128)(2,1)} %pack.1), calls=%async_computation | async-start | bytes 1310720 | tf_op jit(solution)/shard_map/all_to_all | solution.py:443
  8.6 12.7 %copy-start = (bf16[256,4096]{1,0:T(8,128)(2,1)S(1)}, bf16[256,4096]{1,0:T(8,128)(2,1)}, u32[]{:S(2)}) copy-start(bf16[256,4096]{1,0:T(8,128)(2,1)} %x_ref.3) | copy-start | bytes 6291460
  8.6 12.7 %copy-start.5 = (bf16[256,512]{1,0:T(8,128)(2,1)S(1)}, bf16[256,512]{1,0:T(8,128)(2,1)}, u32[]{:S(2)}) copy-start(bf16[256,512]{1,0:T(8,128)(2,1)} %write_ref.3) | copy-start | bytes 786436
  8.6 12.7 %copy-start.6 = (bf16[256,512]{1,0:T(8,128)(2,1)S(1)}, bf16[256,512]{1,0:T(8,128)(2,1)}, u32[]{:S(2)}) copy-start(bf16[256,512]{1,0:T(8,128)(2,1)} %read_ref.3) | copy-start | bytes 786436
  9.9 20.3 %collective-permute-start.1 = (bf16[256,1024]{1,0:T(8,128)(2,1)S(1)}, bf16[256,1024]{1,0:T(8,128)(2,1)S(1)}, u32[]{:S(2)}, u32[]{:S(2)}) collective-permute-start(bf16[256,1024]{1,0:T(8,128)(2,1)S(1)} %join.1), channel_id=1, source_target_pairs={{0,1},{1,2},{2,3},{3,4},{4,5},{5,6},{6,7},{7,8},{8,9},{9,10},{10,1... | collective-permute-start | bytes 1572872 | tf_op jit(solution)/shard_map/ppermute | solution.py:372
  17.8 24.0 %collective-permute-start = (bf16[4224,128]{1,0:T(8,128)(2,1)}, bf16[4224,128]{1,0:T(8,128)(2,1)}, u32[]{:S(2)}, u32[]{:S(2)}) collective-permute-start(bf16[4224,128]{1,0:T(8,128)(2,1)} %get-tuple-element.19), channel_id=1, source_target_pairs={{0,1},{1,2},{2,3},{3,4},{4,5},{5,6},{6,7},{7,8},{8,9},{9,10},{10,1... | collective-permute-start | bytes 3244040 | tf_op jit(solution)/shard_map/ppermute | solution.py:372
  21.3 11.7 %copy-start.2 = (bf16[256,512]{1,0:T(8,128)(2,1)S(1)}, bf16[256,512]{1,0:T(8,128)(2,1)}, u32[]{:S(2)}) copy-start(bf16[256,512]{1,0:T(8,128)(2,1)} %key_ref.1) | copy-start | bytes 786436
  21.4 11.7 %copy-start.3 = (bf16[256,512]{1,0:T(8,128)(2,1)S(1)}, bf16[256,512]{1,0:T(8,128)(2,1)}, u32[]{:S(2)}) copy-start(bf16[256,512]{1,0:T(8,128)(2,1)} %value_ref.1) | copy-start | bytes 786436
  30.1 0.8 %copy-start.8 = (bf16[256,1024]{1,0:T(8,128)(2,1)}, bf16[256,1024]{1,0:T(8,128)(2,1)S(1)}, u32[]{:S(2)}) copy-start(bf16[256,1024]{1,0:T(8,128)(2,1)S(1)} %collective-permute-done.1.prior_ref) | copy-start | bytes 1572868
  31.0 10.9 %copy-start.1 = (bf16[256,4096]{1,0:T(8,128)(2,1)S(1)}, bf16[256,4096]{1,0:T(8,128)(2,1)}, u32[]{:S(2)}) copy-start(bf16[256,4096]{1,0:T(8,128)(2,1)} %gate_ref.1) | copy-start | bytes 6291460
  31.0 2.1 %collective-permute-start.2 = (bf16[8,320,128]{2,1,0:T(8,128)(2,1)S(1)}, bf16[8,320,128]{2,1,0:T(8,128)(2,1)S(1)}, u32[]{:S(2)}, u32[]{:S(2)}) collective-permute-start(bf16[8,320,128]{2,1,0:T(8,128)(2,1)S(1)} %all-to-all-done.rest_0_), channel_id=1, source_target_pairs={{0,1},{1,0},{2,3},{3,2},{4,5},{5,4},{6,7},{7,6},{8,9},{9,8},{10,11... | collective-permute-start | bytes 1966088 | tf_op jit(solution)/shard_map/ppermute | solution.py:491
  33.1 1.2 %copy-start.4 = (bf16[256,2048]{1,0:T(8,128)(2,1)S(1)}, bf16[256,2048]{1,0:T(8,128)(2,1)}, u32[]{:S(2)}) copy-start(bf16[256,2048]{1,0:T(8,128)(2,1)} %query_ref.1) | copy-start | bytes 3145732
  34.3 1.0 %copy-start.9 = (bf16[256,1024]{1,0:T(8,128)(2,1)S(1)}, bf16[256,1024]{1,0:T(8,128)(2,1)}, u32[]{:S(2)}) copy-start(bf16[256,1024]{1,0:T(8,128)(2,1)} %copy-done.8) | copy-start | bytes 1572868
  35.3 6.5 %copy-start.7 = (bf16[256,512]{1,0:T(8,128)(2,1)S(1)}, bf16[256,512]{1,0:T(8,128)(2,1)}, u32[]{:S(2)}) copy-start(bf16[256,512]{1,0:T(8,128)(2,1)} %read_ref.3) | copy-start | bytes 786436
